TPU v7x, 32 devices: a whole 2x2x4 slice. The times are simulated.
32 devices in a mesh: groups: 1, expert: 32 (over z, y, x, core).
Axes of the slice: x: 2, y: 2, z: 4, core: 2. Of those that a mesh axis runs over, the one named last changes fastest.
Arguments:
- hidden: bfloat16 [512, 7168], P(('groups', 'expert')), may hold values from -6 to 6
- expert_ids: int32 [512, 2], P(('groups', 'expert')), may hold values from 0 to 3, all different within a row; in each aligned block of 8 rows (0 to 7, 8 to 15, ...) at most 8 rows name the same one
- route_weights: float32 [512, 2], P(('groups', 'expert')), may hold values from 0.1 to 1
- gate_weight: bfloat16 [32, 7168, 256], P('expert'), may hold values from -0.0625 to 0.0625
- up_weight: bfloat16 [32, 7168, 256], P('expert'), may hold values from -0.0625 to 0.0625
- down_weight: bfloat16 [32, 256, 7168], P('expert'), may hold values from -0.125 to 0.125
- queries: bfloat16 [512, 128, 576], P(('groups', 'expert')), may hold values from -100 to 100
- latent_cache: bfloat16 [512, 512, 576], P(('groups', 'expert')), may hold values from -16 to 16
- lengths: int32 [512], P(('groups', 'expert')), may hold values from 64 to 512, as said below
Outputs:
- routed: bfloat16 [512, 7168], P(('groups', 'expert'))
- attended: bfloat16 [512, 128, 512], P(('groups', 'expert'))
Inputs may be any that keep to these rules, and one draw needn't show every extreme that they name: `expert_ids`: each row names 2 different experts. `lengths`: the first request holds 512 positions.
All inputs are finite; a program needn't handle non-finite values.
Results may differ from a plain program's by a relative error of at most 0.008.
Values may be sent and summed in bfloat16 or wider, within the bound.
No kernel may reach another device: no remote copies, remote signals or barrier semaphores. Data moves between devices by JAX's collectives and lax.ppermute only.
A program may use at most 128 MiB of HBM per device.

v0:
```python
import jax
import jax.numpy as jnp
from jax import lax
from jax.sharding import PartitionSpec as P

LAT = 512
MB = 2
SLICES = 8


score_scale = 0.07216878364870322


def attend(queries, latent_cache, lengths):
    scores = (
        jnp.einsum("rhc,rpc->rhp", queries, latent_cache, preferred_element_type=jnp.float32)
        * score_scale
    )
    positions = jnp.arange(latent_cache.shape[1], dtype=jnp.int32)
    in_range = positions[None, None, :] < lengths[:, None, None]
    masked = jnp.where(in_range, scores, -jnp.inf)
    row_peak = jnp.max(masked, axis=-1, keepdims=True)
    raised = jnp.exp(masked - row_peak)
    weights = (raised / jnp.sum(raised, axis=-1, keepdims=True)).astype(jnp.bfloat16)
    return jnp.einsum(
        "rhp,rpc->rhc", weights, latent_cache[:, :, :LAT], preferred_element_type=jnp.float32
    ).astype(jnp.bfloat16)


def expert_rows(arrived, gate_part, up_part, down_part):
    flat_rows = arrived.reshape(-1, arrived.shape[2])
    gate_value = jnp.dot(flat_rows, gate_part, preferred_element_type=jnp.float32)
    up_value = jnp.dot(flat_rows, up_part, preferred_element_type=jnp.float32)
    inner_value = (jax.nn.silu(gate_value) * up_value).astype(jnp.bfloat16)
    partial_value = jnp.dot(inner_value, down_part, preferred_element_type=jnp.float32)
    return partial_value.reshape(arrived.shape[0], arrived.shape[1], partial_value.shape[1])


def place_rows(ids_block, weight_block, experts):
    count_rows = ids_block.shape[0]
    choose = (ids_block[:, :, None] == jnp.arange(experts, dtype=jnp.int32)[None, None, :]).astype(
        jnp.float32
    )
    chosen = jnp.sum(choose, axis=1)
    mixing = jnp.sum(weight_block[:, :, None] * choose, axis=1)
    earlier = (jnp.arange(count_rows)[:, None] > jnp.arange(count_rows)[None, :]).astype(
        jnp.float32
    )
    ranking = jnp.dot(earlier, chosen, precision=lax.Precision.HIGHEST)
    slot_index = jnp.arange(count_rows).astype(jnp.float32)
    placing = chosen.T[:, None, :] * (ranking.T[:, None, :] == slot_index[None, :, None]).astype(
        jnp.float32
    )
    return (placing, mixing)


def on_device(
    hidden,
    expert_ids,
    route_weights,
    gate_weight,
    up_weight,
    down_weight,
    queries,
    latent_cache,
    lengths,
):
    devices = lax.axis_size("expert")
    experts = devices // SLICES
    half_rows = hidden.shape[0] // MB
    gate_part = gate_weight[0]
    up_part = up_weight[0]
    down_part = down_weight[0]
    routed_blocks = []
    attended_blocks = []
    for batch_index in range(MB):
        first_row = batch_index * half_rows
        last_row = first_row + half_rows
        attended_blocks.append(
            attend(
                queries[first_row:last_row],
                latent_cache[first_row:last_row],
                lengths[first_row:last_row],
            )
        )
        placing, mixing = place_rows(
            expert_ids[first_row:last_row], route_weights[first_row:last_row], experts
        )
        outgoing = jnp.einsum(
            "esr,rd->esd",
            placing.astype(jnp.bfloat16),
            hidden[first_row:last_row],
            preferred_element_type=jnp.float32,
        ).astype(jnp.bfloat16)
        copies = jnp.broadcast_to(
            outgoing[:, None], (experts, SLICES) + outgoing.shape[1:]
        ).reshape(devices, half_rows, -1)
        partial_value = expert_rows(
            lax.all_to_all(copies, "expert", split_axis=0, concat_axis=0, tiled=True),
            gate_part,
            up_part,
            down_part,
        )
        returned = lax.all_to_all(partial_value, "expert", split_axis=0, concat_axis=0, tiled=True)
        summed = returned.reshape(experts, SLICES, half_rows, -1).sum(axis=1)
        weighting = placing * mixing.T[:, None, :]
        routed_blocks.append(
            jnp.einsum("esr,esd->rd", weighting, summed, precision=lax.Precision.HIGHEST).astype(
                jnp.bfloat16
            )
        )
    return (jnp.concatenate(routed_blocks, axis=0), jnp.concatenate(attended_blocks, axis=0))


def solution(mesh):
    in_specs = (
        P(("groups", "expert"), None),
        P(("groups", "expert"), None),
        P(("groups", "expert"), None),
        P("expert", None, None),
        P("expert", None, None),
        P("expert", None, None),
        P(("groups", "expert"), None, None),
        P(("groups", "expert"), None, None),
        P(("groups", "expert")),
    )
    out_specs = (P(("groups", "expert"), None), P(("groups", "expert"), None, None))
    return jax.shard_map(
        on_device, mesh=mesh, in_specs=in_specs, out_specs=out_specs, check_vma=False
    )
```

profile of v0, /device:TPU:0, one launch (start us, length us, event | category | flops | bytes accessed | tf_op | source)
XLA Modules:
  0.0 525.4 jit_solution(7134605737572224832)
XLA Ops:
  0.7 0.9 fusion.136
  1.6 0.8 fusion.137
  2.5 1.3 convolution_convert_fusion.1
  3.8 2.3 broadcast_in_dim.22
  6.1 7.4 %all-to-all-start = ((bf16[32,8,7168]{2,1,0:T(8,128)(2,1)}), bf16[32,8,7168]{2,1,0:T(8,128)(2,1)}, u32[]{:S(2)}, u32[]{:S(2)}) async-start(bf16[32,8,7168]{2,1,0:T(8,128)(2,1)} %bitcast.97), calls=%async_computation | async-start | bytes 7340032 | tf_op jit(solution)/shard_map/all_to_all | solution.py:99
  13.6 0.4 convolution_convert_fusion
  14.0 82.1 %all-to-all-done = bf16[32,8,7168]{2,1,0:T(8,128)(2,1)} async-done(((bf16[32,8,7168]{2,1,0:T(8,128)(2,1)}), bf16[32,8,7168]{2,1,0:T(8,128)(2,1)}, u32[]{:S(2)}, u32[]{:S(2)}) %all-to-all-start) | async-done | bytes 3670048 | tf_op jit(solution)/shard_map/all_to_all | solution.py:99
  96.1 2.3 broadcast_in_dim.23
  98.4 4.1 all-to-all-start.2
  102.5 4.3 fusion.24
  106.8 11.1 %fusion.18 = f32[32,8,7168]{2,1,0:T(8,128)} fusion(bf16[1,256,7168]{2,1,0:T(8,128)(2,1)} %param.14, bf16[1,7168,256]{2,1,0:T(8,128)(2,1)} %param.13, bf16[32,8,7168]{2,1,0:T(8,128)(2,1)} %all-to-all-done, f32[256,256]{1,0:T(8,128)S(1)} %fusion.24), kind=kOutput, calls=%fused_computation.24 | convolution fusion | flops 1879441408 | bytes 18612224 | tf_op jit(solution)/shard_map/dot_general | solution.py:35
  117.9 67.2 %all-to-all-done.2 = bf16[32,8,7168]{2,1,0:T(8,128)(2,1)} async-done(((bf16[32,8,7168]{2,1,0:T(8,128)(2,1)}), bf16[32,8,7168]{2,1,0:T(8,128)(2,1)}, u32[]{:S(2)}, u32[]{:S(2)}) %all-to-all-start.2) | async-done | bytes 3670048 | tf_op jit(solution)/shard_map/all_to_all | solution.py:99
  185.1 4.1 all-to-all-start.1
  189.2 4.3 fusion.14
  193.5 11.2 %fusion.16 = f32[32,8,7168]{2,1,0:T(8,128)} fusion(bf16[1,256,7168]{2,1,0:T(8,128)(2,1)} %param.14, bf16[1,7168,256]{2,1,0:T(8,128)(2,1)} %param.13, bf16[32,8,7168]{2,1,0:T(8,128)(2,1)} %all-to-all-done.2, f32[256,256]{1,0:T(8,128)S(1)} %fusion.14), kind=kOutput, calls=%fused_computation.22 | convolution fusion | flops 1879441408 | bytes 18612224 | tf_op jit(solution)/shard_map/dot_general | solution.py:35
  204.7 147.6 %all-to-all-done.1 = f32[32,8,7168]{2,1,0:T(8,128)} async-done(((f32[32,8,7168]{2,1,0:T(8,128)}), f32[32,8,7168]{2,1,0:T(8,128)}, u32[]{:S(2)}, u32[]{:S(2)}) %all-to-all-start.1) | async-done | bytes 7340064 | tf_op jit(solution)/shard_map/all_to_all | solution.py:104
  352.3 3.8 all-to-all-start.3
  356.3 3.4 fusion.6
  359.8 1.4 copy-done.4
  361.1 0.7 fusion.140
  361.8 3.4 fusion.4
  365.2 1.3 copy-done.3
  366.5 0.7 fusion.139
  367.2 4.9 fusion.30
  372.1 6.0 %fusion.33 = bf16[8,128,512]{2,1,0:T(8,128)(2,1)} fusion(bf16[16,512,576]{1,2,0:T(8,128)(2,1)} %param.16, f32[8,128]{1,0:T(8,128)S(1)} %fusion.139, f32[8,128,512]{2,1,0:T(8,128)} %copy-done.3, pred[8,512]{1,0:T(8,128)(4,1)S(1)} %get-tuple-element.14), kind=kOutput, calls=%fused_computation.44 | convolution fusion | flops 540018176 | bytes 7348224 | tf_op jit(solution)/shard_map/rhp,rpc->rhc/dot_general | solution.py:25
  378.1 2.7 pad_maximum_fusion
  380.8 3.6 bitcast_reduce_fusion.1
  384.4 1.8 fusion.2
  386.2 133.0 %all-to-all-done.3 = f32[32,8,7168]{2,1,0:T(8,128)} async-done(((f32[32,8,7168]{2,1,0:T(8,128)}), f32[32,8,7168]{2,1,0:T(8,128)}, u32[]{:S(2)}, u32[]{:S(2)}) %all-to-all-start.3) | async-done | bytes 7340064 | tf_op jit(solution)/shard_map/all_to_all | solution.py:104
  519.2 3.6 bitcast_reduce_fusion
  522.8 1.8 fusion.3
  524.7 0.7 pad_maximum_fusion.1
  (14 shorter events, 0.4 us)
Async XLA Ops:
  0.6 355.7 %copy-start = (bf16[16,128,576]{1,2,0:T(8,128)(2,1)S(1)}, bf16[16,128,576]{1,2,0:T(8,128)(2,1)}, u32[]{:S(2)}) copy-start(bf16[16,128,576]{1,2,0:T(8,128)(2,1)} %param.15) | copy-start | bytes 7077892
  6.1 7.5 %copy-start.1 = (bf16[16,7168]{1,0:T(8,128)(2,1)S(1)}, bf16[16,7168]{1,0:T(8,128)(2,1)}, u32[]{:S(2)}) copy-start(bf16[16,7168]{1,0:T(8,128)(2,1)} %param.9) | copy-start | bytes 688132
  6.1 90.0 %all-to-all-start = ((bf16[32,8,7168]{2,1,0:T(8,128)(2,1)}), bf16[32,8,7168]{2,1,0:T(8,128)(2,1)}, u32[]{:S(2)}, u32[]{:S(2)}) async-start(bf16[32,8,7168]{2,1,0:T(8,128)(2,1)} %bitcast.97), calls=%async_computation | async-start | bytes 7340032 | tf_op jit(solution)/shard_map/all_to_all | solution.py:99
  98.4 86.7 %all-to-all-start.2 = ((bf16[32,8,7168]{2,1,0:T(8,128)(2,1)}), bf16[32,8,7168]{2,1,0:T(8,128)(2,1)}, u32[]{:S(2)}, u32[]{:S(2)}) async-start(bf16[32,8,7168]{2,1,0:T(8,128)(2,1)} %bitcast.96), calls=%async_computation.2 | async-start | bytes 7340032 | tf_op jit(solution)/shard_map/all_to_all | solution.py:99
  185.1 167.2 %all-to-all-start.1 = ((f32[32,8,7168]{2,1,0:T(8,128)}), f32[32,8,7168]{2,1,0:T(8,128)}, u32[]{:S(2)}, u32[]{:S(2)}) async-start(f32[32,8,7168]{2,1,0:T(8,128)} %fusion.18), calls=%async_computation.1 | async-start | bytes 14680064 | tf_op jit(solution)/shard_map/all_to_all | solution.py:104
  204.7 151.4 %copy-start.2 = (s32[16]{0:T(128)S(1)}, s32[16]{0:T(128)}, u32[]{:S(2)}) copy-start(s32[16]{0:T(128)} %param.17) | copy-start | bytes 196
  352.3 166.9 %all-to-all-start.3 = ((f32[32,8,7168]{2,1,0:T(8,128)}), f32[32,8,7168]{2,1,0:T(8,128)}, u32[]{:S(2)}, u32[]{:S(2)}) async-start(f32[32,8,7168]{2,1,0:T(8,128)} %fusion.16), calls=%async_computation.3 | async-start | bytes 14680064 | tf_op jit(solution)/shard_map/all_to_all | solution.py:104
  359.8 1.4 copy-start.4
  365.2 1.3 copy-start.3
where the time goes:
time: 526 us; the launch traced here: 525 us
  waiting for transfers between devices  430 us (82%)
  matrix products  54.2 us (10%)
  starting transfers between devices  19.4 us (4%)
  other arithmetic  12 us (2%)
  local copies, waits for them, and re-layouts  9.01 us (2%)
    all_to_all x2, waiting for transfers between devices, on_device(): lax.all_to_all(partial_value, 'expert', split_axis=0, concat_axis=0, tile...  281 us
    all_to_all x2, waiting for transfers between devices, on_device(): lax.all_to_all(copies, 'expert', split_axis=0, concat_axis=0, tiled=True)  149 us
    dot_general x2, matrix products, expert_rows(): jnp.dot(inner_value, down_part, preferred_element_type=jnp.float32)  22.3 us
    all_to_all x2, starting transfers between devices, on_device(): lax.all_to_all(copies, 'expert', split_axis=0, concat_axis=0, tiled=True)  11.5 us
    dot_general x2, matrix products, attend(): jnp.einsum('rhp,rpc->rhc', weights, latent_cache[:, :, :LAT], preferred_e...  10.9 us
  transfers between devices with their start and end apart: 4, of which 4 were waited for; matrix products, arithmetic and copies ran while one was open for 11% of the time, Pallas kernels for 0%

commit v1 on v0

v1 whole, which is shorter than its diff:
```python
import functools

import jax
import jax.numpy as jnp
from jax import lax
from jax.experimental import pallas as pl
from jax.experimental.pallas import tpu as pltpu
from jax.sharding import PartitionSpec as P

LAT = 512
SLICES = 8
AXIS = "expert"

score_scale = 0.07216878364870322


def attend_kernel(lengths_ref, queries_ref, cache_ref, out_ref):
    request = pl.program_id(0)
    length = lengths_ref[request]
    cache = cache_ref[0]
    scores = (
        lax.dot_general(
            queries_ref[0], cache, (((1,), (1,)), ((), ())), preferred_element_type=jnp.float32
        )
        * score_scale
    )
    positions = lax.broadcasted_iota(jnp.int32, scores.shape, 1)
    masked = jnp.where(positions < length, scores, -jnp.inf)
    row_peak = jnp.max(masked, axis=-1, keepdims=True)
    raised = jnp.exp(masked - row_peak)
    weights = (raised / jnp.sum(raised, axis=-1, keepdims=True)).astype(jnp.bfloat16)
    out_ref[0] = jnp.dot(
        weights, cache[:, :LAT], preferred_element_type=jnp.float32
    ).astype(jnp.bfloat16)


def attend(queries, latent_cache, lengths):
    requests, heads, width = queries.shape
    context = latent_cache.shape[1]
    return pl.pallas_call(
        attend_kernel,
        grid_spec=pltpu.PrefetchScalarGridSpec(
            num_scalar_prefetch=1,
            grid=(requests,),
            in_specs=[
                pl.BlockSpec((1, heads, width), lambda i, _: (i, 0, 0)),
                pl.BlockSpec((1, context, width), lambda i, _: (i, 0, 0)),
            ],
            out_specs=pl.BlockSpec((1, heads, LAT), lambda i, _: (i, 0, 0)),
        ),
        out_shape=jax.ShapeDtypeStruct((requests, heads, LAT), jnp.bfloat16),
        compiler_params=pltpu.CompilerParams(vmem_limit_bytes=24 * 1024 * 1024),
        cost_estimate=pl.CostEstimate(
            flops=2 * requests * heads * context * (width + LAT),
            bytes_accessed=2 * requests * (context * width + heads * (width + LAT)),
            transcendentals=requests * heads * context,
        ),
        name="latent_attention",
    )(lengths, queries, latent_cache)


def on_device(
    hidden,
    expert_ids,
    route_weights,
    gate_weight,
    up_weight,
    down_weight,
    queries,
    latent_cache,
    lengths,
):
    devices = lax.axis_size(AXIS)
    planes = devices // SLICES
    me = lax.axis_index(AXIS)
    core, plane, place = me % 2, me // SLICES, (me // 2) % 4
    rows, width = hidden.shape
    half, quarter = width // 2, width // 4
    first_core = core == 0

    def swap(value, bit):
        return lax.ppermute(value, AXIS, [(i, i ^ bit) for i in range(devices)])

    def shift(value, by):
        return lax.ppermute(
            value, AXIS, [(i, (i + SLICES * by) % devices) for i in range(devices)]
        )

    in_core = functools.partial(swap, bit=1)
    in_x = functools.partial(swap, bit=2)
    in_y = functools.partial(swap, bit=4)

    low, high = hidden[:, :half], hidden[:, half:]
    kept = jnp.where(first_core, low, high)
    got = in_core(jnp.where(first_core, high, low))
    block = jnp.where(
        first_core, jnp.concatenate([kept, got], 0), jnp.concatenate([got, kept], 0)
    )
    slots = [block] + [None] * (planes - 1)
    order = [k for k in (1, planes - 1) if k > 0] + list(range(2, planes - 1))
    for k in dict.fromkeys(order):
        slots[k] = shift(block, k)
    order = list(dict.fromkeys([0] + order))
    groups = [order[: planes // 2], order[planes // 2 :]]

    gate_part, up_part, down_part = gate_weight[0], up_weight[0], down_weight[0]
    other = (1 - core) * half
    gate_own = lax.dynamic_slice_in_dim(gate_part, core * half, half, 0)
    up_own = lax.dynamic_slice_in_dim(up_part, core * half, half, 0)
    entry_other = in_core(
        jnp.concatenate(
            [
                lax.dynamic_slice_in_dim(gate_part, other, half, 0),
                lax.dynamic_slice_in_dim(up_part, other, half, 0),
            ],
            1,
        )
    )
    entry_own = jnp.concatenate([gate_own, up_own], 1)
    down_own = jnp.where(first_core, down_part[:, :half], down_part[:, half:])
    down_other = in_core(jnp.where(first_core, down_part[:, half:], down_part[:, :half]))
    down_both = jnp.concatenate([down_own, down_other], 0)
    hidden_units = gate_part.shape[1]

    choose = (
        expert_ids[:, :, None] == jnp.arange(planes, dtype=jnp.int32)[None, None, :]
    ).astype(jnp.float32)
    mixing = jnp.sum(route_weights[:, :, None] * choose, axis=1)
    mixing_all = lax.all_gather(mixing, AXIS, axis=0, tiled=True)
    mine = jnp.sum(
        jnp.where(jnp.arange(planes)[None, :] == plane, mixing_all, 0.0), axis=1
    ).reshape(planes, 4, 2 * rows)

    def arrival_mixing(group):
        source_plane = (plane - jnp.array(group) + planes) % planes
        source_place = jnp.arange(4) ^ place
        pick_plane = source_plane[:, None] == jnp.arange(planes)[None, :]
        pick_place = source_place[:, None] == jnp.arange(4)[None, :]
        pick = pick_place[:, None, None, :] & pick_plane[None, :, :, None]
        chosen = jnp.where(pick[..., None], mine[None, None], 0.0)
        return jnp.sum(chosen, axis=(2, 3)).reshape(-1, 1)

    attended = attend(queries, latent_cache, lengths)

    def gather_plane(group):
        part_a = jnp.stack([slots[k][:, :quarter] for k in group])
        part_b = jnp.stack([slots[k][:, quarter:] for k in group])
        pair_a = jnp.stack([part_a, in_x(part_a)])
        pair_b = jnp.stack([part_b, in_y(part_b)])
        four_a = jnp.stack([pair_a, in_y(pair_a)])
        four_b = jnp.stack([pair_b, in_x(pair_b)], 1)
        return jnp.concatenate([four_a, four_b], -1).reshape(-1, half)

    def inner_of(arrived):
        pre_other = jnp.dot(arrived, entry_other, preferred_element_type=jnp.float32)
        pre_own = jnp.dot(arrived, entry_own, preferred_element_type=jnp.float32)
        pre = pre_own + in_core(pre_other)
        gate_value, up_value = pre[:, :hidden_units], pre[:, hidden_units:]
        inner = (jax.nn.silu(gate_value) * up_value).astype(jnp.bfloat16)
        return jnp.concatenate([inner, in_core(inner)], 1)

    def narrow(value):
        return value.astype(jnp.bfloat16)

    def widen(value):
        return value.astype(jnp.float32)

    def sum_plane(partial, group):
        partial = partial.reshape(2, 2, len(group), 2 * rows, half)
        part_a, part_b = partial[..., :quarter], partial[..., quarter:]
        pair_a = part_a[0] + widen(in_y(narrow(part_a[1])))
        pair_b = part_b[:, 0] + widen(in_x(narrow(part_b[:, 1])))
        one_a = pair_a[0] + widen(in_x(narrow(pair_a[1])))
        one_b = pair_b[0] + widen(in_y(narrow(pair_b[1])))
        return jnp.concatenate([one_a, one_b], -1)

    arrived = [gather_plane(group) for group in groups]
    inner = [inner_of(value) for value in arrived]
    total = None
    for group, value in reversed(list(zip(groups, inner))):
        partial = jnp.dot(value, down_both, preferred_element_type=jnp.float32)
        sums = sum_plane(partial * arrival_mixing(group), group)
        for at, k in enumerate(group):
            term = sums[at] if k == 0 else widen(shift(narrow(sums[at]), -k))
            total = term if total is None else total + term

    result = narrow(total)
    top, bottom = result[:rows], result[rows:]
    kept = jnp.where(first_core, top, bottom)
    got = in_core(jnp.where(first_core, bottom, top))
    routed = jnp.where(
        first_core, jnp.concatenate([kept, got], 1), jnp.concatenate([got, kept], 1)
    )
    return routed, attended


def solution(mesh):
    in_specs = (
        P(("groups", "expert"), None),
        P(("groups", "expert"), None),
        P(("groups", "expert"), None),
        P("expert", None, None),
        P("expert", None, None),
        P("expert", None, None),
        P(("groups", "expert"), None, None),
        P(("groups", "expert"), None, None),
        P(("groups", "expert")),
    )
    out_specs = (P(("groups", "expert"), None), P(("groups", "expert"), None, None))
    return jax.shard_map(
        on_device, mesh=mesh, in_specs=in_specs, out_specs=out_specs, check_vma=False
    )
```

time: 526 us -> 192 us (0.37)
  waiting for transfers between devices: 430 us -> 60.9 us
  blocking collectives: 0 us -> 43.5 us
  matrix products: 54.2 us -> 13.9 us
  local copies, waits for them, and re-layouts: 9.01 us -> 29.5 us
  Pallas kernels: 0 us -> 12.5 us
    all_to_all x4 -> x0, waiting for transfers between devices: 430 us -> none  [the longest x2 281 us: on_device(): lax.all_to_all(partial_value, 'expert', split_axis=0, concat_axis=0, tile...]
    ppermute x0 -> x30, waiting for transfers between devices: none -> 60.9 us  [the longest x24 44.3 us: swap(): return lax.ppermute(value, AXIS, [(i, i ^ bit) for i in range(devices)])]
    all_gather x0 -> x1, blocking collectives: none -> 43.5 us  [on_device(): mixing_all = lax.all_gather(mixing, AXIS, axis=0, tiled=True)]
    dot_general x14 -> x6, matrix products: 54.2 us -> 13.9 us  [the longest x2 6.44 us: inner_of(): jnp.dot(arrived, entry_other, preferred_element_type=jnp.float32)]
    ppermute x0 -> x30, starting transfers between devices: none -> 20.2 us  [the longest x24 13.4 us: swap(): return lax.ppermute(value, AXIS, [(i, i ^ bit) for i in range(devices)])]
    unnamed x10 -> x19, local copies, waits for them, and re-layouts: 2.69 us -> 22.4 us
    all_to_all x4 -> x0, starting transfers between devices: 19.4 us -> none  [the longest x2 11.5 us: on_device(): lax.all_to_all(copies, 'expert', split_axis=0, concat_axis=0, tiled=True)]
    pallas_call x0 -> x1, Pallas kernels: none -> 12.5 us  [attend(): pl.pallas_call(attend_kernel, grid_spec=pltpu.PrefetchScalarGridSpec(num_...]
  transfers between devices with their start and end apart: 4 -> 30, of which waited for: 4 -> 15; matrix products, arithmetic and copies ran while one was open for 11% -> 23% of each run, Pallas kernels for 0% -> 7%
where the time goes in v1:
time: 192 us; the launch traced here: 191 us
  waiting for transfers between devices  60.9 us (32%)
  blocking collectives  43.5 us (23%)
  local copies, waits for them, and re-layouts  29.5 us (15%)
  starting transfers between devices  20.2 us (11%)
  matrix products  13.9 us (7%)
  Pallas kernels  12.5 us (7%)
  other arithmetic  9.4 us (5%)
    ppermute x24, waiting for transfers between devices, swap(): return lax.ppermute(value, AXIS, [(i, i ^ bit) for i in range(devices)])  44.3 us
    all_gather x1, blocking collectives, on_device(): mixing_all = lax.all_gather(mixing, AXIS, axis=0, tiled=True)  43.5 us
    unnamed x19, local copies, waits for them, and re-layouts  22.4 us
    ppermute x6, waiting for transfers between devices, shift(): lax.ppermute(value, AXIS, [(i, (i + SLICES * by) % devices) for i in rang...  16.6 us
    ppermute x24, starting transfers between devices, swap(): return lax.ppermute(value, AXIS, [(i, i ^ bit) for i in range(devices)])  13.4 us
    pallas_call x1, Pallas kernels, attend(): pl.pallas_call(attend_kernel, grid_spec=pltpu.PrefetchScalarGridSpec(num_...  12.5 us
    ppermute x6, starting transfers between devices, shift(): lax.ppermute(value, AXIS, [(i, (i + SLICES * by) % devices) for i in rang...  6.87 us
    dot_general x2, matrix products, inner_of(): jnp.dot(arrived, entry_other, preferred_element_type=jnp.float32)  6.44 us
  transfers between devices with their start and end apart: 30, of which 15 were waited for; matrix products, arithmetic and copies ran while one was open for 23% of the time, Pallas kernels for 7%

profile of v1, /device:TPU:0, one launch (start us, length us, event | category | flops | bytes accessed | tf_op | source)
XLA Modules:
  0.0 191.1 jit_solution(4649488178985501713)
XLA Ops:
  2.1 5.5 %dynamic-slice_bitcast_fusion.2 = (bf16[3584,256]{1,0:T(8,128)(2,1)}, bf16[3584,256]{1,0:T(8,128)(2,1)S(1)}, bf16[3584,256]{1,0:T(8,128)(2,1)S(1)}, bf16[3584,256]{1,0:T(8,128)(2,1)}) fusion(bf16[1,7168,256]{2,1,0:T(8,128)(2,1)} %param.15, s32[]{:T(128)S(6)} %select_n.102, s32[]{:T(128)S(6)} %select_n.103, bf16[1,7168,256]{2,1,0:T(8,128)(2,1)} %param.14), kind=kLoop, calls=%fused_computation.13 | loop fusion | bytes 14680072 | tf_op jit(solution)/shard_map/dynamic_slice | solution.py:109
  7.7 2.2 %pad_maximum_fusion.1 = bf16[3584,512]{1,0:T(8,128)(2,1)} fusion(bf16[3584,256]{1,0:T(8,128)(2,1)S(1)} %get-tuple-element.11, bf16[3584,256]{1,0:T(8,128)(2,1)S(1)} %get-tuple-element.48), kind=kLoop, calls=%fused_computation.3 | loop fusion | flops 7340032 | bytes 7340032 | tf_op jit(solution)/shard_map/concatenate | solution.py:111
  11.1 1.5 broadcast_select_fusion.1
  12.9 43.5 %all-gather = f32[32,16,4]{1,2,0:T(4,128)S(1)} all-gather(f32[1,16,4]{1,2,0:T(4,128)S(1)} %bitcast.147), channel_id=1, replica_groups=mesh['groups'=1,'expert'=32] {'expert'}, dimensions={0}, use_global_device_ids=true | all-gather | bytes 8448 | tf_op jit(solution)/shard_map/all_gather | solution.py:129
  57.2 1.9 %collective-permute-start.17 = (bf16[32,3584]{1,0:T(8,128)(2,1)S(1)}, bf16[32,3584]{1,0:T(8,128)(2,1)S(1)}, u32[]{:S(2)}, u32[]{:S(2)}) collective-permute-start(bf16[32,3584]{1,0:T(8,128)(2,1)S(1)} %maximum_select_fusion), channel_id=1, source_target_pairs={{0,8},{1,9},{2,10},{3,11},{4,12},{5,13},{6,14},{7,15},{8,16},{9,17... | collective-permute-start | bytes 688136 | tf_op jit(solution)/shard_map/ppermute | solution.py:85
  59.2 7.0 %collective-permute-done.1 = bf16[32,3584]{1,0:T(8,128)(2,1)S(1)} collective-permute-done((bf16[32,3584]{1,0:T(8,128)(2,1)S(1)}, bf16[32,3584]{1,0:T(8,128)(2,1)S(1)}, u32[]{:S(2)}, u32[]{:S(2)}) %collective-permute-start.1) | collective-permute-done | bytes 229408 | tf_op jit(solution)/shard_map/ppermute | solution.py:85
  66.2 9.7 %collective-permute-done.2 = bf16[32,3584]{1,0:T(8,128)(2,1)S(1)} collective-permute-done((bf16[32,3584]{1,0:T(8,128)(2,1)S(1)}, bf16[32,3584]{1,0:T(8,128)(2,1)S(1)}, u32[]{:S(2)}, u32[]{:S(2)}) %collective-permute-start.2) | collective-permute-done | bytes 229408 | tf_op jit(solution)/shard_map/ppermute | solution.py:85
  76.2 2.1 %collective-permute-start.18 = (bf16[2,32,1792]{2,1,0:T(8,128)(2,1)S(1)}, bf16[2,32,1792]{2,1,0:T(8,128)(2,1)S(1)}, u32[]{:S(2)}, u32[]{:S(2)}) collective-permute-start(bf16[2,32,1792]{2,1,0:T(8,128)(2,1)S(1)} %get-tuple-element.35), channel_id=1, source_target_pairs={{0,2},{1,3},{2,0},{3,1},{4,6},{5,7},{6,4},{7,5},{8,10},{9,11},{10,... | collective-permute-start | bytes 688136 | tf_op jit(solution)/shard_map/ppermute | solution.py:82
  78.3 4.7 %collective-permute-done.5 = bf16[2,32,1792]{2,1,0:T(8,128)(2,1)S(1)} collective-permute-done((bf16[2,32,1792]{2,1,0:T(8,128)(2,1)S(1)}, bf16[2,32,1792]{2,1,0:T(8,128)(2,1)S(1)}, u32[]{:S(2)}, u32[]{:S(2)}) %collective-permute-start.5) | collective-permute-done | bytes 229408 | tf_op jit(solution)/shard_map/ppermute | solution.py:82
  83.4 1.3 collective-permute-done.3
  84.7 4.8 %collective-permute-done.18 = bf16[2,32,1792]{2,1,0:T(8,128)(2,1)S(1)} collective-permute-done((bf16[2,32,1792]{2,1,0:T(8,128)(2,1)S(1)}, bf16[2,32,1792]{2,1,0:T(8,128)(2,1)S(1)}, u32[]{:S(2)}, u32[]{:S(2)}) %collective-permute-start.18) | collective-permute-done | bytes 229408 | tf_op jit(solution)/shard_map/ppermute | solution.py:82
  89.6 2.0 %collective-permute-start.4 = (bf16[2,2,32,1792]{3,2,1,0:T(8,128)(2,1)S(1)}, bf16[2,2,32,1792]{3,2,1,0:T(8,128)(2,1)S(1)}, u32[]{:S(2)}, u32[]{:S(2)}) collective-permute-start(bf16[2,2,32,1792]{3,2,1,0:T(8,128)(2,1)S(1)} %get-tuple-element.17), channel_id=1, source_target_pairs={{0,4},{1,5},{2,6},{3,7},{4,0},{5,1},{6,2},{7,3},{8,12},{9,13},{10,... | collective-permute-start | bytes 1376264 | tf_op jit(solution)/shard_map/ppermute | solution.py:82
  91.8 6.1 %collective-permute-done.6 = bf16[2,2,32,1792]{3,2,1,0:T(8,128)(2,1)S(1)} collective-permute-done((bf16[2,2,32,1792]{3,2,1,0:T(8,128)(2,1)S(1)}, bf16[2,2,32,1792]{3,2,1,0:T(8,128)(2,1)S(1)}, u32[]{:S(2)}, u32[]{:S(2)}) %collective-permute-start.6) | collective-permute-done | bytes 458784 | tf_op jit(solution)/shard_map/ppermute | solution.py:82
  98.2 4.8 %collective-permute-done.4 = bf16[2,2,32,1792]{3,2,1,0:T(8,128)(2,1)S(1)} collective-permute-done((bf16[2,2,32,1792]{3,2,1,0:T(8,128)(2,1)S(1)}, bf16[2,2,32,1792]{3,2,1,0:T(8,128)(2,1)S(1)}, u32[]{:S(2)}, u32[]{:S(2)}) %collective-permute-start.4) | collective-permute-done | bytes 458784 | tf_op jit(solution)/shard_map/ppermute | solution.py:82
  103.2 3.1 %fusion.45 = f32[256,512]{1,0:T(8,128)S(1)} fusion(bf16[256,3584]{1,0:T(8,128)(2,1)S(1)} %bitcast.135, bf16[3584,512]{1,0:T(8,128)(2,1)} %collective-permute-done.7), kind=kOutput, calls=%fused_computation.125 | convolution fusion | flops 939524096 | bytes 6029312 | tf_op jit(solution)/shard_map/dot_general | solution.py:155
  106.4 2.5 %collective-permute-done.19 = bf16[2,2,32,1792]{3,2,1,0:T(8,128)(2,1)S(1)} collective-permute-done((bf16[2,2,32,1792]{3,2,1,0:T(8,128)(2,1)S(1)}, bf16[2,2,32,1792]{3,2,1,0:T(8,128)(2,1)S(1)}, u32[]{:S(2)}, u32[]{:S(2)}) %collective-permute-start.19) | collective-permute-done | bytes 458784 | tf_op jit(solution)/shard_map/ppermute | solution.py:82
  109.2 3.3 %fusion.46 = f32[256,512]{1,0:T(8,128)S(1)} fusion(bf16[256,3584]{1,0:T(8,128)(2,1)S(1)} %bitcast.137, bf16[3584,512]{1,0:T(8,128)(2,1)} %collective-permute-done.7), kind=kOutput, calls=%fused_computation.126 | convolution fusion | flops 939524096 | bytes 6029312 | tf_op jit(solution)/shard_map/dot_general | solution.py:155
  115.9 2.6 %convolution_multiply_fusion.1 = f32[256,3584]{1,0:T(8,128)S(1)} fusion(bf16[256,3584]{1,0:T(8,128)(2,1)} %collective-permute-done.10, bf16[256,3584]{1,0:T(8,128)(2,1)S(1)} %get-tuple-element.12, f32[256]{0:T(256)S(1)} %mul.54, bf16[256,256]{1,0:T(8,128)(2,1)S(1)} %collective-permute-done.9, bf16[256,256]{1,0:T(8,128)(2,1)S(1)} %fusion.17), kind=kOutput, calls=%fused_computation.1 | convolution fusion | flops 948305920 | bytes 7603200 | tf_op jit(solution)/shard_map/dot_general | solution.py:181
  118.7 1.5 collective-permute-start.11
  120.8 2.6 %convolution_multiply_fusion = f32[256,3584]{1,0:T(8,128)S(1)} fusion(bf16[256,3584]{1,0:T(8,128)(2,1)} %collective-permute-done.10, bf16[256,3584]{1,0:T(8,128)(2,1)S(1)} %get-tuple-element.12, f32[256]{0:T(256)S(1)} %mul.59, bf16[256,256]{1,0:T(8,128)(2,1)S(1)} %collective-permute-done.23, bf16[256,256]{1,0:T(8,128)(2,1)S(1)} %fusion.16), kind=kOutput, calls=%fused_computation | convolution fusion | flops 948305920 | bytes 7603200 | tf_op jit(solution)/shard_map/dot_general | solution.py:181
  124.2 1.5 collective-permute-start.26
  125.7 6.4 %collective-permute-done.11 = bf16[2,2,32,1792]{3,2,1,0:T(8,128)(2,1)S(1)} collective-permute-done((bf16[2,2,32,1792]{3,2,1,0:T(8,128)(2,1)S(1)}, bf16[2,2,32,1792]{3,2,1,0:T(8,128)(2,1)S(1)}, u32[]{:S(2)}, u32[]{:S(2)}) %collective-permute-start.11) | collective-permute-done | bytes 458784 | tf_op jit(solution)/shard_map/ppermute | solution.py:82
  132.1 1.5 collective-permute-done.13
  135.1 6.8 %collective-permute-done.24 = bf16[2,2,32,1792]{3,2,1,0:T(8,128)(2,1)S(1)} collective-permute-done((bf16[2,2,32,1792]{3,2,1,0:T(8,128)(2,1)S(1)}, bf16[2,2,32,1792]{3,2,1,0:T(8,128)(2,1)S(1)}, u32[]{:S(2)}, u32[]{:S(2)}) %collective-permute-start.24) | collective-permute-done | bytes 458784 | tf_op jit(solution)/shard_map/ppermute | solution.py:82
  141.9 1.5 collective-permute-done.26
  145.0 3.3 %collective-permute-done.12 = bf16[2,32,1792]{2,1,0:T(8,128)(2,1)S(1)} collective-permute-done((bf16[2,32,1792]{2,1,0:T(8,128)(2,1)S(1)}, bf16[2,32,1792]{2,1,0:T(8,128)(2,1)S(1)}, u32[]{:S(2)}, u32[]{:S(2)}) %collective-permute-start.12) | collective-permute-done | bytes 229408 | tf_op jit(solution)/shard_map/ppermute | solution.py:82
  149.3 2.7 %collective-permute-start.16 = (bf16[32,3584]{1,0:T(8,128)(2,1)}, bf16[32,3584]{1,0:T(8,128)(2,1)}, u32[]{:S(2)}, u32[]{:S(2)}) collective-permute-start(bf16[32,3584]{1,0:T(8,128)(2,1)} %get-tuple-element.15), channel_id=1, source_target_pairs={{0,16},{1,17},{2,18},{3,19},{4,20},{5,21},{6,22},{7,23},{8,24},{9,... | collective-permute-start | bytes 688136 | tf_op jit(solution)/shard_map/ppermute | solution.py:85
  153.1 2.1 %collective-permute-start.28 = (bf16[32,3584]{1,0:T(8,128)(2,1)}, bf16[32,3584]{1,0:T(8,128)(2,1)}, u32[]{:S(2)}, u32[]{:S(2)}) collective-permute-start(bf16[32,3584]{1,0:T(8,128)(2,1)} %fusion.28), channel_id=1, source_target_pairs={{0,24},{1,25},{2,26},{3,27},{4,28},{5,29},{6,30},{7,31},{8,0},{9,1... | collective-permute-start | bytes 688136 | tf_op jit(solution)/shard_map/ppermute | solution.py:85
  155.2 14.1 %copy.48.cache_ref = bf16[16,512,576]{2,1,0:T(8,128)(2,1)} copy(bf16[16,512,576]{1,2,0:T(8,128)(2,1)} %param.18) | data formatting | bytes 18874368 | tf_op args[7]
  169.3 3.1 %copy.47.queries_ref = bf16[16,128,576]{2,1,0:T(8,128)(2,1)S(1)} copy(bf16[16,128,576]{1,2,0:T(8,128)(2,1)} %param.17) | data formatting | bytes 4718592 | tf_op args[6]
  173.8 4.0 %copy-done = bf16[16,512,576]{2,1,0:T(8,128)(2,1)S(1)} copy-done((bf16[16,512,576]{2,1,0:T(8,128)(2,1)S(1)}, bf16[16,512,576]{2,1,0:T(8,128)(2,1)}, u32[]{:S(2)}) %copy-start) | copy-done | bytes 9437208
  177.8 12.5 %latent_attention.1 = bf16[16,128,512]{2,1,0:T(8,128)(2,1)} custom-call(s32[16]{0:T(128)S(1)} %copy-done.1, bf16[16,128,576]{2,1,0:T(8,128)(2,1)S(1)} %copy.47.queries_ref, bf16[16,512,576]{2,1,0:T(8,128)(2,1)S(1)} %copy-done), custom_call_target="tpu_custom_call" | custom-call | flops 2281701376 | bytes 13893632 | tf_op jit(solution)/shard_map/latent_attention/pallas_call | solution.py:40
  (111 shorter events, 17.7 us)
Async XLA Ops:
  1.6 55.4 %collective-permute-start = (bf16[16,3584]{1,0:T(8,128)(2,1)S(1)}, bf16[16,3584]{1,0:T(8,128)(2,1)S(1)}, u32[]{:S(2)}, u32[]{:S(2)}) collective-permute-start(bf16[16,3584]{1,0:T(8,128)(2,1)S(1)} %get-tuple-element.43), channel_id=1, source_target_pairs={{0,1},{1,0},{2,3},{3,2},{4,5},{5,4},{6,7},{7,6},{8,9},{9,8},{10,11... | collective-permute-start | bytes 344072 | tf_op jit(solution)/shard_map/ppermute | solution.py:82
  9.8 93.3 %collective-permute-start.7 = (bf16[3584,512]{1,0:T(8,128)(2,1)}, bf16[3584,512]{1,0:T(8,128)(2,1)}, u32[]{:S(2)}, u32[]{:S(2)}) collective-permute-start(bf16[3584,512]{1,0:T(8,128)(2,1)} %pad_maximum_fusion.1), channel_id=1, source_target_pairs={{0,1},{1,0},{2,3},{3,2},{4,5},{5,4},{6,7},{7,6},{8,9},{9,8},{10,11... | collective-permute-start | bytes 11010056 | tf_op jit(solution)/shard_map/ppermute | solution.py:82
  12.5 103.4 %collective-permute-start.10 = (bf16[256,3584]{1,0:T(8,128)(2,1)}, bf16[256,3584]{1,0:T(8,128)(2,1)}, u32[]{:S(2)}, u32[]{:S(2)}) collective-permute-start(bf16[256,3584]{1,0:T(8,128)(2,1)} %get-tuple-element.13), channel_id=1, source_target_pairs={{0,1},{1,0},{2,3},{3,2},{4,5},{5,4},{6,7},{7,6},{8,9},{9,8},{10,11... | collective-permute-start | bytes 5505032 | tf_op jit(solution)/shard_map/ppermute | solution.py:82
  57.1 9.1 %collective-permute-start.1 = (bf16[32,3584]{1,0:T(8,128)(2,1)S(1)}, bf16[32,3584]{1,0:T(8,128)(2,1)S(1)}, u32[]{:S(2)}, u32[]{:S(2)}) collective-permute-start(bf16[32,3584]{1,0:T(8,128)(2,1)S(1)} %maximum_select_fusion), channel_id=1, source_target_pairs={{0,24},{1,25},{2,26},{3,27},{4,28},{5,29},{6,30},{7,31},{8,0},{9,1... | collective-permute-start | bytes 688136 | tf_op jit(solution)/shard_map/ppermute | solution.py:85
  57.2 18.7 %collective-permute-start.2 = (bf16[32,3584]{1,0:T(8,128)(2,1)S(1)}, bf16[32,3584]{1,0:T(8,128)(2,1)S(1)}, u32[]{:S(2)}, u32[]{:S(2)}) collective-permute-start(bf16[32,3584]{1,0:T(8,128)(2,1)S(1)} %maximum_select_fusion), channel_id=1, source_target_pairs={{0,16},{1,17},{2,18},{3,19},{4,20},{5,21},{6,22},{7,23},{8,24},{9,... | collective-permute-start | bytes 688136 | tf_op jit(solution)/shard_map/ppermute | solution.py:85
  57.2 18.9 %collective-permute-start.17 = (bf16[32,3584]{1,0:T(8,128)(2,1)S(1)}, bf16[32,3584]{1,0:T(8,128)(2,1)S(1)}, u32[]{:S(2)}, u32[]{:S(2)}) collective-permute-start(bf16[32,3584]{1,0:T(8,128)(2,1)S(1)} %maximum_select_fusion), channel_id=1, source_target_pairs={{0,8},{1,9},{2,10},{3,11},{4,12},{5,13},{6,14},{7,15},{8,16},{9,17... | collective-permute-start | bytes 688136 | tf_op jit(solution)/shard_map/ppermute | solution.py:85
  75.9 7.1 %collective-permute-start.5 = (bf16[2,32,1792]{2,1,0:T(8,128)(2,1)S(1)}, bf16[2,32,1792]{2,1,0:T(8,128)(2,1)S(1)}, u32[]{:S(2)}, u32[]{:S(2)}) collective-permute-start(bf16[2,32,1792]{2,1,0:T(8,128)(2,1)S(1)} %get-tuple-element.33), channel_id=1, source_target_pairs={{0,4},{1,5},{2,6},{3,7},{4,0},{5,1},{6,2},{7,3},{8,12},{9,13},{10,... | collective-permute-start | bytes 688136 | tf_op jit(solution)/shard_map/ppermute | solution.py:82
  76.0 8.6 %collective-permute-start.3 = (bf16[2,32,1792]{2,1,0:T(8,128)(2,1)S(1)}, bf16[2,32,1792]{2,1,0:T(8,128)(2,1)S(1)}, u32[]{:S(2)}, u32[]{:S(2)}) collective-permute-start(bf16[2,32,1792]{2,1,0:T(8,128)(2,1)S(1)} %get-tuple-element.27), channel_id=1, source_target_pairs={{0,2},{1,3},{2,0},{3,1},{4,6},{5,7},{6,4},{7,5},{8,10},{9,11},{10,... | collective-permute-start | bytes 688136 | tf_op jit(solution)/shard_map/ppermute | solution.py:82
  76.2 13.4 %collective-permute-start.18 = (bf16[2,32,1792]{2,1,0:T(8,128)(2,1)S(1)}, bf16[2,32,1792]{2,1,0:T(8,128)(2,1)S(1)}, u32[]{:S(2)}, u32[]{:S(2)}) collective-permute-start(bf16[2,32,1792]{2,1,0:T(8,128)(2,1)S(1)} %get-tuple-element.35), channel_id=1, source_target_pairs={{0,2},{1,3},{2,0},{3,1},{4,6},{5,7},{6,4},{7,5},{8,10},{9,11},{10,... | collective-permute-start | bytes 688136 | tf_op jit(solution)/shard_map/ppermute | solution.py:82
  83.0 8.6 %collective-permute-start.20 = (bf16[2,32,1792]{2,1,0:T(8,128)(2,1)S(1)}, bf16[2,32,1792]{2,1,0:T(8,128)(2,1)S(1)}, u32[]{:S(2)}, u32[]{:S(2)}) collective-permute-start(bf16[2,32,1792]{2,1,0:T(8,128)(2,1)S(1)} %get-tuple-element.41), channel_id=1, source_target_pairs={{0,4},{1,5},{2,6},{3,7},{4,0},{5,1},{6,2},{7,3},{8,12},{9,13},{10,... | collective-permute-start | bytes 688136 | tf_op jit(solution)/shard_map/ppermute | solution.py:82
  84.6 13.3 %collective-permute-start.6 = (bf16[2,2,32,1792]{3,2,1,0:T(8,128)(2,1)S(1)}, bf16[2,2,32,1792]{3,2,1,0:T(8,128)(2,1)S(1)}, u32[]{:S(2)}, u32[]{:S(2)}) collective-permute-start(bf16[2,2,32,1792]{3,2,1,0:T(8,128)(2,1)S(1)} %get-tuple-element.19), channel_id=1, source_target_pairs={{0,2},{1,3},{2,0},{3,1},{4,6},{5,7},{6,4},{7,5},{8,10},{9,11},{10,... | collective-permute-start | bytes 1376264 | tf_op jit(solution)/shard_map/ppermute | solution.py:82
  89.6 13.5 %collective-permute-start.4 = (bf16[2,2,32,1792]{3,2,1,0:T(8,128)(2,1)S(1)}, bf16[2,2,32,1792]{3,2,1,0:T(8,128)(2,1)S(1)}, u32[]{:S(2)}, u32[]{:S(2)}) collective-permute-start(bf16[2,2,32,1792]{3,2,1,0:T(8,128)(2,1)S(1)} %get-tuple-element.17), channel_id=1, source_target_pairs={{0,4},{1,5},{2,6},{3,7},{4,0},{5,1},{6,2},{7,3},{8,12},{9,13},{10,... | collective-permute-start | bytes 1376264 | tf_op jit(solution)/shard_map/ppermute | solution.py:82
  91.6 17.3 %collective-permute-start.19 = (bf16[2,2,32,1792]{3,2,1,0:T(8,128)(2,1)S(1)}, bf16[2,2,32,1792]{3,2,1,0:T(8,128)(2,1)S(1)}, u32[]{:S(2)}, u32[]{:S(2)}) collective-permute-start(bf16[2,2,32,1792]{3,2,1,0:T(8,128)(2,1)S(1)} %get-tuple-element.21), channel_id=1, source_target_pairs={{0,4},{1,5},{2,6},{3,7},{4,0},{5,1},{6,2},{7,3},{8,12},{9,13},{10,... | collective-permute-start | bytes 1376264 | tf_op jit(solution)/shard_map/ppermute | solution.py:82
  97.9 11.0 %collective-permute-start.21 = (bf16[2,2,32,1792]{3,2,1,0:T(8,128)(2,1)S(1)}, bf16[2,2,32,1792]{3,2,1,0:T(8,128)(2,1)S(1)}, u32[]{:S(2)}, u32[]{:S(2)}) collective-permute-start(bf16[2,2,32,1792]{3,2,1,0:T(8,128)(2,1)S(1)} %get-tuple-element.23), channel_id=1, source_target_pairs={{0,2},{1,3},{2,0},{3,1},{4,6},{5,7},{6,4},{7,5},{8,10},{9,11},{10,... | collective-permute-start | bytes 1376264 | tf_op jit(solution)/shard_map/ppermute | solution.py:82
  106.3 6.3 %collective-permute-start.8 = (f32[256,512]{1,0:T(8,128)S(1)}, f32[256,512]{1,0:T(8,128)S(1)}, u32[]{:S(2)}, u32[]{:S(2)}) collective-permute-start(f32[256,512]{1,0:T(8,128)S(1)} %fusion.45), channel_id=1, source_target_pairs={{0,1},{1,0},{2,3},{3,2},{4,5},{5,4},{6,7},{7,6},{8,9},{9,8},{10,11... | collective-permute-start | bytes 1572872 | tf_op jit(solution)/shard_map/ppermute | solution.py:82
  112.5 2.0 %collective-permute-start.22 = (f32[256,512]{1,0:T(8,128)S(1)}, f32[256,512]{1,0:T(8,128)S(1)}, u32[]{:S(2)}, u32[]{:S(2)}) collective-permute-start(f32[256,512]{1,0:T(8,128)S(1)} %fusion.46), channel_id=1, source_target_pairs={{0,1},{1,0},{2,3},{3,2},{4,5},{5,4},{6,7},{7,6},{8,9},{9,8},{10,11... | collective-permute-start | bytes 1572872 | tf_op jit(solution)/shard_map/ppermute | solution.py:82
  113.8 2.1 %collective-permute-start.9 = (bf16[256,256]{1,0:T(8,128)(2,1)S(1)}, bf16[256,256]{1,0:T(8,128)(2,1)S(1)}, u32[]{:S(2)}, u32[]{:S(2)}) collective-permute-start(bf16[256,256]{1,0:T(8,128)(2,1)S(1)} %fusion.17), channel_id=1, source_target_pairs={{0,1},{1,0},{2,3},{3,2},{4,5},{5,4},{6,7},{7,6},{8,9},{9,8},{10,11... | collective-permute-start | bytes 393224 | tf_op jit(solution)/shard_map/ppermute | solution.py:82
  115.7 5.0 %collective-permute-start.23 = (bf16[256,256]{1,0:T(8,128)(2,1)S(1)}, bf16[256,256]{1,0:T(8,128)(2,1)S(1)}, u32[]{:S(2)}, u32[]{:S(2)}) collective-permute-start(bf16[256,256]{1,0:T(8,128)(2,1)S(1)} %fusion.16), channel_id=1, source_target_pairs={{0,1},{1,0},{2,3},{3,2},{4,5},{5,4},{6,7},{7,6},{8,9},{9,8},{10,11... | collective-permute-start | bytes 393224 | tf_op jit(solution)/shard_map/ppermute | solution.py:82
  118.7 13.4 %collective-permute-start.11 = (bf16[2,2,32,1792]{3,2,1,0:T(8,128)(2,1)S(1)}, bf16[2,2,32,1792]{3,2,1,0:T(8,128)(2,1)S(1)}, u32[]{:S(2)}, u32[]{:S(2)}) collective-permute-start(bf16[2,2,32,1792]{3,2,1,0:T(8,128)(2,1)S(1)} %slice_bitcast_fusion.11), channel_id=1, source_target_pairs={{0,4},{1,5},{2,6},{3,7},{4,0},{5,1},{6,2},{7,3},{8,12},{9,13},{10,... | collective-permute-start | bytes 1376264 | tf_op jit(solution)/shard_map/ppermute | solution.py:82
  120.2 13.4 %collective-permute-start.13 = (bf16[2,2,32,1792]{3,2,1,0:T(8,128)(2,1)S(1)}, bf16[2,2,32,1792]{3,2,1,0:T(8,128)(2,1)S(1)}, u32[]{:S(2)}, u32[]{:S(2)}) collective-permute-start(bf16[2,2,32,1792]{3,2,1,0:T(8,128)(2,1)S(1)} %slice_bitcast_fusion.9), channel_id=1, source_target_pairs={{0,2},{1,3},{2,0},{3,1},{4,6},{5,7},{6,4},{7,5},{8,10},{9,11},{10,... | collective-permute-start | bytes 1376264 | tf_op jit(solution)/shard_map/ppermute | solution.py:82
  123.4 18.5 %collective-permute-start.24 = (bf16[2,2,32,1792]{3,2,1,0:T(8,128)(2,1)S(1)}, bf16[2,2,32,1792]{3,2,1,0:T(8,128)(2,1)S(1)}, u32[]{:S(2)}, u32[]{:S(2)}) collective-permute-start(bf16[2,2,32,1792]{3,2,1,0:T(8,128)(2,1)S(1)} %slice_bitcast_fusion.7), channel_id=1, source_target_pairs={{0,4},{1,5},{2,6},{3,7},{4,0},{5,1},{6,2},{7,3},{8,12},{9,13},{10,... | collective-permute-start | bytes 1376264 | tf_op jit(solution)/shard_map/ppermute | solution.py:82
  124.2 19.2 %collective-permute-start.26 = (bf16[2,2,32,1792]{3,2,1,0:T(8,128)(2,1)S(1)}, bf16[2,2,32,1792]{3,2,1,0:T(8,128)(2,1)S(1)}, u32[]{:S(2)}, u32[]{:S(2)}) collective-permute-start(bf16[2,2,32,1792]{3,2,1,0:T(8,128)(2,1)S(1)} %slice_bitcast_fusion.5), channel_id=1, source_target_pairs={{0,2},{1,3},{2,0},{3,1},{4,6},{5,7},{6,4},{7,5},{8,10},{9,11},{10,... | collective-permute-start | bytes 1376264 | tf_op jit(solution)/shard_map/ppermute | solution.py:82
  133.8 14.5 %collective-permute-start.12 = (bf16[2,32,1792]{2,1,0:T(8,128)(2,1)S(1)}, bf16[2,32,1792]{2,1,0:T(8,128)(2,1)S(1)}, u32[]{:S(2)}, u32[]{:S(2)}) collective-permute-start(bf16[2,32,1792]{2,1,0:T(8,128)(2,1)S(1)} %fusion.24), channel_id=1, source_target_pairs={{0,2},{1,3},{2,0},{3,1},{4,6},{5,7},{6,4},{7,5},{8,10},{9,11},{10,... | collective-permute-start | bytes 688136 | tf_op jit(solution)/shard_map/ppermute | solution.py:82
  134.4 13.9 %collective-permute-start.14 = (bf16[2,32,1792]{2,1,0:T(8,128)(2,1)S(1)}, bf16[2,32,1792]{2,1,0:T(8,128)(2,1)S(1)}, u32[]{:S(2)}, u32[]{:S(2)}) collective-permute-start(bf16[2,32,1792]{2,1,0:T(8,128)(2,1)S(1)} %fusion.25), channel_id=1, source_target_pairs={{0,4},{1,5},{2,6},{3,7},{4,0},{5,1},{6,2},{7,3},{8,12},{9,13},{10,... | collective-permute-start | bytes 688136 | tf_op jit(solution)/shard_map/ppermute | solution.py:82
  143.6 8.3 %collective-permute-start.27 = (bf16[2,32,1792]{2,1,0:T(8,128)(2,1)S(1)}, bf16[2,32,1792]{2,1,0:T(8,128)(2,1)S(1)}, u32[]{:S(2)}, u32[]{:S(2)}) collective-permute-start(bf16[2,32,1792]{2,1,0:T(8,128)(2,1)S(1)} %fusion.27), channel_id=1, source_target_pairs={{0,4},{1,5},{2,6},{3,7},{4,0},{5,1},{6,2},{7,3},{8,12},{9,13},{10,... | collective-permute-start | bytes 688136 | tf_op jit(solution)/shard_map/ppermute | solution.py:82
  144.3 8.0 %collective-permute-start.25 = (bf16[2,32,1792]{2,1,0:T(8,128)(2,1)S(1)}, bf16[2,32,1792]{2,1,0:T(8,128)(2,1)S(1)}, u32[]{:S(2)}, u32[]{:S(2)}) collective-permute-start(bf16[2,32,1792]{2,1,0:T(8,128)(2,1)S(1)} %fusion.26), channel_id=1, source_target_pairs={{0,2},{1,3},{2,0},{3,1},{4,6},{5,7},{6,4},{7,5},{8,10},{9,11},{10,... | collective-permute-start | bytes 688136 | tf_op jit(solution)/shard_map/ppermute | solution.py:82
  149.3 23.2 %collective-permute-start.15 = (bf16[32,3584]{1,0:T(8,128)(2,1)}, bf16[32,3584]{1,0:T(8,128)(2,1)}, u32[]{:S(2)}, u32[]{:S(2)}) collective-permute-start(bf16[32,3584]{1,0:T(8,128)(2,1)} %get-tuple-element.14), channel_id=1, source_target_pairs={{0,8},{1,9},{2,10},{3,11},{4,12},{5,13},{6,14},{7,15},{8,16},{9,17... | collective-permute-start | bytes 688136 | tf_op jit(solution)/shard_map/ppermute | solution.py:85
  149.3 23.2 %collective-permute-start.16 = (bf16[32,3584]{1,0:T(8,128)(2,1)}, bf16[32,3584]{1,0:T(8,128)(2,1)}, u32[]{:S(2)}, u32[]{:S(2)}) collective-permute-start(bf16[32,3584]{1,0:T(8,128)(2,1)} %get-tuple-element.15), channel_id=1, source_target_pairs={{0,16},{1,17},{2,18},{3,19},{4,20},{5,21},{6,22},{7,23},{8,24},{9,... | collective-permute-start | bytes 688136 | tf_op jit(solution)/shard_map/ppermute | solution.py:85
  153.1 19.3 %collective-permute-start.28 = (bf16[32,3584]{1,0:T(8,128)(2,1)}, bf16[32,3584]{1,0:T(8,128)(2,1)}, u32[]{:S(2)}, u32[]{:S(2)}) collective-permute-start(bf16[32,3584]{1,0:T(8,128)(2,1)} %fusion.28), channel_id=1, source_target_pairs={{0,24},{1,25},{2,26},{3,27},{4,28},{5,29},{6,30},{7,31},{8,0},{9,1... | collective-permute-start | bytes 688136 | tf_op jit(solution)/shard_map/ppermute | solution.py:85
  169.3 4.5 %copy-start.1 = (s32[16]{0:T(128)S(1)}, s32[16]{0:T(128)}, u32[]{:S(2)}) copy-start(s32[16]{0:T(128)} %lengths_ref.1) | copy-start | bytes 196
  173.7 16.6 %collective-permute-start.29 = (bf16[16,3584]{1,0:T(8,128)(2,1)S(1)}, bf16[16,3584]{1,0:T(8,128)(2,1)S(1)}, u32[]{:S(2)}, u32[]{:S(2)}) collective-permute-start(bf16[16,3584]{1,0:T(8,128)(2,1)S(1)} %get-tuple-element.25), channel_id=1, source_target_pairs={{0,1},{1,0},{2,3},{3,2},{4,5},{5,4},{6,7},{7,6},{8,9},{9,8},{10,11... | collective-permute-start | bytes 344072 | tf_op jit(solution)/shard_map/ppermute | solution.py:82
  173.8 4.0 %copy-start = (bf16[16,512,576]{2,1,0:T(8,128)(2,1)S(1)}, bf16[16,512,576]{2,1,0:T(8,128)(2,1)}, u32[]{:S(2)}) copy-start(bf16[16,512,576]{2,1,0:T(8,128)(2,1)} %copy.48.cache_ref) | copy-start | bytes 28311556
  (6 other events, 15.4 us)

commit v2 on v1

v2 whole, which is shorter than its diff:
```python
import functools
import math

import jax
import jax.numpy as jnp
from jax import lax
from jax.experimental import pallas as pl
from jax.experimental.pallas import tpu as pltpu
from jax.sharding import PartitionSpec as P

LAT = 512
SLICES = 8
AXIS = "expert"
ATTEND_CALLS = 4
ATTEND_TOGETHER = 4

score_scale = 0.07216878364870322

SMALL = pl.CostEstimate(flops=1, bytes_accessed=1, transcendentals=0)


def attend_kernel(lengths_ref, queries_ref, cache_ref, *refs, first):
    out_ref = refs[-1]
    each = out_ref.shape[0]
    masked = []
    for at in range(each):
        length = lengths_ref[first + pl.program_id(0) * each + at]
        scores = lax.dot_general(
            queries_ref[at],
            cache_ref[at],
            (((0,), (0,)), ((), ())),
            preferred_element_type=jnp.float32,
        )
        positions = lax.broadcasted_iota(jnp.int32, scores.shape, 1)
        masked.append(jnp.where(positions < length, scores * score_scale, -jnp.inf))
    weights = []
    for scores in masked:
        raised = jnp.exp(scores - jnp.max(scores, axis=-1, keepdims=True))
        weights.append((raised / jnp.sum(raised, axis=-1, keepdims=True)).astype(jnp.bfloat16))
    for at in range(each):
        out_ref[at] = lax.dot_general(
            weights[at],
            cache_ref[at, :LAT],
            (((1,), (1,)), ((), ())),
            preferred_element_type=jnp.float32,
        ).astype(jnp.bfloat16)


def attend(queries, latent_cache, lengths, first, count, held):
    requests, width, heads = queries.shape
    context = latent_cache.shape[2]
    aliases = {} if held is None else {3: 0}
    operands = (lengths, queries, latent_cache) + (() if held is None else (held,))
    each = math.gcd(count, ATTEND_TOGETHER)
    block = first // each
    return pl.pallas_call(
        functools.partial(attend_kernel, first=first),
        grid_spec=pltpu.PrefetchScalarGridSpec(
            num_scalar_prefetch=1,
            grid=(count // each,),
            in_specs=[
                pl.BlockSpec((each, width, heads), lambda i, _: (block + i, 0, 0)),
                pl.BlockSpec((each, width, context), lambda i, _: (block + i, 0, 0)),
            ]
            + ([] if held is None else [pl.BlockSpec(memory_space=pl.ANY)]),
            out_specs=pl.BlockSpec((each, heads, LAT), lambda i, _: (block + i, 0, 0)),
        ),
        out_shape=jax.ShapeDtypeStruct((requests, heads, LAT), jnp.bfloat16),
        input_output_aliases=aliases,
        compiler_params=pltpu.CompilerParams(vmem_limit_bytes=20 * 1024 * 1024),
        cost_estimate=SMALL,
        name="latent_attention",
    )(*operands)


def tile_of(half):
    return half // next(n for n in (7, 4, 2, 1) if half % (n * 128) == 0)


def entry_half_kernel(_, gate_ref, up_ref, out_ref):
    out_ref[0] = gate_ref[...]
    out_ref[1] = up_ref[...]


def entry_half(core, gate, up):
    width, units = gate.shape
    tile = tile_of(width // 2)
    steps = width // 2 // tile
    spec = pl.BlockSpec((tile, units), lambda i, core: ((1 - core[0]) * steps + i, 0))
    return pl.pallas_call(
        entry_half_kernel,
        grid_spec=pltpu.PrefetchScalarGridSpec(
            num_scalar_prefetch=1,
            grid=(steps,),
            in_specs=[spec, spec],
            out_specs=pl.BlockSpec((2, tile, units), lambda i, core: (0, i, 0)),
        ),
        out_shape=jax.ShapeDtypeStruct((2, width // 2, units), gate.dtype),
        compiler_params=pltpu.CompilerParams(vmem_limit_bytes=48 * 1024 * 1024),
        cost_estimate=SMALL,
        name="entry_half",
    )(core.reshape(1), gate, up)


def exit_half_kernel(_, given_ref, kept_ref, given_out_ref, kept_out_ref):
    given_out_ref[...] = given_ref[...]
    kept_out_ref[...] = kept_ref[...]


def exit_half(core, down):
    units, width = down.shape
    tile = tile_of(width // 2)
    steps = width // 2 // tile
    shape = jax.ShapeDtypeStruct((units, width // 2), down.dtype)
    return pl.pallas_call(
        exit_half_kernel,
        grid_spec=pltpu.PrefetchScalarGridSpec(
            num_scalar_prefetch=1,
            grid=(steps,),
            in_specs=[
                pl.BlockSpec((units, tile), lambda i, core: (0, (1 - core[0]) * steps + i)),
                pl.BlockSpec((units, tile), lambda i, core: (0, core[0] * steps + i)),
            ],
            out_specs=[pl.BlockSpec((units, tile), lambda i, core: (0, i))] * 2,
        ),
        out_shape=[shape, shape],
        compiler_params=pltpu.CompilerParams(vmem_limit_bytes=16 * 1024 * 1024),
        cost_estimate=SMALL,
        name="exit_half",
    )(core.reshape(1), down, down)


def entry_kernel(_, rows_ref, gate_ref, up_ref, out_ref):
    @pl.when(pl.program_id(0) == 0)
    def _():
        out_ref[...] = jnp.zeros_like(out_ref)

    rows = rows_ref[...]
    out_ref[0] += jnp.dot(rows, gate_ref[...], preferred_element_type=jnp.float32)
    out_ref[1] += jnp.dot(rows, up_ref[...], preferred_element_type=jnp.float32)


def entry(rows, core, gate, up):
    count, half = rows.shape
    units = gate.shape[-1]
    steps = next(n for n in (7, 4, 2, 1) if half % (n * 128) == 0)
    tile = half // steps
    if gate.ndim == 3:
        specs = [
            pl.BlockSpec((None, tile, units), lambda i, core: (0, i, 0)),
            pl.BlockSpec((None, tile, units), lambda i, core: (1, i, 0)),
        ]
    else:
        specs = [pl.BlockSpec((tile, units), lambda i, core: (core[0] * steps + i, 0))] * 2
    return pl.pallas_call(
        entry_kernel,
        grid_spec=pltpu.PrefetchScalarGridSpec(
            num_scalar_prefetch=1,
            grid=(steps,),
            in_specs=[pl.BlockSpec((count, tile), lambda i, core: (0, i))] + specs,
            out_specs=pl.BlockSpec((2, count, units), lambda i, core: (0, 0, 0)),
        ),
        out_shape=jax.ShapeDtypeStruct((2, count, units), jnp.float32),
        compiler_params=pltpu.CompilerParams(vmem_limit_bytes=16 * 1024 * 1024),
        cost_estimate=SMALL,
        name="entry_products",
    )(core.reshape(1), rows, gate, up)


def inner_kernel(own_ref, other_ref, out_ref):
    gate_value = own_ref[0] + other_ref[0]
    up_value = own_ref[1] + other_ref[1]
    silu = gate_value / (1.0 + jnp.exp(-gate_value))
    out_ref[...] = (silu * up_value).astype(out_ref.dtype)


def inner_units(own, other):
    return pl.pallas_call(
        inner_kernel,
        in_specs=[pl.BlockSpec(memory_space=pltpu.VMEM)] * 2,
        out_specs=pl.BlockSpec(memory_space=pltpu.VMEM),
        out_shape=jax.ShapeDtypeStruct(own.shape[1:], jnp.bfloat16),
        compiler_params=pltpu.CompilerParams(vmem_limit_bytes=12 * 1024 * 1024),
        cost_estimate=SMALL,
        name="inner_units",
    )(own, other)


def exit_kernel(own_ref, other_ref, down_own_ref, down_other_ref, *out_refs, rows):
    own, other = own_ref[...], other_ref[...]
    quarter = down_own_ref.shape[1] // 2
    tile = math.gcd(quarter, 256)
    for at in range(2 * quarter // tile):
        columns = slice(at * tile, (at + 1) * tile)
        part = jnp.dot(own, down_own_ref[:, columns], preferred_element_type=jnp.float32)
        part += jnp.dot(other, down_other_ref[:, columns], preferred_element_type=jnp.float32)
        second = at * tile >= quarter
        begin = at * tile - (quarter if second else 0)
        columns = slice(begin, begin + tile)
        row = 0
        for first in range(0, len(out_refs), 4):
            kept_a, kept_b, sent_a, sent_b = out_refs[first : first + 4]
            for slot in range(kept_a.shape[1]):
                for y in range(2):
                    for x in range(2):
                        value = part[row : row + rows]
                        row += rows
                        if second:
                            target = sent_b if x else kept_b
                            target[y, slot, :, columns] = value.astype(target.dtype)
                        else:
                            target = sent_a if y else kept_a
                            target[x, slot, :, columns] = value.astype(target.dtype)


def exit_sums(own, other, down_own, down_other, rows, sets):
    quarter = down_own.shape[1] // 2
    shapes = []
    for slots in sets:
        shape = (2, slots, rows, quarter)
        shapes += [jax.ShapeDtypeStruct(shape, jnp.float32)] * 2
        shapes += [jax.ShapeDtypeStruct(shape, jnp.bfloat16)] * 2
    outs = pl.pallas_call(
        functools.partial(exit_kernel, rows=rows),
        in_specs=[pl.BlockSpec(memory_space=pltpu.VMEM)] * 4,
        out_specs=[pl.BlockSpec(memory_space=pltpu.VMEM)] * len(shapes),
        out_shape=shapes,
        compiler_params=pltpu.CompilerParams(vmem_limit_bytes=16 * 1024 * 1024),
        cost_estimate=SMALL,
        name="exit_sums",
    )(own, other, down_own, down_other)
    return [
        (tuple(outs[at : at + 2]), tuple(outs[at + 2 : at + 4])) for at in range(0, len(outs), 4)
    ]


def after(value, *others):
    return lax.optimization_barrier((value,) + others)[0]


def on_device(
    hidden,
    expert_ids,
    route_weights,
    gate_weight,
    up_weight,
    down_weight,
    queries,
    latent_cache,
    lengths,
):
    devices = lax.axis_size(AXIS)
    planes = devices // SLICES
    me = lax.axis_index(AXIS)
    core, plane = me % 2, me // SLICES
    rows, width = hidden.shape
    half, quarter = width // 2, width // 4
    first_core = core == 0

    def swap(value, bit):
        return lax.ppermute(value, AXIS, [(i, i ^ bit) for i in range(devices)])

    def shift(value, by):
        return lax.ppermute(
            value, AXIS, [(i, (i + SLICES * by) % devices) for i in range(devices)]
        )

    in_core = functools.partial(swap, bit=1)
    in_x = functools.partial(swap, bit=2)
    in_y = functools.partial(swap, bit=4)

    low, high = hidden[:, :half], hidden[:, half:]
    kept = jnp.where(first_core, low, high)
    got = in_core(jnp.where(first_core, high, low))
    block = jnp.where(
        first_core, jnp.concatenate([kept, got], 0), jnp.concatenate([got, kept], 0)
    )
    choose = (
        expert_ids[:, :, None] == jnp.arange(planes, dtype=jnp.int32)[None, None, :]
    ).astype(jnp.float32)
    mixing = jnp.sum(route_weights[:, :, None] * choose, axis=1)
    mixing_other = in_core(mixing)
    mixing = jnp.where(
        first_core,
        jnp.concatenate([mixing, mixing_other], 0),
        jnp.concatenate([mixing_other, mixing], 0),
    )

    def mixing_of(expert):
        pick = jnp.arange(planes)[None, :] == expert
        return jnp.sum(jnp.where(pick, mixing, 0.0), axis=1, keepdims=True)

    queries_turned = jnp.swapaxes(queries, 1, 2)
    cache_turned = jnp.swapaxes(latent_cache, 1, 2)
    step = rows // ATTEND_CALLS

    def attend_more(number, held, *others):
        return attend(
            queries_turned, cache_turned, after(lengths, *others), number * step, step, held
        )

    def spread_first(slots):
        part_a = jnp.stack([slot[:, :quarter] for slot in slots])
        part_b = jnp.stack([slot[:, quarter:] for slot in slots])
        return (part_a, part_b), (in_x(part_a), in_y(part_b))

    def spread_second(held, got):
        pair_a = jnp.stack([held[0], got[0]])
        pair_b = jnp.stack([held[1], got[1]])
        return (pair_a, pair_b), (in_y(pair_a), in_x(pair_b))

    def spread_rows(held, got):
        four_a = jnp.stack([held[0], got[0]])
        four_b = jnp.stack([held[1], got[1]], 1)
        four = jnp.concatenate([four_a, four_b], -1)
        return jnp.moveaxis(four, 2, 0).reshape(-1, half)

    def narrow(value):
        return value.astype(jnp.bfloat16)

    def widen(value):
        return value.astype(jnp.float32)

    gate_part, up_part, down_part = gate_weight[0], up_weight[0], down_weight[0]

    def gather_second(kept, got):
        pair_a, pair_b = kept[0] + widen(got[0]), kept[1] + widen(got[1])
        return (pair_a[0], pair_b[0]), (narrow(pair_a[1]), narrow(pair_b[1]))

    def gather_rows(kept, got):
        return jnp.concatenate([kept[0] + widen(got[0]), kept[1] + widen(got[1])], -1)

    def returned(sums, slots):
        return [
            (k, sums[at] if k == 0 else shift(narrow(sums[at]), -k))
            for at, k in enumerate(slots)
        ]

    near, far = list(range(1, planes - 1)), [planes - 1]
    join = lax.optimization_barrier

    slot_near = [shift(block, k) for k in near]
    held, got = spread_first([block])
    core, _ = join((core, block))
    entry_give = entry_half(core, gate_part, up_part)
    held, got, entry_give = join((held, got, entry_give))

    entry_other = in_core(entry_give)
    own, own_got = spread_second(held, got)
    attended = attend_more(0, None, entry_give)
    own, own_got, slot_near, attended, block = join((own, own_got, slot_near, attended, block))

    slot_far = [shift(block, k) for k in far]
    held, got = spread_first(slot_near)
    attended = attend_more(1, attended, block)
    held, got, slot_far, attended = join((held, got, slot_far, attended))

    near_held, near_got = spread_second(held, got)
    held, got = spread_first(slot_far)
    attended = attend_more(2, attended, *slot_far)
    down_give, down_own = exit_half(after(core, *slot_far), down_part)
    near_held, near_got, held, got, attended, down_give, down_own = join(
        (near_held, near_got, held, got, attended, down_give, down_own)
    )
    down_other = in_core(down_give)

    far_held, far_got = spread_second(held, got)
    arrived = jnp.concatenate(
        [spread_rows(own, own_got), spread_rows(near_held, near_got)], 0
    )
    pre_other = in_core(entry(arrived, core, entry_other, entry_other))
    pre_own = entry(arrived, core, gate_part, up_part)
    far_held, far_got, pre_own = join((far_held, far_got, pre_own))

    inner = inner_units(pre_own, pre_other)
    inner_other = in_core(inner)
    (own_kept, own_sent), (near_kept, near_sent) = exit_sums(
        inner, inner_other, down_own, down_other, 2 * rows, [1, len(near)]
    )
    near_sent, far_held, far_got = join((near_sent, far_held, far_got))

    near_got = (in_y(near_sent[0]), in_x(near_sent[1]))
    arrived = spread_rows(far_held, far_got)
    pre_other = in_core(entry(arrived, core, entry_other, entry_other))
    pre_own = entry(arrived, core, gate_part, up_part)
    near_kept, near_got, pre_own, pre_other, attended = join(
        (near_kept, near_got, pre_own, pre_other, attended)
    )

    near_kept, near_sent = gather_second(near_kept, near_got)
    near_got = (in_x(near_sent[0]), in_y(near_sent[1]))
    inner = inner_units(pre_own, pre_other)
    inner_other = in_core(inner)
    [(far_kept, far_sent)] = exit_sums(
        inner, inner_other, down_own, down_other, 2 * rows, [len(far)]
    )
    rest_sent = tuple(jnp.concatenate(pair, 1) for pair in zip(far_sent, own_sent))
    rest_kept = tuple(jnp.concatenate(pair, 1) for pair in zip(far_kept, own_kept))
    near_kept, near_got, rest_kept, rest_sent = join((near_kept, near_got, rest_kept, rest_sent))

    terms = returned(gather_rows(near_kept, near_got), near)
    rest_got = (in_y(rest_sent[0]), in_x(rest_sent[1]))
    attended = attend_more(3, attended, *rest_sent)
    rest_kept, rest_got, attended = join((rest_kept, rest_got, attended))

    rest_kept, rest_sent = gather_second(rest_kept, rest_got)
    rest_got = (in_x(rest_sent[0]), in_y(rest_sent[1]))
    terms += returned(gather_rows(rest_kept, rest_got), far + [0])
    total = 0.0
    for k, term in terms:
        total = total + mixing_of((plane + k) % planes) * widen(term)

    result = narrow(total)
    top, bottom = result[:rows], result[rows:]
    kept = jnp.where(first_core, top, bottom)
    got = in_core(jnp.where(first_core, bottom, top))
    routed = jnp.where(
        first_core, jnp.concatenate([kept, got], 1), jnp.concatenate([got, kept], 1)
    )
    return routed, attended


def solution(mesh):
    in_specs = (
        P(("groups", "expert"), None),
        P(("groups", "expert"), None),
        P(("groups", "expert"), None),
        P("expert", None, None),
        P("expert", None, None),
        P("expert", None, None),
        P(("groups", "expert"), None, None),
        P(("groups", "expert"), None, None),
        P(("groups", "expert")),
    )
    out_specs = (P(("groups", "expert"), None), P(("groups", "expert"), None, None))
    return jax.shard_map(
        on_device, mesh=mesh, in_specs=in_specs, out_specs=out_specs, check_vma=False
    )
```

time: 192 us -> 125 us (0.65)
  blocking collectives: 43.5 us -> 0 us
  local copies, waits for them, and re-layouts: 29.5 us -> 7.01 us
  Pallas kernels: 12.5 us -> 31.9 us
  waiting for transfers between devices: 60.9 us -> 46.4 us
  matrix products: 13.9 us -> 0 us
  starting transfers between devices: 20.2 us -> 32.2 us
  other arithmetic: 9.4 us -> 5.74 us
    all_gather x1 -> x0, blocking collectives: 43.5 us -> none  [on_device(): mixing_all = lax.all_gather(mixing, AXIS, axis=0, tiled=True)]
    pallas_call x1 -> x14, Pallas kernels: 12.5 us -> 31.9 us  [the longest x4 10.9 us: attend(): pl.pallas_call(functools.partial(attend_kernel, first=first), grid_spec=p...]
    unnamed x19 -> x58, local copies, waits for them, and re-layouts: 22.4 us -> 6.5 us
    dot_general x6 -> x0, matrix products: 13.9 us -> none  [the longest x2 6.44 us: inner_of(): jnp.dot(arrived, entry_other, preferred_element_type=jnp.float32)]
    ppermute x24 -> x29, starting transfers between devices: 13.4 us -> 25.3 us  [swap(): return lax.ppermute(value, AXIS, [(i, i ^ bit) for i in range(devices)])]
    ppermute x24 -> x29, waiting for transfers between devices: 44.3 us -> 33.9 us  [swap(): return lax.ppermute(value, AXIS, [(i, i ^ bit) for i in range(devices)])]
    dynamic_slice x1 -> x0, local copies, waits for them, and re-layouts: 5.54 us -> none  [on_device(): up_own = lax.dynamic_slice_in_dim(up_part, core * half, half, 0)]
    ppermute x6, waiting for transfers between devices: 16.6 us -> 12.5 us  [shift(): lax.ppermute(value, AXIS, [(i, (i + SLICES * by) % devices) for i in rang...]
  transfers between devices with their start and end apart: 30 -> 35, of which waited for: 15 -> 20; matrix products, arithmetic and copies ran while one was open for 23% -> 3% of each run, Pallas kernels for 7% -> 24%
where the time goes in v2:
time: 125 us
  waiting for transfers between devices  46.4 us (37%)
  starting transfers between devices  32.2 us (26%)
  Pallas kernels  31.9 us (26%)
  local copies, waits for them, and re-layouts  7.01 us (6%)
  other arithmetic  5.74 us (5%)
  between operations  1.33 us (1%)
    ppermute x29, waiting for transfers between devices, swap(): return lax.ppermute(value, AXIS, [(i, i ^ bit) for i in range(devices)])  33.9 us
    ppermute x29, starting transfers between devices, swap(): return lax.ppermute(value, AXIS, [(i, i ^ bit) for i in range(devices)])  25.3 us
    ppermute x6, waiting for transfers between devices, shift(): lax.ppermute(value, AXIS, [(i, (i + SLICES * by) % devices) for i in rang...  12.5 us
    pallas_call x4, Pallas kernels, attend(): pl.pallas_call(functools.partial(attend_kernel, first=first), grid_spec=p...  10.9 us
    pallas_call x4, Pallas kernels, entry(): pl.pallas_call(entry_kernel, grid_spec=pltpu.PrefetchScalarGridSpec(num_s...  9.67 us
    ppermute x6, starting transfers between devices, shift(): lax.ppermute(value, AXIS, [(i, (i + SLICES * by) % devices) for i in rang...  6.91 us
    unnamed x58, local copies, waits for them, and re-layouts  6.5 us
    pallas_call x1, Pallas kernels, entry_half(): pl.pallas_call(entry_half_kernel, grid_spec=pltpu.PrefetchScalarGridSpec(...  6 us
  transfers between devices with their start and end apart: 35, of which 20 were waited for; matrix products, arithmetic and copies ran while one was open for 3% of the time, Pallas kernels for 24%

profile of v2, /device:TPU:0, one launch (start us, length us, event | category | flops | bytes accessed | tf_op | source)
XLA Modules:
  0.0 124.6 jit_solution(18183803070620133136)
XLA Ops:
  3.2 2.9 %collective-permute-start.2 = (bf16[1,32,1792]{2,1,0:T(8,128)(2,1)S(1)}, bf16[1,32,1792]{2,1,0:T(8,128)(2,1)S(1)}, u32[]{:S(2)}, u32[]{:S(2)}) collective-permute-start(bf16[1,32,1792]{2,1,0:T(8,128)(2,1)S(1)} %get-tuple-element.84), channel_id=1, source_target_pairs={{0,2},{1,3},{2,0},{3,1},{4,6},{5,7},{6,4},{7,5},{8,10},{9,11},{10,... | collective-permute-start | bytes 344072 | tf_op jit(solution)/shard_map/ppermute | solution.py:261
  6.1 1.5 %collective-permute-start.3 = (bf16[1,32,1792]{2,1,0:T(8,128)(2,1)S(1)}, bf16[1,32,1792]{2,1,0:T(8,128)(2,1)S(1)}, u32[]{:S(2)}, u32[]{:S(2)}) collective-permute-start(bf16[1,32,1792]{2,1,0:T(8,128)(2,1)S(1)} %get-tuple-element.86), channel_id=1, source_target_pairs={{0,4},{1,5},{2,6},{3,7},{4,0},{5,1},{6,2},{7,3},{8,12},{9,13},{10,... | collective-permute-start | bytes 344072 | tf_op jit(solution)/shard_map/ppermute | solution.py:261
  7.6 1.6 %collective-permute-start.6 = (bf16[32,3584]{1,0:T(8,128)(2,1)S(1)}, bf16[32,3584]{1,0:T(8,128)(2,1)S(1)}, u32[]{:S(2)}, u32[]{:S(2)}) collective-permute-start(bf16[32,3584]{1,0:T(8,128)(2,1)S(1)} %maximum_select_fusion), channel_id=1, source_target_pairs={{0,8},{1,9},{2,10},{3,11},{4,12},{5,13},{6,14},{7,15},{8,16},{9,17... | collective-permute-start | bytes 688136 | tf_op jit(solution)/shard_map/ppermute | solution.py:264
  9.2 2.6 %collective-permute-start.7 = (bf16[32,3584]{1,0:T(8,128)(2,1)S(1)}, bf16[32,3584]{1,0:T(8,128)(2,1)S(1)}, u32[]{:S(2)}, u32[]{:S(2)}) collective-permute-start(bf16[32,3584]{1,0:T(8,128)(2,1)S(1)} %maximum_select_fusion), channel_id=1, source_target_pairs={{0,16},{1,17},{2,18},{3,19},{4,20},{5,21},{6,22},{7,23},{8,24},{9,... | collective-permute-start | bytes 688136 | tf_op jit(solution)/shard_map/ppermute | solution.py:264
  11.8 6.0 %entry_half.1 = bf16[2,3584,256]{2,1,0:T(8,128)(2,1)S(1)} custom-call(s32[1]{0:T(128)} %bitcast.2._, bf16[7168,256]{1,0:T(8,128)(2,1)} %bitcast.110, bf16[7168,256]{1,0:T(8,128)(2,1)} %bitcast.113), custom_call_target="tpu_custom_call" | custom-call | flops 1 | bytes 1 | tf_op jit(solution)/shard_map/entry_half/pallas_call | solution.py:90
  19.1 2.7 %latent_attention.4.refs_0_ = bf16[16,128,512]{2,1,0:T(8,128)(2,1)} custom-call(s32[16]{0:T(128)S(1)} %copy-done.23, bf16[16,576,128]{2,1,0:T(8,128)(2,1)S(1)} %bitcast.106, bf16[16,576,512]{2,1,0:T(8,128)(2,1)S(1)} %bitcast.100), custom_call_target="tpu_custom_call" | custom-call | flops 1 | bytes 1 | tf_op jit(solution)/shard_map/latent_attention/pallas_call | solution.py:56
  21.8 4.6 %collective-permute-done.7 = bf16[32,3584]{1,0:T(8,128)(2,1)S(1)} collective-permute-done((bf16[32,3584]{1,0:T(8,128)(2,1)S(1)}, bf16[32,3584]{1,0:T(8,128)(2,1)S(1)}, u32[]{:S(2)}, u32[]{:S(2)}) %collective-permute-start.7) | collective-permute-done | bytes 229408 | tf_op jit(solution)/shard_map/ppermute | solution.py:264
  27.7 1.6 %collective-permute-start.10 = (bf16[32,3584]{1,0:T(8,128)(2,1)S(1)}, bf16[32,3584]{1,0:T(8,128)(2,1)S(1)}, u32[]{:S(2)}, u32[]{:S(2)}) collective-permute-start(bf16[32,3584]{1,0:T(8,128)(2,1)S(1)} %maximum_select_fusion), channel_id=1, source_target_pairs={{0,24},{1,25},{2,26},{3,27},{4,28},{5,29},{6,30},{7,31},{8,0},{9,1... | collective-permute-start | bytes 688136 | tf_op jit(solution)/shard_map/ppermute | solution.py:264
  29.3 2.7 %latent_attention.5.refs_0_ = bf16[16,128,512]{2,1,0:T(8,128)(2,1)} custom-call(s32[16]{0:T(128)S(1)} %copy-done.23, bf16[16,576,128]{2,1,0:T(8,128)(2,1)S(1)} %bitcast.107, bf16[16,576,512]{2,1,0:T(8,128)(2,1)S(1)} %bitcast.101, bf16[16,128,512]{2,1,0:T(8,128)(2,1)} %latent_attention.4.refs_0_), custom_call_target="tpu_custom_call", output_to_operand_aliasing={{}: (3, {})} | custom-call | flops 1 | bytes 1 | tf_op jit(solution)/shard_map/latent_attention/pallas_call | solution.py:56
  32.0 2.0 %collective-permute-done.9 = bf16[2,32,1792]{2,1,0:T(8,128)(2,1)S(1)} collective-permute-done((bf16[2,32,1792]{2,1,0:T(8,128)(2,1)S(1)}, bf16[2,32,1792]{2,1,0:T(8,128)(2,1)S(1)}, u32[]{:S(2)}, u32[]{:S(2)}) %collective-permute-start.9) | collective-permute-done | bytes 229408 | tf_op jit(solution)/shard_map/ppermute | solution.py:261
  34.7 1.6 %collective-permute-start.12 = (bf16[2,2,32,1792]{3,2,1,0:T(8,128)(2,1)S(1)}, bf16[2,2,32,1792]{3,2,1,0:T(8,128)(2,1)S(1)}, u32[]{:S(2)}, u32[]{:S(2)}) collective-permute-start(bf16[2,2,32,1792]{3,2,1,0:T(8,128)(2,1)S(1)} %pad_maximum_fusion.5), channel_id=1, source_target_pairs={{0,2},{1,3},{2,0},{3,1},{4,6},{5,7},{6,4},{7,5},{8,10},{9,11},{10,... | collective-permute-start | bytes 1376264 | tf_op jit(solution)/shard_map/ppermute | solution.py:261
  36.3 1.6 %collective-permute-start.11 = (bf16[2,2,32,1792]{3,2,1,0:T(8,128)(2,1)S(1)}, bf16[2,2,32,1792]{3,2,1,0:T(8,128)(2,1)S(1)}, u32[]{:S(2)}, u32[]{:S(2)}) collective-permute-start(bf16[2,2,32,1792]{3,2,1,0:T(8,128)(2,1)S(1)} %pad_maximum_fusion.4), channel_id=1, source_target_pairs={{0,4},{1,5},{2,6},{3,7},{4,0},{5,1},{6,2},{7,3},{8,12},{9,13},{10,... | collective-permute-start | bytes 1376264 | tf_op jit(solution)/shard_map/ppermute | solution.py:261
  39.1 2.7 %latent_attention.6.refs_0_ = bf16[16,128,512]{2,1,0:T(8,128)(2,1)} custom-call(s32[16]{0:T(128)S(1)} %copy-done.23, bf16[16,576,128]{2,1,0:T(8,128)(2,1)S(1)} %bitcast.108, bf16[16,576,512]{2,1,0:T(8,128)(2,1)S(1)} %bitcast.102, bf16[16,128,512]{2,1,0:T(8,128)(2,1)} %latent_attention.5.refs_0_), custom_call_target="tpu_custom_call", output_to_operand_aliasing={{}: (3, {})} | custom-call | flops 1 | bytes 1 | tf_op jit(solution)/shard_map/latent_attention/pallas_call | solution.py:56
  42.9 5.3 %collective-permute-done.13 = bf16[1,32,1792]{2,1,0:T(8,128)(2,1)S(1)} collective-permute-done((bf16[1,32,1792]{2,1,0:T(8,128)(2,1)S(1)}, bf16[1,32,1792]{2,1,0:T(8,128)(2,1)S(1)}, u32[]{:S(2)}, u32[]{:S(2)}) %collective-permute-start.13) | collective-permute-done | bytes 114720 | tf_op jit(solution)/shard_map/ppermute | solution.py:261
  50.0 3.0 %entry_products.5 = f32[2,384,256]{2,1,0:T(8,128)S(1)} custom-call(s32[1]{0:T(128)} %bitcast.2._, bf16[384,3584]{1,0:T(8,128)(2,1)S(1)} %pad_maximum_fusion.rows_ref, bf16[2,3584,256]{2,1,0:T(8,128)(2,1)S(1)} %collective-permute-done.17.gate_ref.up_ref, bf16[2,3584,256]{2,1,0:T(8,128)(2,1)S(1)} %collective-permute-done.17.gate_ref.up_ref), custom_call_target="tpu_custom_call" | custom-call | flops 1 | bytes 1 | tf_op jit(solution)/shard_map/entry_products/pallas_call | solution.py:155
  54.3 1.6 %collective-permute-start.15 = (bf16[2,1,32,1792]{3,2,0,1:T(8,128)(2,1)S(1)}, bf16[2,1,32,1792]{3,2,0,1:T(8,128)(2,1)S(1)}, u32[]{:S(2)}, u32[]{:S(2)}) collective-permute-start(bf16[2,1,32,1792]{3,2,0,1:T(8,128)(2,1)S(1)} %pad_maximum_fusion.12), channel_id=1, source_target_pairs={{0,4},{1,5},{2,6},{3,7},{4,0},{5,1},{6,2},{7,3},{8,12},{9,13},{10,... | collective-permute-start | bytes 688136 | tf_op jit(solution)/shard_map/ppermute | solution.py:261
  55.9 3.0 %entry_products.4.own_ref = f32[2,384,256]{2,1,0:T(8,128)S(1)} custom-call(s32[1]{0:T(128)} %bitcast.2._, bf16[384,3584]{1,0:T(8,128)(2,1)S(1)} %pad_maximum_fusion.rows_ref, bf16[7168,256]{1,0:T(8,128)(2,1)S(1)} %bitcast.111, bf16[7168,256]{1,0:T(8,128)(2,1)S(1)} %bitcast.114), custom_call_target="tpu_custom_call" | custom-call | flops 1 | bytes 1 | tf_op jit(solution)/shard_map/entry_products/pallas_call | solution.py:155
  58.8 2.3 %collective-permute-done.16 = bf16[2,1,32,1792]{3,2,0,1:T(8,128)(2,1)S(1)} collective-permute-done((bf16[2,1,32,1792]{3,2,0,1:T(8,128)(2,1)S(1)}, bf16[2,1,32,1792]{3,2,0,1:T(8,128)(2,1)S(1)}, u32[]{:S(2)}, u32[]{:S(2)}) %collective-permute-start.16) | collective-permute-done | bytes 229408 | tf_op jit(solution)/shard_map/ppermute | solution.py:261
  63.2 2.4 %exit_sums.2 = (f32[2,1,32,1792]{3,2,1,0:T(8,128)S(1)}, f32[2,1,32,1792]{3,2,1,0:T(8,128)S(1)}, bf16[2,1,32,1792]{3,2,1,0:T(8,128)(2,1)S(1)}, bf16[2,1,32,1792]{...) custom-call(bf16[384,256]{1,0:T(8,128)(2,1)S(1)} %inner_units.2.own_, ...), custom_call_target="tpu_custom_call" | custom-call | flops 1 | bytes 1 | tf_op jit(solution)/shard_map/exit_sums/pallas_call | solution.py:223
  67.1 1.6 %collective-permute-start.21 = (bf16[2,2,32,1792]{3,2,1,0:T(8,128)(2,1)}, bf16[2,2,32,1792]{3,2,1,0:T(8,128)(2,1)}, u32[]{:S(2)}, u32[]{:S(2)}) collective-permute-start(bf16[2,2,32,1792]{3,2,1,0:T(8,128)(2,1)} %get-tuple-element.128), channel_id=1, source_target_pairs={{0,4},{1,5},{2,6},{3,7},{4,0},{5,1},{6,2},{7,3},{8,12},{9,13},{10,... | collective-permute-start | bytes 1376264 | tf_op jit(solution)/shard_map/ppermute | solution.py:261
  70.3 1.9 %entry_products.7 = f32[2,128,256]{2,1,0:T(8,128)S(1)} custom-call(s32[1]{0:T(128)} %bitcast.2._, bf16[128,3584]{1,0:T(8,128)(2,1)S(1)} %bitcast.118, bf16[2,3584,256]{2,1,0:T(8,128)(2,1)S(1)} %collective-permute-done.17.gate_ref.up_ref, bf16[2,3584,256]{2,1,0:T(8,128)(2,1)S(1)} %collective-permute-done.17.gate_ref.up_ref), custom_call_target="tpu_custom_call" | custom-call | flops 1 | bytes 1 | tf_op jit(solution)/shard_map/entry_products/pallas_call | solution.py:155
  72.9 2.0 %copy-done.3 = bf16[1,7168,256]{2,1,0:T(8,128)(2,1)S(1)} copy-done((bf16[1,7168,256]{2,1,0:T(8,128)(2,1)S(1)}, bf16[1,7168,256]{2,1,0:T(8,128)(2,1)}, u32[]{:S(2)}) %copy-start.3) | copy-done | bytes 3670040
  74.9 2.0 %copy-done.5 = bf16[1,7168,256]{2,1,0:T(8,128)(2,1)S(1)} copy-done((bf16[1,7168,256]{2,1,0:T(8,128)(2,1)S(1)}, bf16[1,7168,256]{2,1,0:T(8,128)(2,1)}, u32[]{:S(2)}) %copy-start.5) | copy-done | bytes 3670040
  76.9 1.9 %entry_products.6.own_ref = f32[2,128,256]{2,1,0:T(8,128)S(1)} custom-call(s32[1]{0:T(128)} %bitcast.2._, bf16[128,3584]{1,0:T(8,128)(2,1)S(1)} %bitcast.119, bf16[7168,256]{1,0:T(8,128)(2,1)S(1)} %bitcast.112, bf16[7168,256]{1,0:T(8,128)(2,1)S(1)} %bitcast.115), custom_call_target="tpu_custom_call" | custom-call | flops 1 | bytes 1 | tf_op jit(solution)/shard_map/entry_products/pallas_call | solution.py:155
  88.9 4.2 %collective-permute-done.25 = bf16[2,32,1792]{2,1,0:T(8,128)(2,1)S(1)} collective-permute-done((bf16[2,32,1792]{2,1,0:T(8,128)(2,1)S(1)}, bf16[2,32,1792]{2,1,0:T(8,128)(2,1)S(1)}, u32[]{:S(2)}, u32[]{:S(2)}) %collective-permute-start.25) | collective-permute-done | bytes 229408 | tf_op jit(solution)/shard_map/ppermute | solution.py:261
  93.4 1.5 %collective-permute-start.29 = (bf16[2,2,32,1792]{3,2,1,0:T(8,128)(2,1)S(1)}, bf16[2,2,32,1792]{3,2,1,0:T(8,128)(2,1)S(1)}, u32[]{:S(2)}, u32[]{:S(2)}) collective-permute-start(bf16[2,2,32,1792]{3,2,1,0:T(8,128)(2,1)S(1)} %pad_maximum_fusion.6), channel_id=1, source_target_pairs={{0,4},{1,5},{2,6},{3,7},{4,0},{5,1},{6,2},{7,3},{8,12},{9,13},{10,... | collective-permute-start | bytes 1376264 | tf_op jit(solution)/shard_map/ppermute | solution.py:261
  97.6 2.7 %latent_attention.7 = bf16[16,128,512]{2,1,0:T(8,128)(2,1)} custom-call(s32[16]{0:T(128)S(1)} %copy-done.23, bf16[16,576,128]{2,1,0:T(8,128)(2,1)S(1)} %bitcast.109, bf16[16,576,512]{2,1,0:T(8,128)(2,1)S(1)} %bitcast.105, bf16[16,128,512]{2,1,0:T(8,128)(2,1)} %latent_attention.6.refs_0_), custom_call_target="tpu_custom_call", output_to_operand_aliasing={{}: (3, {})} | custom-call | flops 1 | bytes 1 | tf_op jit(solution)/shard_map/latent_attention/pallas_call | solution.py:56
  100.3 5.0 %collective-permute-done.29 = bf16[2,2,32,1792]{3,2,1,0:T(8,128)(2,1)S(1)} collective-permute-done((bf16[2,2,32,1792]{3,2,1,0:T(8,128)(2,1)S(1)}, bf16[2,2,32,1792]{3,2,1,0:T(8,128)(2,1)S(1)}, u32[]{:S(2)}, u32[]{:S(2)}) %collective-permute-start.29) | collective-permute-done | bytes 458784 | tf_op jit(solution)/shard_map/ppermute | solution.py:261
  106.5 1.5 %collective-permute-start.31 = (bf16[2,32,1792]{2,1,0:T(8,128)(2,1)S(1)}, bf16[2,32,1792]{2,1,0:T(8,128)(2,1)S(1)}, u32[]{:S(2)}, u32[]{:S(2)}) collective-permute-start(bf16[2,32,1792]{2,1,0:T(8,128)(2,1)S(1)} %fusion.10), channel_id=1, source_target_pairs={{0,2},{1,3},{2,0},{3,1},{4,6},{5,7},{6,4},{7,5},{8,10},{9,11},{10,... | collective-permute-start | bytes 688136 | tf_op jit(solution)/shard_map/ppermute | solution.py:261
  108.8 3.8 %collective-permute-done.31 = bf16[2,32,1792]{2,1,0:T(8,128)(2,1)S(1)} collective-permute-done((bf16[2,32,1792]{2,1,0:T(8,128)(2,1)S(1)}, bf16[2,32,1792]{2,1,0:T(8,128)(2,1)S(1)}, u32[]{:S(2)}, u32[]{:S(2)}) %collective-permute-start.31) | collective-permute-done | bytes 229408 | tf_op jit(solution)/shard_map/ppermute | solution.py:261
  112.7 1.6 %collective-permute-done.32 = bf16[2,32,1792]{2,1,0:T(8,128)(2,1)S(1)} collective-permute-done((bf16[2,32,1792]{2,1,0:T(8,128)(2,1)S(1)}, bf16[2,32,1792]{2,1,0:T(8,128)(2,1)S(1)}, u32[]{:S(2)}, u32[]{:S(2)}) %collective-permute-start.32) | collective-permute-done | bytes 229408 | tf_op jit(solution)/shard_map/ppermute | solution.py:261
  114.5 7.7 %collective-permute-done.33 = bf16[32,3584]{1,0:T(8,128)(2,1)S(1)} collective-permute-done((bf16[32,3584]{1,0:T(8,128)(2,1)S(1)}, bf16[32,3584]{1,0:T(8,128)(2,1)S(1)}, u32[]{:S(2)}, u32[]{:S(2)}) %collective-permute-start.33) | collective-permute-done | bytes 229408 | tf_op jit(solution)/shard_map/ppermute | solution.py:264
  (159 shorter events, 34.1 us)
Async XLA Ops:
  3.2 14.6 %collective-permute-start.2 = (bf16[1,32,1792]{2,1,0:T(8,128)(2,1)S(1)}, bf16[1,32,1792]{2,1,0:T(8,128)(2,1)S(1)}, u32[]{:S(2)}, u32[]{:S(2)}) collective-permute-start(bf16[1,32,1792]{2,1,0:T(8,128)(2,1)S(1)} %get-tuple-element.84), channel_id=1, source_target_pairs={{0,2},{1,3},{2,0},{3,1},{4,6},{5,7},{6,4},{7,5},{8,10},{9,11},{10,... | collective-permute-start | bytes 344072 | tf_op jit(solution)/shard_map/ppermute | solution.py:261
  6.1 11.7 %collective-permute-start.3 = (bf16[1,32,1792]{2,1,0:T(8,128)(2,1)S(1)}, bf16[1,32,1792]{2,1,0:T(8,128)(2,1)S(1)}, u32[]{:S(2)}, u32[]{:S(2)}) collective-permute-start(bf16[1,32,1792]{2,1,0:T(8,128)(2,1)S(1)} %get-tuple-element.86), channel_id=1, source_target_pairs={{0,4},{1,5},{2,6},{3,7},{4,0},{5,1},{6,2},{7,3},{8,12},{9,13},{10,... | collective-permute-start | bytes 344072 | tf_op jit(solution)/shard_map/ppermute | solution.py:261
  7.6 14.2 %collective-permute-start.6 = (bf16[32,3584]{1,0:T(8,128)(2,1)S(1)}, bf16[32,3584]{1,0:T(8,128)(2,1)S(1)}, u32[]{:S(2)}, u32[]{:S(2)}) collective-permute-start(bf16[32,3584]{1,0:T(8,128)(2,1)S(1)} %maximum_select_fusion), channel_id=1, source_target_pairs={{0,8},{1,9},{2,10},{3,11},{4,12},{5,13},{6,14},{7,15},{8,16},{9,17... | collective-permute-start | bytes 688136 | tf_op jit(solution)/shard_map/ppermute | solution.py:264
  9.2 17.2 %collective-permute-start.7 = (bf16[32,3584]{1,0:T(8,128)(2,1)S(1)}, bf16[32,3584]{1,0:T(8,128)(2,1)S(1)}, u32[]{:S(2)}, u32[]{:S(2)}) collective-permute-start(bf16[32,3584]{1,0:T(8,128)(2,1)S(1)} %maximum_select_fusion), channel_id=1, source_target_pairs={{0,16},{1,17},{2,18},{3,19},{4,20},{5,21},{6,22},{7,23},{8,24},{9,... | collective-permute-start | bytes 688136 | tf_op jit(solution)/shard_map/ppermute | solution.py:264
  17.8 8.6 %collective-permute-start.5 = (bf16[2,1,32,1792]{3,2,0,1:T(8,128)(2,1)S(1)}, bf16[2,1,32,1792]{3,2,0,1:T(8,128)(2,1)S(1)}, u32[]{:S(2)}, u32[]{:S(2)}) collective-permute-start(bf16[2,1,32,1792]{3,2,0,1:T(8,128)(2,1)S(1)} %get-tuple-element.180), channel_id=1, source_target_pairs={{0,2},{1,3},{2,0},{3,1},{4,6},{5,7},{6,4},{7,5},{8,10},{9,11},{10,... | collective-permute-start | bytes 688136 | tf_op jit(solution)/shard_map/ppermute | solution.py:261
  18.5 7.9 %collective-permute-start.4 = (bf16[2,1,32,1792]{3,2,0,1:T(8,128)(2,1)S(1)}, bf16[2,1,32,1792]{3,2,0,1:T(8,128)(2,1)S(1)}, u32[]{:S(2)}, u32[]{:S(2)}) collective-permute-start(bf16[2,1,32,1792]{3,2,0,1:T(8,128)(2,1)S(1)} %pad_maximum_fusion.8), channel_id=1, source_target_pairs={{0,4},{1,5},{2,6},{3,7},{4,0},{5,1},{6,2},{7,3},{8,12},{9,13},{10,... | collective-permute-start | bytes 688136 | tf_op jit(solution)/shard_map/ppermute | solution.py:261
  19.0 30.9 %collective-permute-start.17 = (bf16[2,3584,256]{2,1,0:T(8,128)(2,1)S(1)}, bf16[2,3584,256]{2,1,0:T(8,128)(2,1)S(1)}, u32[]{:S(2)}, u32[]{:S(2)}) collective-permute-start(bf16[2,3584,256]{2,1,0:T(8,128)(2,1)S(1)} %entry_half.1), channel_id=1, source_target_pairs={{0,1},{1,0},{2,3},{3,2},{4,5},{5,4},{6,7},{7,6},{8,9},{9,8},{10,11... | collective-permute-start | bytes 11010056 | tf_op jit(solution)/shard_map/ppermute | solution.py:261
  26.5 7.6 %collective-permute-start.9 = (bf16[2,32,1792]{2,1,0:T(8,128)(2,1)S(1)}, bf16[2,32,1792]{2,1,0:T(8,128)(2,1)S(1)}, u32[]{:S(2)}, u32[]{:S(2)}) collective-permute-start(bf16[2,32,1792]{2,1,0:T(8,128)(2,1)S(1)} %pad_maximum_fusion.11), channel_id=1, source_target_pairs={{0,4},{1,5},{2,6},{3,7},{4,0},{5,1},{6,2},{7,3},{8,12},{9,13},{10,... | collective-permute-start | bytes 688136 | tf_op jit(solution)/shard_map/ppermute | solution.py:261
  27.1 7.3 %collective-permute-start.8 = (bf16[2,32,1792]{2,1,0:T(8,128)(2,1)S(1)}, bf16[2,32,1792]{2,1,0:T(8,128)(2,1)S(1)}, u32[]{:S(2)}, u32[]{:S(2)}) collective-permute-start(bf16[2,32,1792]{2,1,0:T(8,128)(2,1)S(1)} %pad_maximum_fusion.10), channel_id=1, source_target_pairs={{0,2},{1,3},{2,0},{3,1},{4,6},{5,7},{6,4},{7,5},{8,10},{9,11},{10,... | collective-permute-start | bytes 688136 | tf_op jit(solution)/shard_map/ppermute | solution.py:261
  27.7 7.0 %collective-permute-start.10 = (bf16[32,3584]{1,0:T(8,128)(2,1)S(1)}, bf16[32,3584]{1,0:T(8,128)(2,1)S(1)}, u32[]{:S(2)}, u32[]{:S(2)}) collective-permute-start(bf16[32,3584]{1,0:T(8,128)(2,1)S(1)} %maximum_select_fusion), channel_id=1, source_target_pairs={{0,24},{1,25},{2,26},{3,27},{4,28},{5,29},{6,30},{7,31},{8,0},{9,1... | collective-permute-start | bytes 688136 | tf_op jit(solution)/shard_map/ppermute | solution.py:264
  34.7 14.8 %collective-permute-start.12 = (bf16[2,2,32,1792]{3,2,1,0:T(8,128)(2,1)S(1)}, bf16[2,2,32,1792]{3,2,1,0:T(8,128)(2,1)S(1)}, u32[]{:S(2)}, u32[]{:S(2)}) collective-permute-start(bf16[2,2,32,1792]{3,2,1,0:T(8,128)(2,1)S(1)} %pad_maximum_fusion.5), channel_id=1, source_target_pairs={{0,2},{1,3},{2,0},{3,1},{4,6},{5,7},{6,4},{7,5},{8,10},{9,11},{10,... | collective-permute-start | bytes 1376264 | tf_op jit(solution)/shard_map/ppermute | solution.py:261
  36.3 13.2 %collective-permute-start.11 = (bf16[2,2,32,1792]{3,2,1,0:T(8,128)(2,1)S(1)}, bf16[2,2,32,1792]{3,2,1,0:T(8,128)(2,1)S(1)}, u32[]{:S(2)}, u32[]{:S(2)}) collective-permute-start(bf16[2,2,32,1792]{3,2,1,0:T(8,128)(2,1)S(1)} %pad_maximum_fusion.4), channel_id=1, source_target_pairs={{0,4},{1,5},{2,6},{3,7},{4,0},{5,1},{6,2},{7,3},{8,12},{9,13},{10,... | collective-permute-start | bytes 1376264 | tf_op jit(solution)/shard_map/ppermute | solution.py:261
  37.9 10.3 %collective-permute-start.13 = (bf16[1,32,1792]{2,1,0:T(8,128)(2,1)S(1)}, bf16[1,32,1792]{2,1,0:T(8,128)(2,1)S(1)}, u32[]{:S(2)}, u32[]{:S(2)}) collective-permute-start(bf16[1,32,1792]{2,1,0:T(8,128)(2,1)S(1)} %get-tuple-element.105), channel_id=1, source_target_pairs={{0,2},{1,3},{2,0},{3,1},{4,6},{5,7},{6,4},{7,5},{8,10},{9,11},{10,... | collective-permute-start | bytes 344072 | tf_op jit(solution)/shard_map/ppermute | solution.py:261
  38.5 11.0 %collective-permute-start.14 = (bf16[1,32,1792]{2,1,0:T(8,128)(2,1)S(1)}, bf16[1,32,1792]{2,1,0:T(8,128)(2,1)S(1)}, u32[]{:S(2)}, u32[]{:S(2)}) collective-permute-start(bf16[1,32,1792]{2,1,0:T(8,128)(2,1)S(1)} %get-tuple-element.107), channel_id=1, source_target_pairs={{0,4},{1,5},{2,6},{3,7},{4,0},{5,1},{6,2},{7,3},{8,12},{9,13},{10,... | collective-permute-start | bytes 344072 | tf_op jit(solution)/shard_map/ppermute | solution.py:261
  49.5 12.3 %collective-permute-start.20 = (bf16[256,3584]{1,0:T(8,128)(2,1)S(1)}, bf16[256,3584]{1,0:T(8,128)(2,1)S(1)}, u32[]{:S(2)}, u32[]{:S(2)}) collective-permute-start(bf16[256,3584]{1,0:T(8,128)(2,1)S(1)} %get-tuple-element.119), channel_id=1, source_target_pairs={{0,1},{1,0},{2,3},{3,2},{4,5},{5,4},{6,7},{7,6},{8,9},{9,8},{10,11... | collective-permute-start | bytes 5505032 | tf_op jit(solution)/shard_map/ppermute | solution.py:261
  53.0 8.6 %collective-permute-start.18 = (f32[2,384,256]{2,1,0:T(8,128)S(1)}, f32[2,384,256]{2,1,0:T(8,128)S(1)}, u32[]{:S(2)}, u32[]{:S(2)}) collective-permute-start(f32[2,384,256]{2,1,0:T(8,128)S(1)} %entry_products.5), channel_id=1, source_target_pairs={{0,1},{1,0},{2,3},{3,2},{4,5},{5,4},{6,7},{7,6},{8,9},{9,8},{10,11... | collective-permute-start | bytes 2359304 | tf_op jit(solution)/shard_map/ppermute | solution.py:261
  53.6 7.6 %collective-permute-start.16 = (bf16[2,1,32,1792]{3,2,0,1:T(8,128)(2,1)S(1)}, bf16[2,1,32,1792]{3,2,0,1:T(8,128)(2,1)S(1)}, u32[]{:S(2)}, u32[]{:S(2)}) collective-permute-start(bf16[2,1,32,1792]{3,2,0,1:T(8,128)(2,1)S(1)} %get-tuple-element.172), channel_id=1, source_target_pairs={{0,2},{1,3},{2,0},{3,1},{4,6},{5,7},{6,4},{7,5},{8,10},{9,11},{10,... | collective-permute-start | bytes 688136 | tf_op jit(solution)/shard_map/ppermute | solution.py:261
  54.3 7.3 %collective-permute-start.15 = (bf16[2,1,32,1792]{3,2,0,1:T(8,128)(2,1)S(1)}, bf16[2,1,32,1792]{3,2,0,1:T(8,128)(2,1)S(1)}, u32[]{:S(2)}, u32[]{:S(2)}) collective-permute-start(bf16[2,1,32,1792]{3,2,0,1:T(8,128)(2,1)S(1)} %pad_maximum_fusion.12), channel_id=1, source_target_pairs={{0,4},{1,5},{2,6},{3,7},{4,0},{5,1},{6,2},{7,3},{8,12},{9,13},{10,... | collective-permute-start | bytes 688136 | tf_op jit(solution)/shard_map/ppermute | solution.py:261
  67.1 12.9 %collective-permute-start.21 = (bf16[2,2,32,1792]{3,2,1,0:T(8,128)(2,1)}, bf16[2,2,32,1792]{3,2,1,0:T(8,128)(2,1)}, u32[]{:S(2)}, u32[]{:S(2)}) collective-permute-start(bf16[2,2,32,1792]{3,2,1,0:T(8,128)(2,1)} %get-tuple-element.128), channel_id=1, source_target_pairs={{0,4},{1,5},{2,6},{3,7},{4,0},{5,1},{6,2},{7,3},{8,12},{9,13},{10,... | collective-permute-start | bytes 1376264 | tf_op jit(solution)/shard_map/ppermute | solution.py:261
  68.7 12.6 %collective-permute-start.22 = (bf16[2,2,32,1792]{3,2,1,0:T(8,128)(2,1)}, bf16[2,2,32,1792]{3,2,1,0:T(8,128)(2,1)}, u32[]{:S(2)}, u32[]{:S(2)}) collective-permute-start(bf16[2,2,32,1792]{3,2,1,0:T(8,128)(2,1)} %get-tuple-element.129), channel_id=1, source_target_pairs={{0,2},{1,3},{2,0},{3,1},{4,6},{5,7},{6,4},{7,5},{8,10},{9,11},{10,... | collective-permute-start | bytes 1376264 | tf_op jit(solution)/shard_map/ppermute | solution.py:261
  72.2 6.6 %collective-permute-start.23 = (f32[2,128,256]{2,1,0:T(8,128)S(1)}, f32[2,128,256]{2,1,0:T(8,128)}, u32[]{:S(2)}, u32[]{:S(2)}) collective-permute-start(f32[2,128,256]{2,1,0:T(8,128)S(1)} %entry_products.7), channel_id=1, source_target_pairs={{0,1},{1,0},{2,3},{3,2},{4,5},{5,4},{6,7},{7,6},{8,9},{9,8},{10,11... | collective-permute-start | bytes 786440 | tf_op jit(solution)/shard_map/ppermute | solution.py:261
  72.3 42.1 %collective-permute-start = (f32[16,4]{0,1:T(4,128)S(1)}, f32[16,4]{0,1:T(4,128)S(1)}, u32[]{:S(2)}, u32[]{:S(2)}) collective-permute-start(f32[16,4]{0,1:T(4,128)S(1)} %select_reduce_fusion), channel_id=1, source_target_pairs={{0,1},{1,0},{2,3},{3,2},{4,5},{5,4},{6,7},{7,6},{8,9},{9,8},{10,11... | collective-permute-start | bytes 776 | tf_op jit(solution)/shard_map/ppermute | solution.py:261
  83.8 3.3 %collective-permute-start.26 = (bf16[128,256]{1,0:T(8,128)(2,1)S(1)}, bf16[128,256]{1,0:T(8,128)(2,1)S(1)}, u32[]{:S(2)}, u32[]{:S(2)}) collective-permute-start(bf16[128,256]{1,0:T(8,128)(2,1)S(1)} %inner_units.3.own_ref), channel_id=1, source_target_pairs={{0,1},{1,0},{2,3},{3,2},{4,5},{5,4},{6,7},{7,6},{8,9},{9,8},{10,11... | collective-permute-start | bytes 196616 | tf_op jit(solution)/shard_map/ppermute | solution.py:261
  85.1 8.1 %collective-permute-start.25 = (bf16[2,32,1792]{2,1,0:T(8,128)(2,1)S(1)}, bf16[2,32,1792]{2,1,0:T(8,128)(2,1)S(1)}, u32[]{:S(2)}, u32[]{:S(2)}) collective-permute-start(bf16[2,32,1792]{2,1,0:T(8,128)(2,1)S(1)} %fusion.9), channel_id=1, source_target_pairs={{0,4},{1,5},{2,6},{3,7},{4,0},{5,1},{6,2},{7,3},{8,12},{9,13},{10,... | collective-permute-start | bytes 688136 | tf_op jit(solution)/shard_map/ppermute | solution.py:261
  85.7 7.7 %collective-permute-start.24 = (bf16[2,32,1792]{2,1,0:T(8,128)(2,1)S(1)}, bf16[2,32,1792]{2,1,0:T(8,128)(2,1)S(1)}, u32[]{:S(2)}, u32[]{:S(2)}) collective-permute-start(bf16[2,32,1792]{2,1,0:T(8,128)(2,1)S(1)} %fusion.8), channel_id=1, source_target_pairs={{0,2},{1,3},{2,0},{3,1},{4,6},{5,7},{6,4},{7,5},{8,10},{9,11},{10,... | collective-permute-start | bytes 688136 | tf_op jit(solution)/shard_map/ppermute | solution.py:261
  93.4 11.9 %collective-permute-start.29 = (bf16[2,2,32,1792]{3,2,1,0:T(8,128)(2,1)S(1)}, bf16[2,2,32,1792]{3,2,1,0:T(8,128)(2,1)S(1)}, u32[]{:S(2)}, u32[]{:S(2)}) collective-permute-start(bf16[2,2,32,1792]{3,2,1,0:T(8,128)(2,1)S(1)} %pad_maximum_fusion.6), channel_id=1, source_target_pairs={{0,4},{1,5},{2,6},{3,7},{4,0},{5,1},{6,2},{7,3},{8,12},{9,13},{10,... | collective-permute-start | bytes 1376264 | tf_op jit(solution)/shard_map/ppermute | solution.py:261
  94.9 11.5 %collective-permute-start.30 = (bf16[2,2,32,1792]{3,2,1,0:T(8,128)(2,1)S(1)}, bf16[2,2,32,1792]{3,2,1,0:T(8,128)(2,1)S(1)}, u32[]{:S(2)}, u32[]{:S(2)}) collective-permute-start(bf16[2,2,32,1792]{3,2,1,0:T(8,128)(2,1)S(1)} %pad_maximum_fusion.7), channel_id=1, source_target_pairs={{0,2},{1,3},{2,0},{3,1},{4,6},{5,7},{6,4},{7,5},{8,10},{9,11},{10,... | collective-permute-start | bytes 1376264 | tf_op jit(solution)/shard_map/ppermute | solution.py:261
  96.5 18.0 %collective-permute-start.27 = (bf16[32,3584]{1,0:T(8,128)(2,1)S(1)}, bf16[32,3584]{1,0:T(8,128)(2,1)S(1)}, u32[]{:S(2)}, u32[]{:S(2)}) collective-permute-start(bf16[32,3584]{1,0:T(8,128)(2,1)S(1)} %get-tuple-element.168), channel_id=1, source_target_pairs={{0,24},{1,25},{2,26},{3,27},{4,28},{5,29},{6,30},{7,31},{8,0},{9,1... | collective-permute-start | bytes 688136 | tf_op jit(solution)/shard_map/ppermute | solution.py:264
  97.5 17.0 %collective-permute-start.28 = (bf16[32,3584]{1,0:T(8,128)(2,1)S(1)}, bf16[32,3584]{1,0:T(8,128)(2,1)S(1)}, u32[]{:S(2)}, u32[]{:S(2)}) collective-permute-start(bf16[32,3584]{1,0:T(8,128)(2,1)S(1)} %get-tuple-element.169), channel_id=1, source_target_pairs={{0,16},{1,17},{2,18},{3,19},{4,20},{5,21},{6,22},{7,23},{8,24},{9,... | collective-permute-start | bytes 688136 | tf_op jit(solution)/shard_map/ppermute | solution.py:264
  106.5 6.1 %collective-permute-start.31 = (bf16[2,32,1792]{2,1,0:T(8,128)(2,1)S(1)}, bf16[2,32,1792]{2,1,0:T(8,128)(2,1)S(1)}, u32[]{:S(2)}, u32[]{:S(2)}) collective-permute-start(bf16[2,32,1792]{2,1,0:T(8,128)(2,1)S(1)} %fusion.10), channel_id=1, source_target_pairs={{0,2},{1,3},{2,0},{3,1},{4,6},{5,7},{6,4},{7,5},{8,10},{9,11},{10,... | collective-permute-start | bytes 688136 | tf_op jit(solution)/shard_map/ppermute | solution.py:261
  108.2 6.1 %collective-permute-start.32 = (bf16[2,32,1792]{2,1,0:T(8,128)(2,1)S(1)}, bf16[2,32,1792]{2,1,0:T(8,128)(2,1)S(1)}, u32[]{:S(2)}, u32[]{:S(2)}) collective-permute-start(bf16[2,32,1792]{2,1,0:T(8,128)(2,1)S(1)} %fusion.11), channel_id=1, source_target_pairs={{0,4},{1,5},{2,6},{3,7},{4,0},{5,1},{6,2},{7,3},{8,12},{9,13},{10,... | collective-permute-start | bytes 688136 | tf_op jit(solution)/shard_map/ppermute | solution.py:261
  114.3 7.9 %collective-permute-start.33 = (bf16[32,3584]{1,0:T(8,128)(2,1)S(1)}, bf16[32,3584]{1,0:T(8,128)(2,1)S(1)}, u32[]{:S(2)}, u32[]{:S(2)}) collective-permute-start(bf16[32,3584]{1,0:T(8,128)(2,1)S(1)} %fusion.12), channel_id=1, source_target_pairs={{0,8},{1,9},{2,10},{3,11},{4,12},{5,13},{6,14},{7,15},{8,16},{9,17... | collective-permute-start | bytes 688136 | tf_op jit(solution)/shard_map/ppermute | solution.py:264
  (32 other events, 184.6 us)

commit v3 on v2

--- a/solution.py
+++ b/solution.py
@@ -84,8 +84,8 @@
 
 def entry_half(core, gate, up):
     width, units = gate.shape
-    tile = tile_of(width // 2)
-    steps = width // 2 // tile
+    steps = 2
+    tile = width // 2 // steps
     spec = pl.BlockSpec((tile, units), lambda i, core: ((1 - core[0]) * steps + i, 0))
     return pl.pallas_call(
         entry_half_kernel,
@@ -96,10 +96,26 @@
             out_specs=pl.BlockSpec((2, tile, units), lambda i, core: (0, i, 0)),
         ),
         out_shape=jax.ShapeDtypeStruct((2, width // 2, units), gate.dtype),
-        compiler_params=pltpu.CompilerParams(vmem_limit_bytes=48 * 1024 * 1024),
+        compiler_params=pltpu.CompilerParams(vmem_limit_bytes=16 * 1024 * 1024),
         cost_estimate=SMALL,
         name="entry_half",
     )(core.reshape(1), gate, up)
+
+
+def hold_kernel(in_ref, out_ref):
+    out_ref[0] = in_ref[0]
+
+
+def hold(value):
+    return pl.pallas_call(
+        hold_kernel,
+        in_specs=[pl.BlockSpec(memory_space=pltpu.SMEM)],
+        out_specs=pl.BlockSpec(memory_space=pltpu.SMEM),
+        out_shape=jax.ShapeDtypeStruct((1,), value.dtype),
+        compiler_params=pltpu.CompilerParams(vmem_limit_bytes=1024 * 1024),
+        cost_estimate=SMALL,
+        name="hold",
+    )(value.reshape(1))[0]
 
 
 def exit_half_kernel(_, given_ref, kept_ref, given_out_ref, kept_out_ref):
@@ -130,41 +146,30 @@
     )(core.reshape(1), down, down)
 
 
-def entry_kernel(_, rows_ref, gate_ref, up_ref, out_ref):
-    @pl.when(pl.program_id(0) == 0)
-    def _():
-        out_ref[...] = jnp.zeros_like(out_ref)
-
+def entry_kernel(core_ref, rows_ref, *refs):
+    weight_refs, out_ref = refs[:-1], refs[-1]
+    half = rows_ref.shape[1]
     rows = rows_ref[...]
-    out_ref[0] += jnp.dot(rows, gate_ref[...], preferred_element_type=jnp.float32)
-    out_ref[1] += jnp.dot(rows, up_ref[...], preferred_element_type=jnp.float32)
-
-
-def entry(rows, core, gate, up):
-    count, half = rows.shape
-    units = gate.shape[-1]
-    steps = next(n for n in (7, 4, 2, 1) if half % (n * 128) == 0)
-    tile = half // steps
-    if gate.ndim == 3:
-        specs = [
-            pl.BlockSpec((None, tile, units), lambda i, core: (0, i, 0)),
-            pl.BlockSpec((None, tile, units), lambda i, core: (1, i, 0)),
-        ]
-    else:
-        specs = [pl.BlockSpec((tile, units), lambda i, core: (core[0] * steps + i, 0))] * 2
+    for which in range(2):
+        if len(weight_refs) == 1:
+            weight = weight_refs[0][which]
+        else:
+            begin = pl.multiple_of(core_ref[0] * half, half)
+            weight = weight_refs[which][pl.ds(begin, half)]
+        out_ref[which] = jnp.dot(rows, weight, preferred_element_type=jnp.float32)
+
+
+def entry(rows, core, *weights):
     return pl.pallas_call(
         entry_kernel,
-        grid_spec=pltpu.PrefetchScalarGridSpec(
-            num_scalar_prefetch=1,
-            grid=(steps,),
-            in_specs=[pl.BlockSpec((count, tile), lambda i, core: (0, i))] + specs,
-            out_specs=pl.BlockSpec((2, count, units), lambda i, core: (0, 0, 0)),
-        ),
-        out_shape=jax.ShapeDtypeStruct((2, count, units), jnp.float32),
+        in_specs=[pl.BlockSpec(memory_space=pltpu.SMEM)]
+        + [pl.BlockSpec(memory_space=pltpu.VMEM)] * (1 + len(weights)),
+        out_specs=pl.BlockSpec(memory_space=pltpu.VMEM),
+        out_shape=jax.ShapeDtypeStruct((2, rows.shape[0], weights[0].shape[-1]), jnp.float32),
         compiler_params=pltpu.CompilerParams(vmem_limit_bytes=16 * 1024 * 1024),
         cost_estimate=SMALL,
         name="entry_products",
-    )(core.reshape(1), rows, gate, up)
+    )(core.reshape(1), rows, *weights)
 
 
 def inner_kernel(own_ref, other_ref, out_ref):
@@ -174,64 +179,65 @@
     out_ref[...] = (silu * up_value).astype(out_ref.dtype)
 
 
-def inner_units(own, other):
+def inner_units(own, other, vmem=12):
     return pl.pallas_call(
         inner_kernel,
         in_specs=[pl.BlockSpec(memory_space=pltpu.VMEM)] * 2,
         out_specs=pl.BlockSpec(memory_space=pltpu.VMEM),
         out_shape=jax.ShapeDtypeStruct(own.shape[1:], jnp.bfloat16),
-        compiler_params=pltpu.CompilerParams(vmem_limit_bytes=12 * 1024 * 1024),
+        compiler_params=pltpu.CompilerParams(vmem_limit_bytes=vmem * 1024 * 1024),
         cost_estimate=SMALL,
         name="inner_units",
     )(own, other)
 
 
-def exit_kernel(own_ref, other_ref, down_own_ref, down_other_ref, *out_refs, rows):
-    own, other = own_ref[...], other_ref[...]
+def exit_kernel(own_ref, other_ref, down_own_ref, down_other_ref, *out_refs, sets, rows, sent):
     quarter = down_own_ref.shape[1] // 2
     tile = math.gcd(quarter, 256)
-    for at in range(2 * quarter // tile):
-        columns = slice(at * tile, (at + 1) * tile)
-        part = jnp.dot(own, down_own_ref[:, columns], preferred_element_type=jnp.float32)
-        part += jnp.dot(other, down_other_ref[:, columns], preferred_element_type=jnp.float32)
-        second = at * tile >= quarter
-        begin = at * tile - (quarter if second else 0)
-        columns = slice(begin, begin + tile)
-        row = 0
-        for first in range(0, len(out_refs), 4):
-            kept_a, kept_b, sent_a, sent_b = out_refs[first : first + 4]
-            for slot in range(kept_a.shape[1]):
-                for y in range(2):
-                    for x in range(2):
+
+    def picked(ref, second):
+        strips = []
+        for begin, slots in sets:
+            for slot in range(slots):
+                for other in range(2):
+                    y, x = (other, sent) if second else (sent, other)
+                    at = ((begin + slot) * 4 + y * 2 + x) * rows
+                    strips.append(ref[at : at + rows])
+        return jnp.concatenate(strips, 0)
+
+    for second in range(2):
+        own, other = picked(own_ref, second), picked(other_ref, second)
+        for at in range(quarter // tile):
+            source = slice(second * quarter + at * tile, second * quarter + (at + 1) * tile)
+            columns = slice(at * tile, (at + 1) * tile)
+            part = jnp.dot(own, down_own_ref[:, source], preferred_element_type=jnp.float32)
+            part += jnp.dot(other, down_other_ref[:, source], preferred_element_type=jnp.float32)
+            row = 0
+            for number, (_, slots) in enumerate(sets):
+                target = out_refs[2 * number + second]
+                for slot in range(slots):
+                    for which in range(2):
                         value = part[row : row + rows]
+                        target[which, slot, :, columns] = value.astype(target.dtype)
                         row += rows
-                        if second:
-                            target = sent_b if x else kept_b
-                            target[y, slot, :, columns] = value.astype(target.dtype)
-                        else:
-                            target = sent_a if y else kept_a
-                            target[x, slot, :, columns] = value.astype(target.dtype)
-
-
-def exit_sums(own, other, down_own, down_other, rows, sets):
-    quarter = down_own.shape[1] // 2
+
+
+def exit_sums(inner, down, rows, sets, sent):
+    quarter = down[0].shape[1] // 2
+    dtype = jnp.bfloat16 if sent else jnp.float32
     shapes = []
-    for slots in sets:
-        shape = (2, slots, rows, quarter)
-        shapes += [jax.ShapeDtypeStruct(shape, jnp.float32)] * 2
-        shapes += [jax.ShapeDtypeStruct(shape, jnp.bfloat16)] * 2
+    for _, slots in sets:
+        shapes += [jax.ShapeDtypeStruct((2, slots, rows, quarter), dtype)] * 2
     outs = pl.pallas_call(
-        functools.partial(exit_kernel, rows=rows),
+        functools.partial(exit_kernel, sets=sets, rows=rows, sent=int(sent)),
         in_specs=[pl.BlockSpec(memory_space=pltpu.VMEM)] * 4,
         out_specs=[pl.BlockSpec(memory_space=pltpu.VMEM)] * len(shapes),
         out_shape=shapes,
         compiler_params=pltpu.CompilerParams(vmem_limit_bytes=16 * 1024 * 1024),
         cost_estimate=SMALL,
         name="exit_sums",
-    )(own, other, down_own, down_other)
-    return [
-        (tuple(outs[at : at + 2]), tuple(outs[at + 2 : at + 4])) for at in range(0, len(outs), 4)
-    ]
+    )(*inner, *down)
+    return [tuple(outs[at : at + 2]) for at in range(0, len(outs), 2)]
 
 
 def after(value, *others):
@@ -336,76 +342,87 @@
             for at, k in enumerate(slots)
         ]
 
-    near, far = list(range(1, planes - 1)), [planes - 1]
+    early = [planes // 2]
+    late = [k for k in range(1, planes) if k not in early]
+    first_set, late_set = (0, 1 + len(early)), (0, len(late))
     join = lax.optimization_barrier
 
-    slot_near = [shift(block, k) for k in near]
+    def send_first(sent):
+        return in_y(sent[0]), in_x(sent[1])
+
+    def send_second(sent):
+        return in_x(sent[0]), in_y(sent[1])
+
+    slot_early = [shift(block, k) for k in early]
     held, got = spread_first([block])
     core, _ = join((core, block))
+    core = hold(core)
+    held, got, block, core = join((held, got, block, core))
+
+    own, own_got = spread_second(held, got)
     entry_give = entry_half(core, gate_part, up_part)
-    held, got, entry_give = join((held, got, entry_give))
-
+    own, own_got, slot_early, block, entry_give = join(
+        (own, own_got, slot_early, block, entry_give)
+    )
     entry_other = in_core(entry_give)
-    own, own_got = spread_second(held, got)
-    attended = attend_more(0, None, entry_give)
-    own, own_got, slot_near, attended, block = join((own, own_got, slot_near, attended, block))
-
-    slot_far = [shift(block, k) for k in far]
-    held, got = spread_first(slot_near)
-    attended = attend_more(1, attended, block)
-    held, got, slot_far, attended = join((held, got, slot_far, attended))
-
-    near_held, near_got = spread_second(held, got)
-    held, got = spread_first(slot_far)
-    attended = attend_more(2, attended, *slot_far)
-    down_give, down_own = exit_half(after(core, *slot_far), down_part)
-    near_held, near_got, held, got, attended, down_give, down_own = join(
-        (near_held, near_got, held, got, attended, down_give, down_own)
-    )
-    down_other = in_core(down_give)
-
-    far_held, far_got = spread_second(held, got)
+
+    slot_late = [shift(block, k) for k in late]
+    held, got = spread_first(slot_early)
+    held, got = join((held, got))
+
+    early_held, early_got = spread_second(held, got)
+    down_give, down_own = exit_half(after(core, *held), down_part)
+    early_held, early_got, slot_late, down_give, down_own = join(
+        (early_held, early_got, slot_late, down_give, down_own)
+    )
+
+    down = (down_own, in_core(down_give))
+    held, got = spread_first(slot_late)
     arrived = jnp.concatenate(
-        [spread_rows(own, own_got), spread_rows(near_held, near_got)], 0
-    )
-    pre_other = in_core(entry(arrived, core, entry_other, entry_other))
+        [spread_rows(own, own_got), spread_rows(early_held, early_got)], 0
+    )
+    pre_other = entry(arrived, core, entry_other)
+    held, got, pre_other, arrived = join((held, got, pre_other, arrived))
+
+    late_held, late_got = spread_second(held, got)
     pre_own = entry(arrived, core, gate_part, up_part)
-    far_held, far_got, pre_own = join((far_held, far_got, pre_own))
-
-    inner = inner_units(pre_own, pre_other)
-    inner_other = in_core(inner)
-    (own_kept, own_sent), (near_kept, near_sent) = exit_sums(
-        inner, inner_other, down_own, down_other, 2 * rows, [1, len(near)]
-    )
-    near_sent, far_held, far_got = join((near_sent, far_held, far_got))
-
-    near_got = (in_y(near_sent[0]), in_x(near_sent[1]))
-    arrived = spread_rows(far_held, far_got)
-    pre_other = in_core(entry(arrived, core, entry_other, entry_other))
+    inner = inner_units(pre_own, in_core(pre_other))
+    inner = (inner, in_core(inner))
+    (sent,) = exit_sums(inner, down, 2 * rows, [first_set], True)
+    late_held, late_got, sent, inner = join((late_held, late_got, sent, inner))
+
+    got = send_first(sent)
+    arrived = spread_rows(late_held, late_got)
+    pre_other = entry(arrived, core, entry_other)
     pre_own = entry(arrived, core, gate_part, up_part)
-    near_kept, near_got, pre_own, pre_other, attended = join(
-        (near_kept, near_got, pre_own, pre_other, attended)
-    )
-
-    near_kept, near_sent = gather_second(near_kept, near_got)
-    near_got = (in_x(near_sent[0]), in_y(near_sent[1]))
-    inner = inner_units(pre_own, pre_other)
-    inner_other = in_core(inner)
-    [(far_kept, far_sent)] = exit_sums(
-        inner, inner_other, down_own, down_other, 2 * rows, [len(far)]
-    )
-    rest_sent = tuple(jnp.concatenate(pair, 1) for pair in zip(far_sent, own_sent))
-    rest_kept = tuple(jnp.concatenate(pair, 1) for pair in zip(far_kept, own_kept))
-    near_kept, near_got, rest_kept, rest_sent = join((near_kept, near_got, rest_kept, rest_sent))
-
-    terms = returned(gather_rows(near_kept, near_got), near)
-    rest_got = (in_y(rest_sent[0]), in_x(rest_sent[1]))
-    attended = attend_more(3, attended, *rest_sent)
-    rest_kept, rest_got, attended = join((rest_kept, rest_got, attended))
-
-    rest_kept, rest_sent = gather_second(rest_kept, rest_got)
-    rest_got = (in_x(rest_sent[0]), in_y(rest_sent[1]))
-    terms += returned(gather_rows(rest_kept, rest_got), far + [0])
+    (kept,) = exit_sums(inner, down, 2 * rows, [first_set], False)
+    kept, got, pre_own, pre_other = join((kept, got, pre_own, pre_other))
+
+    kept, sent = gather_second(kept, got)
+    got = send_second(sent)
+    inner = inner_units(pre_own, in_core(pre_other))
+    inner = (inner, in_core(inner))
+    (late_sent,) = exit_sums(inner, down, 2 * rows, [late_set], True)
+    kept, got, inner, late_sent = join((kept, got, inner, late_sent))
+
+    sums = gather_rows(kept, got)
+    terms = returned(sums, [0] + early)
+    late_got = send_first(late_sent)
+    (late_kept,) = exit_sums(inner, down, 2 * rows, [late_set], False)
+    attended = attend_more(0, None, *late_sent)
+    late_kept, late_got, attended = join((late_kept, late_got, attended))
+
+    late_kept, late_sent = gather_second(late_kept, late_got)
+    late_got = send_second(late_sent)
+    attended = attend_more(1, attended, *late_sent)
+    late_kept, late_got, attended = join((late_kept, late_got, attended))
+
+    terms += returned(gather_rows(late_kept, late_got), late)
+    attended = attend_more(2, attended, *late_got)
+    attended = attend_more(3, attended, attended)
+    slots = [k for k, _ in terms]
+    terms, attended = join(([term for _, term in terms], attended))
+    terms = list(zip(slots, terms))
     total = 0.0
     for k, term in terms:
         total = total + mixing_of((plane + k) % planes) * widen(term)

time: 125 us -> 116 us (0.928)
  waiting for transfers between devices: 46.4 us -> 27 us
  local copies, waits for them, and re-layouts: 7.01 us -> 15 us
  starting transfers between devices: 32.2 us -> 33.9 us
    ppermute x29, waiting for transfers between devices: 33.9 us -> 21.8 us  [swap(): return lax.ppermute(value, AXIS, [(i, i ^ bit) for i in range(devices)])]
    unnamed x58 -> x36, local copies, waits for them, and re-layouts: 6.5 us -> 14.4 us
    ppermute x6, waiting for transfers between devices: 12.5 us -> 5.23 us  [shift(): lax.ppermute(value, AXIS, [(i, (i + SLICES * by) % devices) for i in rang...]
    pallas_call x1, Pallas kernels: 6 us -> 1.16 us  [entry_half(): pl.pallas_call(entry_half_kernel, grid_spec=pltpu.PrefetchScalarGridSpec(...]
    ppermute x6, starting transfers between devices: 6.91 us -> 11.6 us  [shift(): lax.ppermute(value, AXIS, [(i, (i + SLICES * by) % devices) for i in rang...]
    pallas_call x6 -> x9, Pallas kernels: 12.7 us -> 16.5 us  [the longest x4 8.73 us: exit_sums(): pl.pallas_call(functools.partial(exit_kernel, sets=sets, rows=rows, sent=...]
    ppermute x29, starting transfers between devices: 25.3 us -> 22.3 us  [swap(): return lax.ppermute(value, AXIS, [(i, i ^ bit) for i in range(devices)])]
    pallas_call x1, Pallas kernels: 1 us -> 3.78 us  [exit_half(): pl.pallas_call(exit_half_kernel, grid_spec=pltpu.PrefetchScalarGridSpec(n...]
  transfers between devices with their start and end apart: 35 -> 35, of which waited for: 20 -> 22; matrix products, arithmetic and copies ran while one was open for 3% -> 4% of each run, Pallas kernels for 24% -> 28%
where the time goes in v3:
time: 116 us
  starting transfers between devices  33.9 us (29%)
  Pallas kernels  32.7 us (28%)
  waiting for transfers between devices  27 us (23%)
  local copies, waits for them, and re-layouts  15 us (13%)
  other arithmetic  5.66 us (5%)
  between operations  1.24 us (1%)
    ppermute x29, starting transfers between devices, swap(): return lax.ppermute(value, AXIS, [(i, i ^ bit) for i in range(devices)])  22.3 us
    ppermute x29, waiting for transfers between devices, swap(): return lax.ppermute(value, AXIS, [(i, i ^ bit) for i in range(devices)])  21.8 us
    unnamed x36, local copies, waits for them, and re-layouts  14.4 us
    ppermute x6, starting transfers between devices, shift(): lax.ppermute(value, AXIS, [(i, (i + SLICES * by) % devices) for i in rang...  11.6 us
    pallas_call x4, Pallas kernels, attend(): pl.pallas_call(functools.partial(attend_kernel, first=first), grid_spec=p...  11 us
    pallas_call x4, Pallas kernels, exit_sums(): pl.pallas_call(functools.partial(exit_kernel, sets=sets, rows=rows, sent=...  8.73 us
    pallas_call x4, Pallas kernels, entry(): pl.pallas_call(entry_kernel, in_specs=[pl.BlockSpec(memory_space=pltpu.SM...  7.24 us
    ppermute x6, waiting for transfers between devices, shift(): lax.ppermute(value, AXIS, [(i, (i + SLICES * by) % devices) for i in rang...  5.23 us
  transfers between devices with their start and end apart: 35, of which 22 were waited for; matrix products, arithmetic and copies ran while one was open for 4% of the time, Pallas kernels for 28%

profile of v3, /device:TPU:0, one launch (start us, length us, event | category | flops | bytes accessed | tf_op | source)
XLA Modules:
  0.0 115.5 jit_solution(6039644136117697198)
XLA Ops:
  3.2 2.9 %collective-permute-start.2 = (bf16[1,32,1792]{2,1,0:T(8,128)(2,1)S(1)}, bf16[1,32,1792]{2,1,0:T(8,128)(2,1)S(1)}, u32[]{:S(2)}, u32[]{:S(2)}) collective-permute-start(bf16[1,32,1792]{2,1,0:T(8,128)(2,1)S(1)} %get-tuple-element.87), channel_id=1, source_target_pairs={{0,2},{1,3},{2,0},{3,1},{4,6},{5,7},{6,4},{7,5},{8,10},{9,11},{10,... | collective-permute-start | bytes 344072 | tf_op jit(solution)/shard_map/ppermute | solution.py:267
  7.6 2.6 %collective-permute-start.6 = (bf16[32,3584]{1,0:T(8,128)(2,1)S(1)}, bf16[32,3584]{1,0:T(8,128)(2,1)S(1)}, u32[]{:S(2)}, u32[]{:S(2)}) collective-permute-start(bf16[32,3584]{1,0:T(8,128)(2,1)S(1)} %maximum_select_fusion), channel_id=1, source_target_pairs={{0,16},{1,17},{2,18},{3,19},{4,20},{5,21},{6,22},{7,23},{8,24},{9,... | collective-permute-start | bytes 688136 | tf_op jit(solution)/shard_map/ppermute | solution.py:270
  11.5 1.8 %collective-permute-start.4 = (bf16[2,1,32,1792]{3,2,0,1:T(8,128)(2,1)S(1)}, bf16[2,1,32,1792]{3,2,0,1:T(8,128)(2,1)S(1)}, u32[]{:S(2)}, u32[]{:S(2)}) collective-permute-start(bf16[2,1,32,1792]{3,2,0,1:T(8,128)(2,1)S(1)} %pad_maximum_fusion.4), channel_id=1, source_target_pairs={{0,4},{1,5},{2,6},{3,7},{4,0},{5,1},{6,2},{7,3},{8,12},{9,13},{10,... | collective-permute-start | bytes 688136 | tf_op jit(solution)/shard_map/ppermute | solution.py:267
  13.3 2.0 %copy-done.1 = bf16[1,7168,256]{2,1,0:T(8,128)(2,1)S(1)} copy-done((bf16[1,7168,256]{2,1,0:T(8,128)(2,1)S(1)}, bf16[1,7168,256]{2,1,0:T(8,128)(2,1)}, u32[]{:S(2)}) %copy-start.1) | copy-done | bytes 3670040
  15.3 2.0 %copy-done.4 = bf16[1,7168,256]{2,1,0:T(8,128)(2,1)S(1)} copy-done((bf16[1,7168,256]{2,1,0:T(8,128)(2,1)S(1)}, bf16[1,7168,256]{2,1,0:T(8,128)(2,1)}, u32[]{:S(2)}) %copy-start.4) | copy-done | bytes 3670040
  18.5 2.0 %collective-permute-done.6 = bf16[32,3584]{1,0:T(8,128)(2,1)S(1)} collective-permute-done((bf16[32,3584]{1,0:T(8,128)(2,1)S(1)}, bf16[32,3584]{1,0:T(8,128)(2,1)S(1)}, u32[]{:S(2)}, u32[]{:S(2)}) %collective-permute-start.6) | collective-permute-done | bytes 229408 | tf_op jit(solution)/shard_map/ppermute | solution.py:270
  22.6 2.8 %collective-permute-start.12 = (bf16[32,3584]{1,0:T(8,128)(2,1)S(1)}, bf16[32,3584]{1,0:T(8,128)(2,1)S(1)}, u32[]{:S(2)}, u32[]{:S(2)}) collective-permute-start(bf16[32,3584]{1,0:T(8,128)(2,1)S(1)} %maximum_select_fusion), channel_id=1, source_target_pairs={{0,24},{1,25},{2,26},{3,27},{4,28},{5,29},{6,30},{7,31},{8,0},{9,1... | collective-permute-start | bytes 688136 | tf_op jit(solution)/shard_map/ppermute | solution.py:270
  26.5 1.6 %collective-permute-start.10 = (bf16[2,1,32,1792]{3,2,0,1:T(8,128)(2,1)S(1)}, bf16[2,1,32,1792]{3,2,0,1:T(8,128)(2,1)S(1)}, u32[]{:S(2)}, u32[]{:S(2)}) collective-permute-start(bf16[2,1,32,1792]{3,2,0,1:T(8,128)(2,1)S(1)} %get-tuple-element.182), channel_id=1, source_target_pairs={{0,2},{1,3},{2,0},{3,1},{4,6},{5,7},{6,4},{7,5},{8,10},{9,11},{10,... | collective-permute-start | bytes 688136 | tf_op jit(solution)/shard_map/ppermute | solution.py:267
  28.8 1.9 %copy-done.9 = bf16[1,256,7168]{2,1,0:T(8,128)(2,1)S(1)} copy-done((bf16[1,256,7168]{2,1,0:T(8,128)(2,1)S(1)}, bf16[1,256,7168]{2,1,0:T(8,128)(2,1)}, u32[]{:S(2)}) %copy-start.9) | copy-done | bytes 3670040
  30.7 3.8 %exit_half.1 = (bf16[256,3584]{1,0:T(8,128)(2,1)}, bf16[256,3584]{1,0:T(8,128)(2,1)S(1)}) custom-call(s32[1]{0:T(128)} %bitcast.21._, bf16[256,7168]{1,0:T(8,128)(2,1)S(1)} %bitcast.110, bf16[256,7168]{1,0:T(8,128)(2,1)S(1)} %bitcast.111), custom_call_target="tpu_custom_call" | custom-call | flops 1 | bytes 1 | tf_op jit(solution)/shard_map/exit_half/pallas_call | solution.py:131
  38.0 1.7 %entry_products.4 = f32[2,256,256]{2,1,0:T(8,128)S(1)} custom-call(s32[1]{0:T(128)} %bitcast.10._.core_ref, bf16[256,3584]{1,0:T(8,128)(2,1)S(1)} %pad_maximum_fusion.rows_ref, bf16[2,3584,256]{2,1,0:T(8,128)(2,1)S(1)} %collective-permute-done.15.refs_0_), custom_call_target="tpu_custom_call" | custom-call | flops 1 | bytes 1 | tf_op jit(solution)/shard_map/entry_products/pallas_call | solution.py:163
  40.4 2.7 %collective-permute-done.14 = bf16[2,32,1792]{2,1,0:T(8,128)(2,1)S(1)} collective-permute-done((bf16[2,32,1792]{2,1,0:T(8,128)(2,1)S(1)}, bf16[2,32,1792]{2,1,0:T(8,128)(2,1)S(1)}, u32[]{:S(2)}, u32[]{:S(2)}) %collective-permute-start.14) | collective-permute-done | bytes 229408 | tf_op jit(solution)/shard_map/ppermute | solution.py:267
  47.3 2.0 %copy-done.2 = bf16[1,7168,256]{2,1,0:T(8,128)(2,1)S(1)} copy-done((bf16[1,7168,256]{2,1,0:T(8,128)(2,1)S(1)}, bf16[1,7168,256]{2,1,0:T(8,128)(2,1)}, u32[]{:S(2)}) %copy-start.2) | copy-done | bytes 3670040
  49.3 2.0 %copy-done.5 = bf16[1,7168,256]{2,1,0:T(8,128)(2,1)S(1)} copy-done((bf16[1,7168,256]{2,1,0:T(8,128)(2,1)S(1)}, bf16[1,7168,256]{2,1,0:T(8,128)(2,1)}, u32[]{:S(2)}) %copy-start.5) | copy-done | bytes 3670040
  52.8 1.7 %entry_products.5.own_ref = f32[2,256,256]{2,1,0:T(8,128)S(1)} custom-call(s32[1]{0:T(128)} %bitcast.10._.core_ref, bf16[256,3584]{1,0:T(8,128)(2,1)S(1)} %copy-done.8, bf16[7168,256]{1,0:T(8,128)(2,1)S(1)} %bitcast.103, bf16[7168,256]{1,0:T(8,128)(2,1)S(1)} %bitcast.106), custom_call_target="tpu_custom_call" | custom-call | flops 1 | bytes 1 | tf_op jit(solution)/shard_map/entry_products/pallas_call | solution.py:163
  56.2 2.2 %exit_sums.4 = (bf16[2,2,32,1792]{3,2,1,0:T(8,128)(2,1)S(1)}, bf16[2,2,32,1792]{3,2,1,0:T(8,128)(2,1)S(1)}) custom-call(bf16[256,256]{1,0:T(8,128)(2,1)S(1)} %inner_units.2.own_ref, bf16[256,256]{1,0:T(8,128)(2,1)S(1)} %collective-permute-done.19.other_ref, bf16[256,3584]{1,0:T(8,128)(2,1)S(1)} %get-tuple-element.119.down_own_ref, ...), custom_call_target="tpu_custom_call" | custom-call | flops 1 | bytes 1 | tf_op jit(solution)/shard_map/exit_sums/pallas_call | solution.py:231
  60.9 1.6 %maximum_bitcast_fusion = bf16[2,2,2,32,3584]{4,3,0,1,2:T(8,128)(2,1)S(1)} fusion(bf16[2,1,2,32,1792]{4,3,2,0,1:T(8,128)(2,1)} %bitcast.47, bf16[2,1,2,32,1792]{4,3,2,0,1:T(8,128)(2,1)S(1)} %bitcast.114, bf16[1,2,2,32,1792]{4,3,2,0,1:T(8,128)(2,1)} %bitcast.45, bf16[1,2,2,32,1792]{4,3,2,0,1:T(8,128)(2,1)} %bitcast.44), kind=kLoop, calls=%fused_computation.1 | loop fusion | flops 7340032 | bytes 3670016 | tf_op jit(solution)/shard_map/transpose | solution.py:322
  64.7 1.9 %entry_products.6.own_ref = f32[2,256,256]{2,1,0:T(8,128)S(1)} custom-call(s32[1]{0:T(128)} %bitcast.10._.core_ref, bf16[256,3584]{1,0:T(8,128)(2,1)S(1)} %bitcast.108, bf16[7168,256]{1,0:T(8,128)(2,1)S(1)} %bitcast.104, bf16[7168,256]{1,0:T(8,128)(2,1)S(1)} %bitcast.107), custom_call_target="tpu_custom_call" | custom-call | flops 1 | bytes 1 | tf_op jit(solution)/shard_map/entry_products/pallas_call | solution.py:163
  66.8 1.9 %entry_products.7 = f32[2,256,256]{2,1,0:T(8,128)S(1)} custom-call(s32[1]{0:T(128)} %bitcast.10._.core_ref, bf16[256,3584]{1,0:T(8,128)(2,1)S(1)} %bitcast.109, bf16[2,3584,256]{2,1,0:T(8,128)(2,1)S(1)} %copy-done.11), custom_call_target="tpu_custom_call" | custom-call | flops 1 | bytes 1 | tf_op jit(solution)/shard_map/entry_products/pallas_call | solution.py:163
  68.7 2.3 %exit_sums.5 = (f32[2,2,32,1792]{3,2,1,0:T(8,128)S(1)}, f32[2,2,32,1792]{3,2,1,0:T(8,128)S(1)}) custom-call(bf16[256,256]{1,0:T(8,128)(2,1)S(1)} %inner_units.2.own_ref, bf16[256,256]{1,0:T(8,128)(2,1)S(1)} %collective-permute-done.19.other_ref, bf16[256,3584]{1,0:T(8,128)(2,1)S(1)} %get-tuple-element.119.down_own_ref, ...), custom_call_target="tpu_custom_call" | custom-call | flops 1 | bytes 1 | tf_op jit(solution)/shard_map/exit_sums/pallas_call | solution.py:231
  75.9 2.1 %exit_sums.6 = (bf16[2,2,32,1792]{3,2,1,0:T(8,128)(2,1)S(1)}, bf16[2,2,32,1792]{3,2,1,0:T(8,128)(2,1)S(1)}) custom-call(bf16[256,256]{1,0:T(8,128)(2,1)S(1)} %inner_units.3.own_ref, bf16[256,256]{1,0:T(8,128)(2,1)S(1)} %collective-permute-done.26.other_ref, bf16[256,3584]{1,0:T(8,128)(2,1)S(1)} %get-tuple-element.119.down_own_ref, ...), custom_call_target="tpu_custom_call" | custom-call | flops 1 | bytes 1 | tf_op jit(solution)/shard_map/exit_sums/pallas_call | solution.py:231
  78.1 2.6 %collective-permute-done.24 = bf16[2,32,1792]{2,1,0:T(8,128)(2,1)S(1)} collective-permute-done((bf16[2,32,1792]{2,1,0:T(8,128)(2,1)S(1)}, bf16[2,32,1792]{2,1,0:T(8,128)(2,1)S(1)}, u32[]{:S(2)}, u32[]{:S(2)}) %collective-permute-start.24) | collective-permute-done | bytes 229408 | tf_op jit(solution)/shard_map/ppermute | solution.py:267
  83.3 2.0 %collective-permute-start.27 = (bf16[32,3584]{1,0:T(8,128)(2,1)S(1)}, bf16[32,3584]{1,0:T(8,128)(2,1)S(1)}, u32[]{:S(2)}, u32[]{:S(2)}) collective-permute-start(bf16[32,3584]{1,0:T(8,128)(2,1)S(1)} %fusion.5), channel_id=1, source_target_pairs={{0,16},{1,17},{2,18},{3,19},{4,20},{5,21},{6,22},{7,23},{8,24},{9,... | collective-permute-start | bytes 688136 | tf_op jit(solution)/shard_map/ppermute | solution.py:270
  85.4 2.8 %latent_attention.4.refs_0_ = bf16[16,128,512]{2,1,0:T(8,128)(2,1)} custom-call(s32[16]{0:T(128)S(1)} %copy-done.12, bf16[16,576,128]{2,1,0:T(8,128)(2,1)S(1)} %bitcast.98, bf16[16,576,512]{2,1,0:T(8,128)(2,1)S(1)} %bitcast.94), custom_call_target="tpu_custom_call" | custom-call | flops 1 | bytes 1 | tf_op jit(solution)/shard_map/latent_attention/pallas_call | solution.py:56
  88.1 2.1 %exit_sums.7 = (f32[2,2,32,1792]{3,2,1,0:T(8,128)S(1)}, f32[2,2,32,1792]{3,2,1,0:T(8,128)S(1)}) custom-call(bf16[256,256]{1,0:T(8,128)(2,1)S(1)} %inner_units.3.own_ref, bf16[256,256]{1,0:T(8,128)(2,1)S(1)} %collective-permute-done.26.other_ref, bf16[256,3584]{1,0:T(8,128)(2,1)S(1)} %get-tuple-element.119.down_own_ref, ...), custom_call_target="tpu_custom_call" | custom-call | flops 1 | bytes 1 | tf_op jit(solution)/shard_map/exit_sums/pallas_call | solution.py:231
  90.3 2.8 %collective-permute-done.28 = bf16[2,2,32,1792]{3,2,1,0:T(8,128)(2,1)S(1)} collective-permute-done((bf16[2,2,32,1792]{3,2,1,0:T(8,128)(2,1)S(1)}, bf16[2,2,32,1792]{3,2,1,0:T(8,128)(2,1)S(1)}, u32[]{:S(2)}, u32[]{:S(2)}) %collective-permute-start.28) | collective-permute-done | bytes 458784 | tf_op jit(solution)/shard_map/ppermute | solution.py:267
  95.9 2.8 %latent_attention.5.refs_0_ = bf16[16,128,512]{2,1,0:T(8,128)(2,1)} custom-call(s32[16]{0:T(128)S(1)} %copy-done.12, bf16[16,576,128]{2,1,0:T(8,128)(2,1)S(1)} %bitcast.99, bf16[16,576,512]{2,1,0:T(8,128)(2,1)S(1)} %bitcast.95, bf16[16,128,512]{2,1,0:T(8,128)(2,1)} %latent_attention.4.refs_0_), custom_call_target="tpu_custom_call", output_to_operand_aliasing={{}: (3, {})} | custom-call | flops 1 | bytes 1 | tf_op jit(solution)/shard_map/latent_attention/pallas_call | solution.py:56
  98.6 1.9 %collective-permute-done.31 = bf16[2,32,1792]{2,1,0:T(8,128)(2,1)S(1)} collective-permute-done((bf16[2,32,1792]{2,1,0:T(8,128)(2,1)S(1)}, bf16[2,32,1792]{2,1,0:T(8,128)(2,1)S(1)}, u32[]{:S(2)}, u32[]{:S(2)}) %collective-permute-start.31) | collective-permute-done | bytes 229408 | tf_op jit(solution)/shard_map/ppermute | solution.py:267
  101.4 3.2 %collective-permute-start.32 = (bf16[32,3584]{1,0:T(8,128)(2,1)S(1)}, bf16[32,3584]{1,0:T(8,128)(2,1)S(1)}, u32[]{:S(2)}, u32[]{:S(2)}) collective-permute-start(bf16[32,3584]{1,0:T(8,128)(2,1)S(1)} %get-tuple-element.175), channel_id=1, source_target_pairs={{0,24},{1,25},{2,26},{3,27},{4,28},{5,29},{6,30},{7,31},{8,0},{9,1... | collective-permute-start | bytes 688136 | tf_op jit(solution)/shard_map/ppermute | solution.py:270
  104.6 2.8 %latent_attention.6.refs_0_ = bf16[16,128,512]{2,1,0:T(8,128)(2,1)} custom-call(s32[16]{0:T(128)S(1)} %copy-done.12, bf16[16,576,128]{2,1,0:T(8,128)(2,1)S(1)} %bitcast.100, bf16[16,576,512]{2,1,0:T(8,128)(2,1)S(1)} %bitcast.96, bf16[16,128,512]{2,1,0:T(8,128)(2,1)} %latent_attention.5.refs_0_), custom_call_target="tpu_custom_call", output_to_operand_aliasing={{}: (3, {})} | custom-call | flops 1 | bytes 1 | tf_op jit(solution)/shard_map/latent_attention/pallas_call | solution.py:56
  107.3 2.8 %latent_attention.7 = bf16[16,128,512]{2,1,0:T(8,128)(2,1)} custom-call(s32[16]{0:T(128)S(1)} %copy-done.12, bf16[16,576,128]{2,1,0:T(8,128)(2,1)S(1)} %bitcast.101, bf16[16,576,512]{2,1,0:T(8,128)(2,1)S(1)} %bitcast.97, bf16[16,128,512]{2,1,0:T(8,128)(2,1)} %latent_attention.6.refs_0_), custom_call_target="tpu_custom_call", output_to_operand_aliasing={{}: (3, {})} | custom-call | flops 1 | bytes 1 | tf_op jit(solution)/shard_map/latent_attention/pallas_call | solution.py:56
  110.1 3.0 %collective-permute-done.33 = bf16[32,3584]{1,0:T(8,128)(2,1)S(1)} collective-permute-done((bf16[32,3584]{1,0:T(8,128)(2,1)S(1)}, bf16[32,3584]{1,0:T(8,128)(2,1)S(1)}, u32[]{:S(2)}, u32[]{:S(2)}) %collective-permute-start.33) | collective-permute-done | bytes 229408 | tf_op jit(solution)/shard_map/ppermute | solution.py:270
  (139 shorter events, 40.0 us)
Async XLA Ops:
  1.6 1.5 %collective-permute-start.1 = (bf16[16,3584]{1,0:T(8,128)(2,1)S(1)}, bf16[16,3584]{1,0:T(8,128)(2,1)S(1)}, u32[]{:S(2)}, u32[]{:S(2)}) collective-permute-start(bf16[16,3584]{1,0:T(8,128)(2,1)S(1)} %get-tuple-element.191), channel_id=1, source_target_pairs={{0,1},{1,0},{2,3},{3,2},{4,5},{5,4},{6,7},{7,6},{8,9},{9,8},{10,11... | collective-permute-start | bytes 344072 | tf_op jit(solution)/shard_map/ppermute | solution.py:267
  3.2 7.5 %collective-permute-start.2 = (bf16[1,32,1792]{2,1,0:T(8,128)(2,1)S(1)}, bf16[1,32,1792]{2,1,0:T(8,128)(2,1)S(1)}, u32[]{:S(2)}, u32[]{:S(2)}) collective-permute-start(bf16[1,32,1792]{2,1,0:T(8,128)(2,1)S(1)} %get-tuple-element.87), channel_id=1, source_target_pairs={{0,2},{1,3},{2,0},{3,1},{4,6},{5,7},{6,4},{7,5},{8,10},{9,11},{10,... | collective-permute-start | bytes 344072 | tf_op jit(solution)/shard_map/ppermute | solution.py:267
  6.1 4.9 %collective-permute-start.3 = (bf16[1,32,1792]{2,1,0:T(8,128)(2,1)S(1)}, bf16[1,32,1792]{2,1,0:T(8,128)(2,1)S(1)}, u32[]{:S(2)}, u32[]{:S(2)}) collective-permute-start(bf16[1,32,1792]{2,1,0:T(8,128)(2,1)S(1)} %get-tuple-element.89), channel_id=1, source_target_pairs={{0,4},{1,5},{2,6},{3,7},{4,0},{5,1},{6,2},{7,3},{8,12},{9,13},{10,... | collective-permute-start | bytes 344072 | tf_op jit(solution)/shard_map/ppermute | solution.py:267
  7.6 12.9 %collective-permute-start.6 = (bf16[32,3584]{1,0:T(8,128)(2,1)S(1)}, bf16[32,3584]{1,0:T(8,128)(2,1)S(1)}, u32[]{:S(2)}, u32[]{:S(2)}) collective-permute-start(bf16[32,3584]{1,0:T(8,128)(2,1)S(1)} %maximum_select_fusion), channel_id=1, source_target_pairs={{0,16},{1,17},{2,18},{3,19},{4,20},{5,21},{6,22},{7,23},{8,24},{9,... | collective-permute-start | bytes 688136 | tf_op jit(solution)/shard_map/ppermute | solution.py:270
  11.0 9.5 %collective-permute-start.5 = (bf16[2,1,32,1792]{3,2,0,1:T(8,128)(2,1)S(1)}, bf16[2,1,32,1792]{3,2,0,1:T(8,128)(2,1)S(1)}, u32[]{:S(2)}, u32[]{:S(2)}) collective-permute-start(bf16[2,1,32,1792]{3,2,0,1:T(8,128)(2,1)S(1)} %get-tuple-element.186), channel_id=1, source_target_pairs={{0,2},{1,3},{2,0},{3,1},{4,6},{5,7},{6,4},{7,5},{8,10},{9,11},{10,... | collective-permute-start | bytes 688136 | tf_op jit(solution)/shard_map/ppermute | solution.py:267
  11.5 9.0 %collective-permute-start.4 = (bf16[2,1,32,1792]{3,2,0,1:T(8,128)(2,1)S(1)}, bf16[2,1,32,1792]{3,2,0,1:T(8,128)(2,1)S(1)}, u32[]{:S(2)}, u32[]{:S(2)}) collective-permute-start(bf16[2,1,32,1792]{3,2,0,1:T(8,128)(2,1)S(1)} %pad_maximum_fusion.4), channel_id=1, source_target_pairs={{0,4},{1,5},{2,6},{3,7},{4,0},{5,1},{6,2},{7,3},{8,12},{9,13},{10,... | collective-permute-start | bytes 688136 | tf_op jit(solution)/shard_map/ppermute | solution.py:267
  20.5 17.5 %collective-permute-start.15 = (bf16[2,3584,256]{2,1,0:T(8,128)(2,1)S(1)}, bf16[2,3584,256]{2,1,0:T(8,128)(2,1)S(1)}, u32[]{:S(2)}, u32[]{:S(2)}) collective-permute-start(bf16[2,3584,256]{2,1,0:T(8,128)(2,1)S(1)} %entry_half.1), channel_id=1, source_target_pairs={{0,1},{1,0},{2,3},{3,2},{4,5},{5,4},{6,7},{7,6},{8,9},{9,8},{10,11... | collective-permute-start | bytes 11010056 | tf_op jit(solution)/shard_map/ppermute | solution.py:267
  20.6 5.6 %collective-permute-start.7 = (bf16[1,32,1792]{2,1,0:T(8,128)(2,1)S(1)}, bf16[1,32,1792]{2,1,0:T(8,128)(2,1)S(1)}, u32[]{:S(2)}, u32[]{:S(2)}) collective-permute-start(bf16[1,32,1792]{2,1,0:T(8,128)(2,1)S(1)} %get-tuple-element.94), channel_id=1, source_target_pairs={{0,2},{1,3},{2,0},{3,1},{4,6},{5,7},{6,4},{7,5},{8,10},{9,11},{10,... | collective-permute-start | bytes 344072 | tf_op jit(solution)/shard_map/ppermute | solution.py:267
  21.2 5.3 %collective-permute-start.8 = (bf16[1,32,1792]{2,1,0:T(8,128)(2,1)S(1)}, bf16[1,32,1792]{2,1,0:T(8,128)(2,1)S(1)}, u32[]{:S(2)}, u32[]{:S(2)}) collective-permute-start(bf16[1,32,1792]{2,1,0:T(8,128)(2,1)S(1)} %get-tuple-element.96), channel_id=1, source_target_pairs={{0,4},{1,5},{2,6},{3,7},{4,0},{5,1},{6,2},{7,3},{8,12},{9,13},{10,... | collective-permute-start | bytes 344072 | tf_op jit(solution)/shard_map/ppermute | solution.py:267
  21.6 12.9 %collective-permute-start.11 = (bf16[32,3584]{1,0:T(8,128)(2,1)S(1)}, bf16[32,3584]{1,0:T(8,128)(2,1)S(1)}, u32[]{:S(2)}, u32[]{:S(2)}) collective-permute-start(bf16[32,3584]{1,0:T(8,128)(2,1)S(1)} %maximum_select_fusion), channel_id=1, source_target_pairs={{0,8},{1,9},{2,10},{3,11},{4,12},{5,13},{6,14},{7,15},{8,16},{9,17... | collective-permute-start | bytes 688136 | tf_op jit(solution)/shard_map/ppermute | solution.py:270
  22.6 12.1 %collective-permute-start.12 = (bf16[32,3584]{1,0:T(8,128)(2,1)S(1)}, bf16[32,3584]{1,0:T(8,128)(2,1)S(1)}, u32[]{:S(2)}, u32[]{:S(2)}) collective-permute-start(bf16[32,3584]{1,0:T(8,128)(2,1)S(1)} %maximum_select_fusion), channel_id=1, source_target_pairs={{0,24},{1,25},{2,26},{3,27},{4,28},{5,29},{6,30},{7,31},{8,0},{9,1... | collective-permute-start | bytes 688136 | tf_op jit(solution)/shard_map/ppermute | solution.py:270
  26.5 8.3 %collective-permute-start.10 = (bf16[2,1,32,1792]{3,2,0,1:T(8,128)(2,1)S(1)}, bf16[2,1,32,1792]{3,2,0,1:T(8,128)(2,1)S(1)}, u32[]{:S(2)}, u32[]{:S(2)}) collective-permute-start(bf16[2,1,32,1792]{3,2,0,1:T(8,128)(2,1)S(1)} %get-tuple-element.182), channel_id=1, source_target_pairs={{0,2},{1,3},{2,0},{3,1},{4,6},{5,7},{6,4},{7,5},{8,10},{9,11},{10,... | collective-permute-start | bytes 688136 | tf_op jit(solution)/shard_map/ppermute | solution.py:267
  28.0 6.7 %collective-permute-start.9 = (bf16[2,1,32,1792]{3,2,0,1:T(8,128)(2,1)S(1)}, bf16[2,1,32,1792]{3,2,0,1:T(8,128)(2,1)S(1)}, u32[]{:S(2)}, u32[]{:S(2)}) collective-permute-start(bf16[2,1,32,1792]{3,2,0,1:T(8,128)(2,1)S(1)} %pad_maximum_fusion.6), channel_id=1, source_target_pairs={{0,4},{1,5},{2,6},{3,7},{4,0},{5,1},{6,2},{7,3},{8,12},{9,13},{10,... | collective-permute-start | bytes 688136 | tf_op jit(solution)/shard_map/ppermute | solution.py:267
  34.9 20.4 %collective-permute-start.20 = (bf16[256,3584]{1,0:T(8,128)(2,1)}, bf16[256,3584]{1,0:T(8,128)(2,1)}, u32[]{:S(2)}, u32[]{:S(2)}) collective-permute-start(bf16[256,3584]{1,0:T(8,128)(2,1)} %get-tuple-element.120), channel_id=1, source_target_pairs={{0,1},{1,0},{2,3},{3,2},{4,5},{5,4},{6,7},{7,6},{8,9},{9,8},{10,11... | collective-permute-start | bytes 5505032 | tf_op jit(solution)/shard_map/ppermute | solution.py:267
  35.0 8.1 %collective-permute-start.14 = (bf16[2,32,1792]{2,1,0:T(8,128)(2,1)S(1)}, bf16[2,32,1792]{2,1,0:T(8,128)(2,1)S(1)}, u32[]{:S(2)}, u32[]{:S(2)}) collective-permute-start(bf16[2,32,1792]{2,1,0:T(8,128)(2,1)S(1)} %pad_maximum_fusion.9), channel_id=1, source_target_pairs={{0,4},{1,5},{2,6},{3,7},{4,0},{5,1},{6,2},{7,3},{8,12},{9,13},{10,... | collective-permute-start | bytes 688136 | tf_op jit(solution)/shard_map/ppermute | solution.py:267
  36.4 7.8 %collective-permute-start.13 = (bf16[2,32,1792]{2,1,0:T(8,128)(2,1)S(1)}, bf16[2,32,1792]{2,1,0:T(8,128)(2,1)S(1)}, u32[]{:S(2)}, u32[]{:S(2)}) collective-permute-start(bf16[2,32,1792]{2,1,0:T(8,128)(2,1)S(1)} %pad_maximum_fusion.8), channel_id=1, source_target_pairs={{0,2},{1,3},{2,0},{3,1},{4,6},{5,7},{6,4},{7,5},{8,10},{9,11},{10,... | collective-permute-start | bytes 688136 | tf_op jit(solution)/shard_map/ppermute | solution.py:267
  44.2 10.4 %collective-permute-start.18 = (f32[2,256,256]{2,1,0:T(8,128)S(1)}, f32[2,256,256]{2,1,0:T(8,128)S(1)}, u32[]{:S(2)}, u32[]{:S(2)}) collective-permute-start(f32[2,256,256]{2,1,0:T(8,128)S(1)} %entry_products.4), channel_id=1, source_target_pairs={{0,1},{1,0},{2,3},{3,2},{4,5},{5,4},{6,7},{7,6},{8,9},{9,8},{10,11... | collective-permute-start | bytes 1572872 | tf_op jit(solution)/shard_map/ppermute | solution.py:267
  44.2 14.1 %collective-permute-start.17 = (bf16[2,2,32,1792]{3,2,1,0:T(8,128)(2,1)S(1)}, bf16[2,2,32,1792]{3,2,1,0:T(8,128)(2,1)}, u32[]{:S(2)}, u32[]{:S(2)}) collective-permute-start(bf16[2,2,32,1792]{3,2,1,0:T(8,128)(2,1)S(1)} %pad_maximum_fusion.3), channel_id=1, source_target_pairs={{0,2},{1,3},{2,0},{3,1},{4,6},{5,7},{6,4},{7,5},{8,10},{9,11},{10,... | collective-permute-start | bytes 1376264 | tf_op jit(solution)/shard_map/ppermute | solution.py:267
  46.6 13.0 %collective-permute-start.16 = (bf16[2,2,32,1792]{3,2,1,0:T(8,128)(2,1)}, bf16[2,2,32,1792]{3,2,1,0:T(8,128)(2,1)}, u32[]{:S(2)}, u32[]{:S(2)}) collective-permute-start(bf16[2,2,32,1792]{3,2,1,0:T(8,128)(2,1)} %pad_maximum_fusion.2), channel_id=1, source_target_pairs={{0,4},{1,5},{2,6},{3,7},{4,0},{5,1},{6,2},{7,3},{8,12},{9,13},{10,... | collective-permute-start | bytes 1376264 | tf_op jit(solution)/shard_map/ppermute | solution.py:267
  47.1 8.1 %collective-permute-start = (f32[16,4]{0,1:T(4,128)S(1)}, f32[16,4]{0,1:T(4,128)S(1)}, u32[]{:S(2)}, u32[]{:S(2)}) collective-permute-start(f32[16,4]{0,1:T(4,128)S(1)} %select_reduce_fusion), channel_id=1, source_target_pairs={{0,1},{1,0},{2,3},{3,2},{4,5},{5,4},{6,7},{7,6},{8,9},{9,8},{10,11... | collective-permute-start | bytes 776 | tf_op jit(solution)/shard_map/ppermute | solution.py:267
  59.5 11.8 %collective-permute-start.21 = (bf16[2,2,32,1792]{3,2,1,0:T(8,128)(2,1)S(1)}, bf16[2,2,32,1792]{3,2,1,0:T(8,128)(2,1)S(1)}, u32[]{:S(2)}, u32[]{:S(2)}) collective-permute-start(bf16[2,2,32,1792]{3,2,1,0:T(8,128)(2,1)S(1)} %get-tuple-element.127), channel_id=1, source_target_pairs={{0,4},{1,5},{2,6},{3,7},{4,0},{5,1},{6,2},{7,3},{8,12},{9,13},{10,... | collective-permute-start | bytes 1376264 | tf_op jit(solution)/shard_map/ppermute | solution.py:267
  60.0 12.4 %collective-permute-start.22 = (bf16[2,2,32,1792]{3,2,1,0:T(8,128)(2,1)S(1)}, bf16[2,2,32,1792]{3,2,1,0:T(8,128)(2,1)S(1)}, u32[]{:S(2)}, u32[]{:S(2)}) collective-permute-start(bf16[2,2,32,1792]{3,2,1,0:T(8,128)(2,1)S(1)} %get-tuple-element.128), channel_id=1, source_target_pairs={{0,2},{1,3},{2,0},{3,1},{4,6},{5,7},{6,4},{7,5},{8,10},{9,11},{10,... | collective-permute-start | bytes 1376264 | tf_op jit(solution)/shard_map/ppermute | solution.py:267
  72.4 1.9 %collective-permute-start.25 = (f32[2,256,256]{2,1,0:T(8,128)S(1)}, f32[2,256,256]{2,1,0:T(8,128)S(1)}, u32[]{:S(2)}, u32[]{:S(2)}) collective-permute-start(f32[2,256,256]{2,1,0:T(8,128)S(1)} %entry_products.7), channel_id=1, source_target_pairs={{0,1},{1,0},{2,3},{3,2},{4,5},{5,4},{6,7},{7,6},{8,9},{9,8},{10,11... | collective-permute-start | bytes 1572872 | tf_op jit(solution)/shard_map/ppermute | solution.py:267
  72.6 8.1 %collective-permute-start.24 = (bf16[2,32,1792]{2,1,0:T(8,128)(2,1)S(1)}, bf16[2,32,1792]{2,1,0:T(8,128)(2,1)S(1)}, u32[]{:S(2)}, u32[]{:S(2)}) collective-permute-start(bf16[2,32,1792]{2,1,0:T(8,128)(2,1)S(1)} %fusion.4), channel_id=1, source_target_pairs={{0,4},{1,5},{2,6},{3,7},{4,0},{5,1},{6,2},{7,3},{8,12},{9,13},{10,... | collective-permute-start | bytes 688136 | tf_op jit(solution)/shard_map/ppermute | solution.py:267
  73.4 7.8 %collective-permute-start.23 = (bf16[2,32,1792]{2,1,0:T(8,128)(2,1)S(1)}, bf16[2,32,1792]{2,1,0:T(8,128)(2,1)S(1)}, u32[]{:S(2)}, u32[]{:S(2)}) collective-permute-start(bf16[2,32,1792]{2,1,0:T(8,128)(2,1)S(1)} %fusion.3), channel_id=1, source_target_pairs={{0,2},{1,3},{2,0},{3,1},{4,6},{5,7},{6,4},{7,5},{8,10},{9,11},{10,... | collective-permute-start | bytes 688136 | tf_op jit(solution)/shard_map/ppermute | solution.py:267
  81.2 11.8 %collective-permute-start.28 = (bf16[2,2,32,1792]{3,2,1,0:T(8,128)(2,1)S(1)}, bf16[2,2,32,1792]{3,2,1,0:T(8,128)(2,1)S(1)}, u32[]{:S(2)}, u32[]{:S(2)}) collective-permute-start(bf16[2,2,32,1792]{3,2,1,0:T(8,128)(2,1)S(1)} %get-tuple-element.149), channel_id=1, source_target_pairs={{0,4},{1,5},{2,6},{3,7},{4,0},{5,1},{6,2},{7,3},{8,12},{9,13},{10,... | collective-permute-start | bytes 1376264 | tf_op jit(solution)/shard_map/ppermute | solution.py:267
  82.6 11.6 %collective-permute-start.29 = (bf16[2,2,32,1792]{3,2,1,0:T(8,128)(2,1)S(1)}, bf16[2,2,32,1792]{3,2,1,0:T(8,128)(2,1)S(1)}, u32[]{:S(2)}, u32[]{:S(2)}) collective-permute-start(bf16[2,2,32,1792]{3,2,1,0:T(8,128)(2,1)S(1)} %get-tuple-element.150), channel_id=1, source_target_pairs={{0,2},{1,3},{2,0},{3,1},{4,6},{5,7},{6,4},{7,5},{8,10},{9,11},{10,... | collective-permute-start | bytes 1376264 | tf_op jit(solution)/shard_map/ppermute | solution.py:267
  83.3 26.8 %collective-permute-start.27 = (bf16[32,3584]{1,0:T(8,128)(2,1)S(1)}, bf16[32,3584]{1,0:T(8,128)(2,1)S(1)}, u32[]{:S(2)}, u32[]{:S(2)}) collective-permute-start(bf16[32,3584]{1,0:T(8,128)(2,1)S(1)} %fusion.5), channel_id=1, source_target_pairs={{0,16},{1,17},{2,18},{3,19},{4,20},{5,21},{6,22},{7,23},{8,24},{9,... | collective-permute-start | bytes 688136 | tf_op jit(solution)/shard_map/ppermute | solution.py:270
  94.4 6.1 %collective-permute-start.31 = (bf16[2,32,1792]{2,1,0:T(8,128)(2,1)S(1)}, bf16[2,32,1792]{2,1,0:T(8,128)(2,1)S(1)}, u32[]{:S(2)}, u32[]{:S(2)}) collective-permute-start(bf16[2,32,1792]{2,1,0:T(8,128)(2,1)S(1)} %fusion.7), channel_id=1, source_target_pairs={{0,4},{1,5},{2,6},{3,7},{4,0},{5,1},{6,2},{7,3},{8,12},{9,13},{10,... | collective-permute-start | bytes 688136 | tf_op jit(solution)/shard_map/ppermute | solution.py:267
  95.2 6.0 %collective-permute-start.30 = (bf16[2,32,1792]{2,1,0:T(8,128)(2,1)S(1)}, bf16[2,32,1792]{2,1,0:T(8,128)(2,1)S(1)}, u32[]{:S(2)}, u32[]{:S(2)}) collective-permute-start(bf16[2,32,1792]{2,1,0:T(8,128)(2,1)S(1)} %fusion.6), channel_id=1, source_target_pairs={{0,2},{1,3},{2,0},{3,1},{4,6},{5,7},{6,4},{7,5},{8,10},{9,11},{10,... | collective-permute-start | bytes 688136 | tf_op jit(solution)/shard_map/ppermute | solution.py:267
  101.4 8.7 %collective-permute-start.32 = (bf16[32,3584]{1,0:T(8,128)(2,1)S(1)}, bf16[32,3584]{1,0:T(8,128)(2,1)S(1)}, u32[]{:S(2)}, u32[]{:S(2)}) collective-permute-start(bf16[32,3584]{1,0:T(8,128)(2,1)S(1)} %get-tuple-element.175), channel_id=1, source_target_pairs={{0,24},{1,25},{2,26},{3,27},{4,28},{5,29},{6,30},{7,31},{8,0},{9,1... | collective-permute-start | bytes 688136 | tf_op jit(solution)/shard_map/ppermute | solution.py:270
  104.6 8.6 %collective-permute-start.33 = (bf16[32,3584]{1,0:T(8,128)(2,1)S(1)}, bf16[32,3584]{1,0:T(8,128)(2,1)S(1)}, u32[]{:S(2)}, u32[]{:S(2)}) collective-permute-start(bf16[32,3584]{1,0:T(8,128)(2,1)S(1)} %get-tuple-element.174), channel_id=1, source_target_pairs={{0,8},{1,9},{2,10},{3,11},{4,12},{5,13},{6,14},{7,15},{8,16},{9,17... | collective-permute-start | bytes 688136 | tf_op jit(solution)/shard_map/ppermute | solution.py:270
  (21 other events, 101.2 us)

commit v4 on v3

--- a/solution.py
+++ b/solution.py
@@ -77,25 +77,24 @@
     return half // next(n for n in (7, 4, 2, 1) if half % (n * 128) == 0)
 
 
-def entry_half_kernel(_, gate_ref, up_ref, out_ref):
-    out_ref[0] = gate_ref[...]
-    out_ref[1] = up_ref[...]
+def entry_half_kernel(core_ref, gate_ref, up_ref, given_ref, kept_ref):
+    half = kept_ref.shape[1]
+    given = pl.multiple_of((1 - core_ref[0]) * half, half)
+    kept = pl.multiple_of(core_ref[0] * half, half)
+    for which, ref in enumerate((gate_ref, up_ref)):
+        given_ref[which] = ref[pl.ds(given, half)]
+        kept_ref[which] = ref[pl.ds(kept, half)]
 
 
 def entry_half(core, gate, up):
     width, units = gate.shape
-    steps = 2
-    tile = width // 2 // steps
-    spec = pl.BlockSpec((tile, units), lambda i, core: ((1 - core[0]) * steps + i, 0))
+    shape = jax.ShapeDtypeStruct((2, width // 2, units), gate.dtype)
     return pl.pallas_call(
         entry_half_kernel,
-        grid_spec=pltpu.PrefetchScalarGridSpec(
-            num_scalar_prefetch=1,
-            grid=(steps,),
-            in_specs=[spec, spec],
-            out_specs=pl.BlockSpec((2, tile, units), lambda i, core: (0, i, 0)),
-        ),
-        out_shape=jax.ShapeDtypeStruct((2, width // 2, units), gate.dtype),
+        in_specs=[pl.BlockSpec(memory_space=pltpu.SMEM)]
+        + [pl.BlockSpec(memory_space=pltpu.VMEM)] * 2,
+        out_specs=[pl.BlockSpec(memory_space=pltpu.VMEM)] * 2,
+        out_shape=[shape, shape],
         compiler_params=pltpu.CompilerParams(vmem_limit_bytes=16 * 1024 * 1024),
         cost_estimate=SMALL,
         name="entry_half",
@@ -146,30 +145,23 @@
     )(core.reshape(1), down, down)
 
 
-def entry_kernel(core_ref, rows_ref, *refs):
-    weight_refs, out_ref = refs[:-1], refs[-1]
-    half = rows_ref.shape[1]
-    rows = rows_ref[...]
+def entry_kernel(rows_ref, weight_ref, out_ref):
     for which in range(2):
-        if len(weight_refs) == 1:
-            weight = weight_refs[0][which]
-        else:
-            begin = pl.multiple_of(core_ref[0] * half, half)
-            weight = weight_refs[which][pl.ds(begin, half)]
-        out_ref[which] = jnp.dot(rows, weight, preferred_element_type=jnp.float32)
-
-
-def entry(rows, core, *weights):
+        out_ref[which] = jnp.dot(
+            rows_ref[...], weight_ref[which], preferred_element_type=jnp.float32
+        )
+
+
+def entry(rows, weight):
     return pl.pallas_call(
         entry_kernel,
-        in_specs=[pl.BlockSpec(memory_space=pltpu.SMEM)]
-        + [pl.BlockSpec(memory_space=pltpu.VMEM)] * (1 + len(weights)),
+        in_specs=[pl.BlockSpec(memory_space=pltpu.VMEM)] * 2,
         out_specs=pl.BlockSpec(memory_space=pltpu.VMEM),
-        out_shape=jax.ShapeDtypeStruct((2, rows.shape[0], weights[0].shape[-1]), jnp.float32),
+        out_shape=jax.ShapeDtypeStruct((2, rows.shape[0], weight.shape[2]), jnp.float32),
         compiler_params=pltpu.CompilerParams(vmem_limit_bytes=16 * 1024 * 1024),
         cost_estimate=SMALL,
         name="entry_products",
-    )(core.reshape(1), rows, *weights)
+    )(rows, weight)
 
 
 def inner_kernel(own_ref, other_ref, out_ref):
@@ -258,7 +250,7 @@
     devices = lax.axis_size(AXIS)
     planes = devices // SLICES
     me = lax.axis_index(AXIS)
-    core, plane = me % 2, me // SLICES
+    core, plane = lax.rem(me, 2), lax.div(me, SLICES)
     rows, width = hidden.shape
     half, quarter = width // 2, width // 4
     first_core = core == 0
@@ -342,9 +334,9 @@
             for at, k in enumerate(slots)
         ]
 
-    early = [planes // 2]
-    late = [k for k in range(1, planes) if k not in early]
-    first_set, late_set = (0, 1 + len(early)), (0, len(late))
+    early = [1, planes - 1]
+    late = list(range(2, planes - 1))
+    own_set, early_set, late_set = (0, 1), (1, len(early)), (0, len(late))
     join = lax.optimization_barrier
 
     def send_first(sent):
@@ -360,72 +352,80 @@
     held, got, block, core = join((held, got, block, core))
 
     own, own_got = spread_second(held, got)
-    entry_give = entry_half(core, gate_part, up_part)
-    own, own_got, slot_early, block, entry_give = join(
-        (own, own_got, slot_early, block, entry_give)
+    entry_give, entry_own = entry_half(core, gate_part, up_part)
+    own, own_got, slot_early, block, entry_give, entry_own = join(
+        (own, own_got, slot_early, block, entry_give, entry_own)
     )
     entry_other = in_core(entry_give)
 
     slot_late = [shift(block, k) for k in late]
     held, got = spread_first(slot_early)
-    held, got = join((held, got))
+    shares = [mixing_of(lax.rem(plane + k, planes)) for k in range(planes)]
+    held, got, shares = join((held, got, shares))
 
     early_held, early_got = spread_second(held, got)
     down_give, down_own = exit_half(after(core, *held), down_part)
-    early_held, early_got, slot_late, down_give, down_own = join(
-        (early_held, early_got, slot_late, down_give, down_own)
+    held, got = spread_first(slot_late)
+    early_held, early_got, held, got, down_give, down_own = join(
+        (early_held, early_got, held, got, down_give, down_own)
     )
 
     down = (down_own, in_core(down_give))
-    held, got = spread_first(slot_late)
     arrived = jnp.concatenate(
         [spread_rows(own, own_got), spread_rows(early_held, early_got)], 0
     )
-    pre_other = entry(arrived, core, entry_other)
-    held, got, pre_other, arrived = join((held, got, pre_other, arrived))
-
+    pre_other = entry(arrived, entry_other)
     late_held, late_got = spread_second(held, got)
-    pre_own = entry(arrived, core, gate_part, up_part)
+    pre_own = entry(arrived, entry_own)
     inner = inner_units(pre_own, in_core(pre_other))
     inner = (inner, in_core(inner))
-    (sent,) = exit_sums(inner, down, 2 * rows, [first_set], True)
+    (sent,) = exit_sums(inner, down, 2 * rows, [early_set], True)
     late_held, late_got, sent, inner = join((late_held, late_got, sent, inner))
 
     got = send_first(sent)
     arrived = spread_rows(late_held, late_got)
-    pre_other = entry(arrived, core, entry_other)
-    pre_own = entry(arrived, core, gate_part, up_part)
-    (kept,) = exit_sums(inner, down, 2 * rows, [first_set], False)
-    kept, got, pre_own, pre_other = join((kept, got, pre_own, pre_other))
+    pre_other = entry(arrived, entry_other)
+    pre_own = entry(arrived, entry_own)
+    (kept,) = exit_sums(inner, down, 2 * rows, [early_set], False)
+    (own_sent,) = exit_sums(inner, down, 2 * rows, [own_set], True)
+    (own_kept,) = exit_sums(inner, down, 2 * rows, [own_set], False)
+    attended = attend_more(0, None, *sent)
+    kept, got, own_sent, own_kept, pre_own, pre_other, attended = join(
+        (kept, got, own_sent, own_kept, pre_own, pre_other, attended)
+    )
 
     kept, sent = gather_second(kept, got)
     got = send_second(sent)
     inner = inner_units(pre_own, in_core(pre_other))
     inner = (inner, in_core(inner))
     (late_sent,) = exit_sums(inner, down, 2 * rows, [late_set], True)
-    kept, got, inner, late_sent = join((kept, got, inner, late_sent))
-
-    sums = gather_rows(kept, got)
-    terms = returned(sums, [0] + early)
-    late_got = send_first(late_sent)
     (late_kept,) = exit_sums(inner, down, 2 * rows, [late_set], False)
-    attended = attend_more(0, None, *late_sent)
-    late_kept, late_got, attended = join((late_kept, late_got, attended))
-
-    late_kept, late_sent = gather_second(late_kept, late_got)
-    late_got = send_second(late_sent)
+    kept, got, late_sent, late_kept = join((kept, got, late_sent, late_kept))
+
+    terms = returned(gather_rows(kept, got), early)
+    got = send_first(late_sent)
     attended = attend_more(1, attended, *late_sent)
-    late_kept, late_got, attended = join((late_kept, late_got, attended))
-
-    terms += returned(gather_rows(late_kept, late_got), late)
-    attended = attend_more(2, attended, *late_got)
-    attended = attend_more(3, attended, attended)
+    late_kept, got, attended = join((late_kept, got, attended))
+
+    kept, sent = gather_second(late_kept, got)
+    got = send_second(sent)
+    attended = attend_more(2, attended, *sent)
+    kept, got, attended, own_sent = join((kept, got, attended, own_sent))
+
+    terms += returned(gather_rows(kept, got), late)
+    got = send_first(own_sent)
+    attended = attend_more(3, attended, *own_sent)
+    own_kept, got, attended = join((own_kept, got, attended))
+
+    kept, sent = gather_second(own_kept, got)
+    got = send_second(sent)
+    terms += returned(gather_rows(kept, got), [0])
     slots = [k for k, _ in terms]
     terms, attended = join(([term for _, term in terms], attended))
     terms = list(zip(slots, terms))
     total = 0.0
     for k, term in terms:
-        total = total + mixing_of((plane + k) % planes) * widen(term)
+        total = total + shares[k] * widen(term)
 
     result = narrow(total)
     top, bottom = result[:rows], result[rows:]

time: 116 us -> 108 us (0.931)
  waiting for transfers between devices: 27 us -> 37.7 us
  Pallas kernels: 32.7 us -> 23.2 us
  local copies, waits for them, and re-layouts: 15 us -> 5.86 us
  other arithmetic: 5.66 us -> 3.45 us
  starting transfers between devices: 33.9 us -> 35.8 us
    ppermute x29 -> x33, waiting for transfers between devices: 21.8 us -> 31.5 us  [swap(): return lax.ppermute(value, AXIS, [(i, i ^ bit) for i in range(devices)])]
    unnamed x36 -> x20, local copies, waits for them, and re-layouts: 14.4 us -> 5.31 us
    pallas_call x4 -> x6, Pallas kernels: 8.73 us -> 4.27 us  [exit_sums(): pl.pallas_call(functools.partial(exit_kernel, sets=sets, rows=rows, sent=...]
    ppermute x29 -> x33, starting transfers between devices: 22.3 us -> 26.8 us  [swap(): return lax.ppermute(value, AXIS, [(i, i ^ bit) for i in range(devices)])]
    pallas_call x5, Pallas kernels: 8.4 us -> 5.55 us  [the longest x4 4.43 us: entry(): pl.pallas_call(entry_kernel, in_specs=[pl.BlockSpec(memory_space=pltpu.VM...]
    ppermute x6, starting transfers between devices: 11.6 us -> 9.08 us  [shift(): lax.ppermute(value, AXIS, [(i, (i + SLICES * by) % devices) for i in rang...]
    pallas_call x1, Pallas kernels: 3.78 us -> 1.67 us  [exit_half(): pl.pallas_call(exit_half_kernel, grid_spec=pltpu.PrefetchScalarGridSpec(n...]
    transpose x1, other arithmetic: 1.59 us -> 0.14 us  [spread_rows(): return jnp.moveaxis(four, 2, 0).reshape(-1, half)]
  transfers between devices with their start and end apart: 35 -> 39, of which waited for: 22 -> 23; matrix products, arithmetic and copies ran while one was open for 4% -> 2% of each run, Pallas kernels for 28% -> 22%
where the time goes in v4:
time: 108 us; the launch traced here: 107 us
  waiting for transfers between devices  37.7 us (35%)
  starting transfers between devices  35.8 us (33%)
  Pallas kernels  23.2 us (21%)
  local copies, waits for them, and re-layouts  5.86 us (5%)
  other arithmetic  3.45 us (3%)
  between operations  1.26 us (1%)
    ppermute x33, waiting for transfers between devices, swap(): return lax.ppermute(value, AXIS, [(i, i ^ bit) for i in range(devices)])  31.5 us
    ppermute x33, starting transfers between devices, swap(): return lax.ppermute(value, AXIS, [(i, i ^ bit) for i in range(devices)])  26.8 us
    pallas_call x4, Pallas kernels, attend(): pl.pallas_call(functools.partial(attend_kernel, first=first), grid_spec=p...  11 us
    ppermute x6, starting transfers between devices, shift(): lax.ppermute(value, AXIS, [(i, (i + SLICES * by) % devices) for i in rang...  9.08 us
    ppermute x6, waiting for transfers between devices, shift(): lax.ppermute(value, AXIS, [(i, (i + SLICES * by) % devices) for i in rang...  6.27 us
    unnamed x20, local copies, waits for them, and re-layouts  5.31 us
    pallas_call x4, Pallas kernels, entry(): pl.pallas_call(entry_kernel, in_specs=[pl.BlockSpec(memory_space=pltpu.VM...  4.43 us
    pallas_call x6, Pallas kernels, exit_sums(): pl.pallas_call(functools.partial(exit_kernel, sets=sets, rows=rows, sent=...  4.27 us
  transfers between devices with their start and end apart: 39, of which 23 were waited for; matrix products, arithmetic and copies ran while one was open for 2% of the time, Pallas kernels for 22%

profile of v4, /device:TPU:0, one launch (start us, length us, event | category | flops | bytes accessed | tf_op | source)
XLA Modules:
  0.0 107.4 jit_solution(8055282599542247036)
XLA Ops:
  3.2 2.9 %collective-permute-start.1 = (bf16[1,32,1792]{2,1,0:T(8,128)(2,1)S(1)}, bf16[1,32,1792]{2,1,0:T(8,128)(2,1)S(1)}, u32[]{:S(2)}, u32[]{:S(2)}) collective-permute-start(bf16[1,32,1792]{2,1,0:T(8,128)(2,1)S(1)} %get-tuple-element.107), channel_id=1, source_target_pairs={{0,2},{1,3},{2,0},{3,1},{4,6},{5,7},{6,4},{7,5},{8,10},{9,11},{10,... | collective-permute-start | bytes 344072 | tf_op jit(solution)/shard_map/ppermute | solution.py:259
  6.1 1.5 %collective-permute-start.2 = (bf16[1,32,1792]{2,1,0:T(8,128)(2,1)S(1)}, bf16[1,32,1792]{2,1,0:T(8,128)(2,1)S(1)}, u32[]{:S(2)}, u32[]{:S(2)}) collective-permute-start(bf16[1,32,1792]{2,1,0:T(8,128)(2,1)S(1)} %get-tuple-element.109), channel_id=1, source_target_pairs={{0,4},{1,5},{2,6},{3,7},{4,0},{5,1},{6,2},{7,3},{8,12},{9,13},{10,... | collective-permute-start | bytes 344072 | tf_op jit(solution)/shard_map/ppermute | solution.py:259
  7.6 1.6 %collective-permute-start.5 = (bf16[32,3584]{1,0:T(8,128)(2,1)S(1)}, bf16[32,3584]{1,0:T(8,128)(2,1)S(1)}, u32[]{:S(2)}, u32[]{:S(2)}) collective-permute-start(bf16[32,3584]{1,0:T(8,128)(2,1)S(1)} %maximum_select_fusion), channel_id=1, source_target_pairs={{0,8},{1,9},{2,10},{3,11},{4,12},{5,13},{6,14},{7,15},{8,16},{9,17... | collective-permute-start | bytes 688136 | tf_op jit(solution)/shard_map/ppermute | solution.py:262
  9.2 2.2 %collective-permute-start.6 = (bf16[32,3584]{1,0:T(8,128)(2,1)S(1)}, bf16[32,3584]{1,0:T(8,128)(2,1)S(1)}, u32[]{:S(2)}, u32[]{:S(2)}) collective-permute-start(bf16[32,3584]{1,0:T(8,128)(2,1)S(1)} %maximum_select_fusion), channel_id=1, source_target_pairs={{0,24},{1,25},{2,26},{3,27},{4,28},{5,29},{6,30},{7,31},{8,0},{9,1... | collective-permute-start | bytes 688136 | tf_op jit(solution)/shard_map/ppermute | solution.py:262
  13.4 2.0 %copy-done.2 = bf16[1,7168,256]{2,1,0:T(8,128)(2,1)S(1)} copy-done((bf16[1,7168,256]{2,1,0:T(8,128)(2,1)S(1)}, bf16[1,7168,256]{2,1,0:T(8,128)(2,1)}, u32[]{:S(2)}) %copy-start.2) | copy-done | bytes 3670040
  15.4 2.0 %copy-done.3 = bf16[1,7168,256]{2,1,0:T(8,128)(2,1)S(1)} copy-done((bf16[1,7168,256]{2,1,0:T(8,128)(2,1)S(1)}, bf16[1,7168,256]{2,1,0:T(8,128)(2,1)}, u32[]{:S(2)}) %copy-start.3) | copy-done | bytes 3670040
  18.6 2.3 %collective-permute-done.6 = bf16[32,3584]{1,0:T(8,128)(2,1)S(1)} collective-permute-done((bf16[32,3584]{1,0:T(8,128)(2,1)S(1)}, bf16[32,3584]{1,0:T(8,128)(2,1)S(1)}, u32[]{:S(2)}, u32[]{:S(2)}) %collective-permute-start.6) | collective-permute-done | bytes 229408 | tf_op jit(solution)/shard_map/ppermute | solution.py:262
  22.5 1.7 %collective-permute-start.12 = (bf16[32,3584]{1,0:T(8,128)(2,1)S(1)}, bf16[32,3584]{1,0:T(8,128)(2,1)S(1)}, u32[]{:S(2)}, u32[]{:S(2)}) collective-permute-start(bf16[32,3584]{1,0:T(8,128)(2,1)S(1)} %maximum_select_fusion), channel_id=1, source_target_pairs={{0,16},{1,17},{2,18},{3,19},{4,20},{5,21},{6,22},{7,23},{8,24},{9,... | collective-permute-start | bytes 688136 | tf_op jit(solution)/shard_map/ppermute | solution.py:262
  24.2 4.9 %collective-permute-done.8 = bf16[2,32,1792]{2,1,0:T(8,128)(2,1)S(1)} collective-permute-done((bf16[2,32,1792]{2,1,0:T(8,128)(2,1)S(1)}, bf16[2,32,1792]{2,1,0:T(8,128)(2,1)S(1)}, u32[]{:S(2)}, u32[]{:S(2)}) %collective-permute-start.8) | collective-permute-done | bytes 229408 | tf_op jit(solution)/shard_map/ppermute | solution.py:259
  30.1 1.6 %collective-permute-start.10 = (bf16[2,2,32,1792]{3,2,1,0:T(8,128)(2,1)S(1)}, bf16[2,2,32,1792]{3,2,1,0:T(8,128)(2,1)S(1)}, u32[]{:S(2)}, u32[]{:S(2)}) collective-permute-start(bf16[2,2,32,1792]{3,2,1,0:T(8,128)(2,1)S(1)} %pad_maximum_fusion.1), channel_id=1, source_target_pairs={{0,4},{1,5},{2,6},{3,7},{4,0},{5,1},{6,2},{7,3},{8,12},{9,13},{10,... | collective-permute-start | bytes 1376264 | tf_op jit(solution)/shard_map/ppermute | solution.py:259
  31.7 3.9 %collective-permute-done.12 = bf16[32,3584]{1,0:T(8,128)(2,1)S(1)} collective-permute-done((bf16[32,3584]{1,0:T(8,128)(2,1)S(1)}, bf16[32,3584]{1,0:T(8,128)(2,1)S(1)}, u32[]{:S(2)}, u32[]{:S(2)}) %collective-permute-start.12) | collective-permute-done | bytes 229408 | tf_op jit(solution)/shard_map/ppermute | solution.py:262
  35.7 1.6 %collective-permute-start.13 = (bf16[1,32,1792]{2,1,0:T(8,128)(2,1)S(1)}, bf16[1,32,1792]{2,1,0:T(8,128)(2,1)S(1)}, u32[]{:S(2)}, u32[]{:S(2)}) collective-permute-start(bf16[1,32,1792]{2,1,0:T(8,128)(2,1)S(1)} %get-tuple-element.126), channel_id=1, source_target_pairs={{0,2},{1,3},{2,0},{3,1},{4,6},{5,7},{6,4},{7,5},{8,10},{9,11},{10,... | collective-permute-start | bytes 344072 | tf_op jit(solution)/shard_map/ppermute | solution.py:259
  37.2 1.5 %collective-permute-start.14 = (bf16[1,32,1792]{2,1,0:T(8,128)(2,1)S(1)}, bf16[1,32,1792]{2,1,0:T(8,128)(2,1)S(1)}, u32[]{:S(2)}, u32[]{:S(2)}) collective-permute-start(bf16[1,32,1792]{2,1,0:T(8,128)(2,1)S(1)} %get-tuple-element.128), channel_id=1, source_target_pairs={{0,4},{1,5},{2,6},{3,7},{4,0},{5,1},{6,2},{7,3},{8,12},{9,13},{10,... | collective-permute-start | bytes 344072 | tf_op jit(solution)/shard_map/ppermute | solution.py:259
  38.9 1.7 %exit_half.1 = (bf16[256,3584]{1,0:T(8,128)(2,1)S(1)}, bf16[256,3584]{1,0:T(8,128)(2,1)S(1)}) custom-call(s32[1]{0:T(128)} %bitcast.28._, bf16[256,7168]{1,0:T(8,128)(2,1)S(1)} %bitcast.122, bf16[256,7168]{1,0:T(8,128)(2,1)S(1)} %bitcast.123), custom_call_target="tpu_custom_call" | custom-call | flops 1 | bytes 1 | tf_op jit(solution)/shard_map/exit_half/pallas_call | solution.py:130
  40.6 3.2 %collective-permute-done.13 = bf16[1,32,1792]{2,1,0:T(8,128)(2,1)S(1)} collective-permute-done((bf16[1,32,1792]{2,1,0:T(8,128)(2,1)S(1)}, bf16[1,32,1792]{2,1,0:T(8,128)(2,1)S(1)}, u32[]{:S(2)}, u32[]{:S(2)}) %collective-permute-start.13) | collective-permute-done | bytes 114720 | tf_op jit(solution)/shard_map/ppermute | solution.py:259
  44.7 1.6 %entry_products.5 = f32[2,384,256]{2,1,0:T(8,128)S(1)} custom-call(bf16[384,3584]{1,0:T(8,128)(2,1)S(1)} %pad_maximum_fusion.rows_ref, bf16[2,3584,256]{2,1,0:T(8,128)(2,1)S(1)} %collective-permute-done.17.weight_ref), custom_call_target="tpu_custom_call" | custom-call | flops 1 | bytes 1 | tf_op jit(solution)/shard_map/entry_products/pallas_call | solution.py:156
  46.9 1.6 %collective-permute-start.16 = (bf16[2,1,32,1792]{3,2,0,1:T(8,128)(2,1)S(1)}, bf16[2,1,32,1792]{3,2,0,1:T(8,128)(2,1)S(1)}, u32[]{:S(2)}, u32[]{:S(2)}) collective-permute-start(bf16[2,1,32,1792]{3,2,0,1:T(8,128)(2,1)S(1)} %get-tuple-element.218), channel_id=1, source_target_pairs={{0,2},{1,3},{2,0},{3,1},{4,6},{5,7},{6,4},{7,5},{8,10},{9,11},{10,... | collective-permute-start | bytes 688136 | tf_op jit(solution)/shard_map/ppermute | solution.py:259
  48.5 1.6 %collective-permute-start.15 = (bf16[2,1,32,1792]{3,2,0,1:T(8,128)(2,1)S(1)}, bf16[2,1,32,1792]{3,2,0,1:T(8,128)(2,1)S(1)}, u32[]{:S(2)}, u32[]{:S(2)}) collective-permute-start(bf16[2,1,32,1792]{3,2,0,1:T(8,128)(2,1)S(1)} %pad_maximum_fusion.7), channel_id=1, source_target_pairs={{0,4},{1,5},{2,6},{3,7},{4,0},{5,1},{6,2},{7,3},{8,12},{9,13},{10,... | collective-permute-start | bytes 688136 | tf_op jit(solution)/shard_map/ppermute | solution.py:259
  50.0 1.6 %entry_products.4.own_ref = f32[2,384,256]{2,1,0:T(8,128)S(1)} custom-call(bf16[384,3584]{1,0:T(8,128)(2,1)S(1)} %pad_maximum_fusion.rows_ref, bf16[2,3584,256]{2,1,0:T(8,128)(2,1)S(1)} %get-tuple-element.138.weight_ref), custom_call_target="tpu_custom_call" | custom-call | flops 1 | bytes 1 | tf_op jit(solution)/shard_map/entry_products/pallas_call | solution.py:156
  51.9 1.4 %collective-permute-done.19.other_ref = bf16[384,256]{1,0:T(8,128)(2,1)S(1)} collective-permute-done((bf16[384,256]{1,0:T(8,128)(2,1)S(1)}, bf16[384,256]{1,0:T(8,128)(2,1)S(1)}, u32[]{:S(2)}, u32[]{:S(2)}) %collective-permute-start.19) | collective-permute-done | bytes 196640 | tf_op jit(solution)/shard_map/ppermute | solution.py:259
  55.8 1.5 %collective-permute-start.21 = (bf16[2,2,32,1792]{3,2,1,0:T(8,128)(2,1)S(1)}, bf16[2,2,32,1792]{3,2,1,0:T(8,128)(2,1)S(1)}, u32[]{:S(2)}, u32[]{:S(2)}) collective-permute-start(bf16[2,2,32,1792]{3,2,1,0:T(8,128)(2,1)S(1)} %get-tuple-element.148), channel_id=1, source_target_pairs={{0,4},{1,5},{2,6},{3,7},{4,0},{5,1},{6,2},{7,3},{8,12},{9,13},{10,... | collective-permute-start | bytes 1376264 | tf_op jit(solution)/shard_map/ppermute | solution.py:259
  59.9 2.8 %latent_attention.4.refs_0_ = bf16[16,128,512]{2,1,0:T(8,128)(2,1)} custom-call(s32[16]{0:T(128)S(1)} %copy-done.4, bf16[16,576,128]{2,1,0:T(8,128)(2,1)S(1)} %bitcast.118, bf16[16,576,512]{2,1,0:T(8,128)(2,1)S(1)} %bitcast.114), custom_call_target="tpu_custom_call" | custom-call | flops 1 | bytes 1 | tf_op jit(solution)/shard_map/latent_attention/pallas_call | solution.py:56
  65.4 1.6 %collective-permute-done.21 = bf16[2,2,32,1792]{3,2,1,0:T(8,128)(2,1)S(1)} collective-permute-done((bf16[2,2,32,1792]{3,2,1,0:T(8,128)(2,1)S(1)}, bf16[2,2,32,1792]{3,2,1,0:T(8,128)(2,1)S(1)}, u32[]{:S(2)}, u32[]{:S(2)}) %collective-permute-start.21) | collective-permute-done | bytes 458784 | tf_op jit(solution)/shard_map/ppermute | solution.py:259
  72.7 3.8 %collective-permute-done.24 = bf16[2,32,1792]{2,1,0:T(8,128)(2,1)S(1)} collective-permute-done((bf16[2,32,1792]{2,1,0:T(8,128)(2,1)S(1)}, bf16[2,32,1792]{2,1,0:T(8,128)(2,1)S(1)}, u32[]{:S(2)}, u32[]{:S(2)}) %collective-permute-start.24) | collective-permute-done | bytes 229408 | tf_op jit(solution)/shard_map/ppermute | solution.py:259
  76.9 1.5 %collective-permute-start.29 = (bf16[2,1,32,1792]{3,2,1,0:T(8,128)(2,1)S(1)}, bf16[2,1,32,1792]{3,2,1,0:T(8,128)(2,1)S(1)}, u32[]{:S(2)}, u32[]{:S(2)}) collective-permute-start(bf16[2,1,32,1792]{3,2,1,0:T(8,128)(2,1)S(1)} %get-tuple-element.175), channel_id=1, source_target_pairs={{0,4},{1,5},{2,6},{3,7},{4,0},{5,1},{6,2},{7,3},{8,12},{9,13},{10,... | collective-permute-start | bytes 688136 | tf_op jit(solution)/shard_map/ppermute | solution.py:259
  79.2 2.4 %collective-permute-start.27 = (bf16[32,3584]{1,0:T(8,128)(2,1)S(1)}, bf16[32,3584]{1,0:T(8,128)(2,1)S(1)}, u32[]{:S(2)}, u32[]{:S(2)}) collective-permute-start(bf16[32,3584]{1,0:T(8,128)(2,1)S(1)} %get-tuple-element.215), channel_id=1, source_target_pairs={{0,24},{1,25},{2,26},{3,27},{4,28},{5,29},{6,30},{7,31},{8,0},{9,1... | collective-permute-start | bytes 688136 | tf_op jit(solution)/shard_map/ppermute | solution.py:262
  81.5 2.8 %latent_attention.5.refs_0_ = bf16[16,128,512]{2,1,0:T(8,128)(2,1)} custom-call(s32[16]{0:T(128)S(1)} %copy-done.4, bf16[16,576,128]{2,1,0:T(8,128)(2,1)S(1)} %bitcast.119, bf16[16,576,512]{2,1,0:T(8,128)(2,1)S(1)} %bitcast.115, bf16[16,128,512]{2,1,0:T(8,128)(2,1)} %latent_attention.4.refs_0_), custom_call_target="tpu_custom_call", output_to_operand_aliasing={{}: (3, {})} | custom-call | flops 1 | bytes 1 | tf_op jit(solution)/shard_map/latent_attention/pallas_call | solution.py:56
  86.6 2.8 %latent_attention.6.refs_0_ = bf16[16,128,512]{2,1,0:T(8,128)(2,1)} custom-call(s32[16]{0:T(128)S(1)} %copy-done.4, bf16[16,576,128]{2,1,0:T(8,128)(2,1)S(1)} %bitcast.120, bf16[16,576,512]{2,1,0:T(8,128)(2,1)S(1)} %bitcast.116, bf16[16,128,512]{2,1,0:T(8,128)(2,1)} %latent_attention.5.refs_0_), custom_call_target="tpu_custom_call", output_to_operand_aliasing={{}: (3, {})} | custom-call | flops 1 | bytes 1 | tf_op jit(solution)/shard_map/latent_attention/pallas_call | solution.py:56
  90.6 1.9 %collective-permute-start.34 = (bf16[2,1,32,1792]{3,2,1,0:T(8,128)(2,1)S(1)}, bf16[2,1,32,1792]{3,2,1,0:T(8,128)(2,1)S(1)}, u32[]{:S(2)}, u32[]{:S(2)}) collective-permute-start(bf16[2,1,32,1792]{3,2,1,0:T(8,128)(2,1)S(1)} %get-tuple-element.193), channel_id=1, source_target_pairs={{0,4},{1,5},{2,6},{3,7},{4,0},{5,1},{6,2},{7,3},{8,12},{9,13},{10,... | collective-permute-start | bytes 688136 | tf_op jit(solution)/shard_map/ppermute | solution.py:259
  94.1 2.7 %latent_attention.7 = bf16[16,128,512]{2,1,0:T(8,128)(2,1)} custom-call(s32[16]{0:T(128)S(1)} %copy-done.4, bf16[16,576,128]{2,1,0:T(8,128)(2,1)S(1)} %bitcast.121, bf16[16,576,512]{2,1,0:T(8,128)(2,1)S(1)} %bitcast.117, bf16[16,128,512]{2,1,0:T(8,128)(2,1)} %latent_attention.6.refs_0_), custom_call_target="tpu_custom_call", output_to_operand_aliasing={{}: (3, {})} | custom-call | flops 1 | bytes 1 | tf_op jit(solution)/shard_map/latent_attention/pallas_call | solution.py:56
  96.9 2.8 %collective-permute-done.35 = bf16[2,1,32,1792]{3,2,1,0:T(8,128)(2,1)S(1)} collective-permute-done((bf16[2,1,32,1792]{3,2,1,0:T(8,128)(2,1)S(1)}, bf16[2,1,32,1792]{3,2,1,0:T(8,128)(2,1)S(1)}, u32[]{:S(2)}, u32[]{:S(2)}) %collective-permute-start.35) | collective-permute-done | bytes 229408 | tf_op jit(solution)/shard_map/ppermute | solution.py:259
  100.9 3.7 %collective-permute-done.36 = bf16[1,32,1792]{2,1,0:T(8,128)(2,1)S(1)} collective-permute-done((bf16[1,32,1792]{2,1,0:T(8,128)(2,1)S(1)}, bf16[1,32,1792]{2,1,0:T(8,128)(2,1)S(1)}, u32[]{:S(2)}, u32[]{:S(2)}) %collective-permute-start.36) | collective-permute-done | bytes 114720 | tf_op jit(solution)/shard_map/ppermute | solution.py:259
  (139 shorter events, 33.3 us)
Async XLA Ops:
  3.2 8.8 %collective-permute-start.1 = (bf16[1,32,1792]{2,1,0:T(8,128)(2,1)S(1)}, bf16[1,32,1792]{2,1,0:T(8,128)(2,1)S(1)}, u32[]{:S(2)}, u32[]{:S(2)}) collective-permute-start(bf16[1,32,1792]{2,1,0:T(8,128)(2,1)S(1)} %get-tuple-element.107), channel_id=1, source_target_pairs={{0,2},{1,3},{2,0},{3,1},{4,6},{5,7},{6,4},{7,5},{8,10},{9,11},{10,... | collective-permute-start | bytes 344072 | tf_op jit(solution)/shard_map/ppermute | solution.py:259
  6.1 5.9 %collective-permute-start.2 = (bf16[1,32,1792]{2,1,0:T(8,128)(2,1)S(1)}, bf16[1,32,1792]{2,1,0:T(8,128)(2,1)S(1)}, u32[]{:S(2)}, u32[]{:S(2)}) collective-permute-start(bf16[1,32,1792]{2,1,0:T(8,128)(2,1)S(1)} %get-tuple-element.109), channel_id=1, source_target_pairs={{0,4},{1,5},{2,6},{3,7},{4,0},{5,1},{6,2},{7,3},{8,12},{9,13},{10,... | collective-permute-start | bytes 344072 | tf_op jit(solution)/shard_map/ppermute | solution.py:259
  7.6 11.0 %collective-permute-start.5 = (bf16[32,3584]{1,0:T(8,128)(2,1)S(1)}, bf16[32,3584]{1,0:T(8,128)(2,1)S(1)}, u32[]{:S(2)}, u32[]{:S(2)}) collective-permute-start(bf16[32,3584]{1,0:T(8,128)(2,1)S(1)} %maximum_select_fusion), channel_id=1, source_target_pairs={{0,8},{1,9},{2,10},{3,11},{4,12},{5,13},{6,14},{7,15},{8,16},{9,17... | collective-permute-start | bytes 688136 | tf_op jit(solution)/shard_map/ppermute | solution.py:262
  9.2 11.7 %collective-permute-start.6 = (bf16[32,3584]{1,0:T(8,128)(2,1)S(1)}, bf16[32,3584]{1,0:T(8,128)(2,1)S(1)}, u32[]{:S(2)}, u32[]{:S(2)}) collective-permute-start(bf16[32,3584]{1,0:T(8,128)(2,1)S(1)} %maximum_select_fusion), channel_id=1, source_target_pairs={{0,24},{1,25},{2,26},{3,27},{4,28},{5,29},{6,30},{7,31},{8,0},{9,1... | collective-permute-start | bytes 688136 | tf_op jit(solution)/shard_map/ppermute | solution.py:262
  12.0 8.9 %collective-permute-start.4 = (bf16[2,1,32,1792]{3,2,0,1:T(8,128)(2,1)S(1)}, bf16[2,1,32,1792]{3,2,0,1:T(8,128)(2,1)S(1)}, u32[]{:S(2)}, u32[]{:S(2)}) collective-permute-start(bf16[2,1,32,1792]{3,2,0,1:T(8,128)(2,1)S(1)} %get-tuple-element.226), channel_id=1, source_target_pairs={{0,2},{1,3},{2,0},{3,1},{4,6},{5,7},{6,4},{7,5},{8,10},{9,11},{10,... | collective-permute-start | bytes 688136 | tf_op jit(solution)/shard_map/ppermute | solution.py:259
  12.7 8.3 %collective-permute-start.3 = (bf16[2,1,32,1792]{3,2,0,1:T(8,128)(2,1)S(1)}, bf16[2,1,32,1792]{3,2,0,1:T(8,128)(2,1)S(1)}, u32[]{:S(2)}, u32[]{:S(2)}) collective-permute-start(bf16[2,1,32,1792]{3,2,0,1:T(8,128)(2,1)S(1)} %pad_maximum_fusion.3), channel_id=1, source_target_pairs={{0,4},{1,5},{2,6},{3,7},{4,0},{5,1},{6,2},{7,3},{8,12},{9,13},{10,... | collective-permute-start | bytes 688136 | tf_op jit(solution)/shard_map/ppermute | solution.py:259
  13.3 9.1 %collective-permute-start.9 = (f32[16,4]{0,1:T(4,128)S(1)}, f32[16,4]{0,1:T(4,128)S(1)}, u32[]{:S(2)}, u32[]{:S(2)}) collective-permute-start(f32[16,4]{0,1:T(4,128)S(1)} %select_reduce_fusion), channel_id=1, source_target_pairs={{0,1},{1,0},{2,3},{3,2},{4,5},{5,4},{6,7},{7,6},{8,9},{9,8},{10,11... | collective-permute-start | bytes 776 | tf_op jit(solution)/shard_map/ppermute | solution.py:259
  20.9 23.7 %collective-permute-start.17 = (bf16[2,3584,256]{2,1,0:T(8,128)(2,1)S(1)}, bf16[2,3584,256]{2,1,0:T(8,128)(2,1)S(1)}, u32[]{:S(2)}, u32[]{:S(2)}) collective-permute-start(bf16[2,3584,256]{2,1,0:T(8,128)(2,1)S(1)} %get-tuple-element.139), channel_id=1, source_target_pairs={{0,1},{1,0},{2,3},{3,2},{4,5},{5,4},{6,7},{7,6},{8,9},{9,8},{10,11... | collective-permute-start | bytes 11010056 | tf_op jit(solution)/shard_map/ppermute | solution.py:259
  21.0 8.1 %collective-permute-start.8 = (bf16[2,32,1792]{2,1,0:T(8,128)(2,1)S(1)}, bf16[2,32,1792]{2,1,0:T(8,128)(2,1)S(1)}, u32[]{:S(2)}, u32[]{:S(2)}) collective-permute-start(bf16[2,32,1792]{2,1,0:T(8,128)(2,1)S(1)} %pad_maximum_fusion.6), channel_id=1, source_target_pairs={{0,4},{1,5},{2,6},{3,7},{4,0},{5,1},{6,2},{7,3},{8,12},{9,13},{10,... | collective-permute-start | bytes 688136 | tf_op jit(solution)/shard_map/ppermute | solution.py:259
  21.6 7.8 %collective-permute-start.7 = (bf16[2,32,1792]{2,1,0:T(8,128)(2,1)S(1)}, bf16[2,32,1792]{2,1,0:T(8,128)(2,1)S(1)}, u32[]{:S(2)}, u32[]{:S(2)}) collective-permute-start(bf16[2,32,1792]{2,1,0:T(8,128)(2,1)S(1)} %pad_maximum_fusion.5), channel_id=1, source_target_pairs={{0,2},{1,3},{2,0},{3,1},{4,6},{5,7},{6,4},{7,5},{8,10},{9,11},{10,... | collective-permute-start | bytes 688136 | tf_op jit(solution)/shard_map/ppermute | solution.py:259
  22.5 13.2 %collective-permute-start.12 = (bf16[32,3584]{1,0:T(8,128)(2,1)S(1)}, bf16[32,3584]{1,0:T(8,128)(2,1)S(1)}, u32[]{:S(2)}, u32[]{:S(2)}) collective-permute-start(bf16[32,3584]{1,0:T(8,128)(2,1)S(1)} %maximum_select_fusion), channel_id=1, source_target_pairs={{0,16},{1,17},{2,18},{3,19},{4,20},{5,21},{6,22},{7,23},{8,24},{9,... | collective-permute-start | bytes 688136 | tf_op jit(solution)/shard_map/ppermute | solution.py:262
  29.5 14.7 %collective-permute-start.11 = (bf16[2,2,32,1792]{3,2,1,0:T(8,128)(2,1)S(1)}, bf16[2,2,32,1792]{3,2,1,0:T(8,128)(2,1)S(1)}, u32[]{:S(2)}, u32[]{:S(2)}) collective-permute-start(bf16[2,2,32,1792]{3,2,1,0:T(8,128)(2,1)S(1)} %pad_maximum_fusion.2), channel_id=1, source_target_pairs={{0,2},{1,3},{2,0},{3,1},{4,6},{5,7},{6,4},{7,5},{8,10},{9,11},{10,... | collective-permute-start | bytes 1376264 | tf_op jit(solution)/shard_map/ppermute | solution.py:259
  30.1 14.1 %collective-permute-start.10 = (bf16[2,2,32,1792]{3,2,1,0:T(8,128)(2,1)S(1)}, bf16[2,2,32,1792]{3,2,1,0:T(8,128)(2,1)S(1)}, u32[]{:S(2)}, u32[]{:S(2)}) collective-permute-start(bf16[2,2,32,1792]{3,2,1,0:T(8,128)(2,1)S(1)} %pad_maximum_fusion.1), channel_id=1, source_target_pairs={{0,4},{1,5},{2,6},{3,7},{4,0},{5,1},{6,2},{7,3},{8,12},{9,13},{10,... | collective-permute-start | bytes 1376264 | tf_op jit(solution)/shard_map/ppermute | solution.py:259
  35.7 8.1 %collective-permute-start.13 = (bf16[1,32,1792]{2,1,0:T(8,128)(2,1)S(1)}, bf16[1,32,1792]{2,1,0:T(8,128)(2,1)S(1)}, u32[]{:S(2)}, u32[]{:S(2)}) collective-permute-start(bf16[1,32,1792]{2,1,0:T(8,128)(2,1)S(1)} %get-tuple-element.126), channel_id=1, source_target_pairs={{0,2},{1,3},{2,0},{3,1},{4,6},{5,7},{6,4},{7,5},{8,10},{9,11},{10,... | collective-permute-start | bytes 344072 | tf_op jit(solution)/shard_map/ppermute | solution.py:259
  37.2 7.0 %collective-permute-start.14 = (bf16[1,32,1792]{2,1,0:T(8,128)(2,1)S(1)}, bf16[1,32,1792]{2,1,0:T(8,128)(2,1)S(1)}, u32[]{:S(2)}, u32[]{:S(2)}) collective-permute-start(bf16[1,32,1792]{2,1,0:T(8,128)(2,1)S(1)} %get-tuple-element.128), channel_id=1, source_target_pairs={{0,4},{1,5},{2,6},{3,7},{4,0},{5,1},{6,2},{7,3},{8,12},{9,13},{10,... | collective-permute-start | bytes 344072 | tf_op jit(solution)/shard_map/ppermute | solution.py:259
  44.2 7.7 %collective-permute-start.20 = (bf16[256,3584]{1,0:T(8,128)(2,1)S(1)}, bf16[256,3584]{1,0:T(8,128)(2,1)S(1)}, u32[]{:S(2)}, u32[]{:S(2)}) collective-permute-start(bf16[256,3584]{1,0:T(8,128)(2,1)S(1)} %get-tuple-element.141), channel_id=1, source_target_pairs={{0,1},{1,0},{2,3},{3,2},{4,5},{5,4},{6,7},{7,6},{8,9},{9,8},{10,11... | collective-permute-start | bytes 5505032 | tf_op jit(solution)/shard_map/ppermute | solution.py:259
  46.3 5.4 %collective-permute-start.18 = (f32[2,384,256]{2,1,0:T(8,128)S(1)}, f32[2,384,256]{2,1,0:T(8,128)S(1)}, u32[]{:S(2)}, u32[]{:S(2)}) collective-permute-start(f32[2,384,256]{2,1,0:T(8,128)S(1)} %entry_products.5), channel_id=1, source_target_pairs={{0,1},{1,0},{2,3},{3,2},{4,5},{5,4},{6,7},{7,6},{8,9},{9,8},{10,11... | collective-permute-start | bytes 2359304 | tf_op jit(solution)/shard_map/ppermute | solution.py:259
  46.9 7.6 %collective-permute-start.16 = (bf16[2,1,32,1792]{3,2,0,1:T(8,128)(2,1)S(1)}, bf16[2,1,32,1792]{3,2,0,1:T(8,128)(2,1)S(1)}, u32[]{:S(2)}, u32[]{:S(2)}) collective-permute-start(bf16[2,1,32,1792]{3,2,0,1:T(8,128)(2,1)S(1)} %get-tuple-element.218), channel_id=1, source_target_pairs={{0,2},{1,3},{2,0},{3,1},{4,6},{5,7},{6,4},{7,5},{8,10},{9,11},{10,... | collective-permute-start | bytes 688136 | tf_op jit(solution)/shard_map/ppermute | solution.py:259
  48.5 7.3 %collective-permute-start.15 = (bf16[2,1,32,1792]{3,2,0,1:T(8,128)(2,1)S(1)}, bf16[2,1,32,1792]{3,2,0,1:T(8,128)(2,1)S(1)}, u32[]{:S(2)}, u32[]{:S(2)}) collective-permute-start(bf16[2,1,32,1792]{3,2,0,1:T(8,128)(2,1)S(1)} %pad_maximum_fusion.7), channel_id=1, source_target_pairs={{0,4},{1,5},{2,6},{3,7},{4,0},{5,1},{6,2},{7,3},{8,12},{9,13},{10,... | collective-permute-start | bytes 688136 | tf_op jit(solution)/shard_map/ppermute | solution.py:259
  55.8 11.3 %collective-permute-start.21 = (bf16[2,2,32,1792]{3,2,1,0:T(8,128)(2,1)S(1)}, bf16[2,2,32,1792]{3,2,1,0:T(8,128)(2,1)S(1)}, u32[]{:S(2)}, u32[]{:S(2)}) collective-permute-start(bf16[2,2,32,1792]{3,2,1,0:T(8,128)(2,1)S(1)} %get-tuple-element.148), channel_id=1, source_target_pairs={{0,4},{1,5},{2,6},{3,7},{4,0},{5,1},{6,2},{7,3},{8,12},{9,13},{10,... | collective-permute-start | bytes 1376264 | tf_op jit(solution)/shard_map/ppermute | solution.py:259
  57.3 11.0 %collective-permute-start.22 = (bf16[2,2,32,1792]{3,2,1,0:T(8,128)(2,1)S(1)}, bf16[2,2,32,1792]{3,2,1,0:T(8,128)(2,1)S(1)}, u32[]{:S(2)}, u32[]{:S(2)}) collective-permute-start(bf16[2,2,32,1792]{3,2,1,0:T(8,128)(2,1)S(1)} %get-tuple-element.149), channel_id=1, source_target_pairs={{0,2},{1,3},{2,0},{3,1},{4,6},{5,7},{6,4},{7,5},{8,10},{9,11},{10,... | collective-permute-start | bytes 1376264 | tf_op jit(solution)/shard_map/ppermute | solution.py:259
  68.4 8.1 %collective-permute-start.24 = (bf16[2,32,1792]{2,1,0:T(8,128)(2,1)S(1)}, bf16[2,32,1792]{2,1,0:T(8,128)(2,1)S(1)}, u32[]{:S(2)}, u32[]{:S(2)}) collective-permute-start(bf16[2,32,1792]{2,1,0:T(8,128)(2,1)S(1)} %fusion.1), channel_id=1, source_target_pairs={{0,4},{1,5},{2,6},{3,7},{4,0},{5,1},{6,2},{7,3},{8,12},{9,13},{10,... | collective-permute-start | bytes 688136 | tf_op jit(solution)/shard_map/ppermute | solution.py:259
  69.1 7.8 %collective-permute-start.23 = (bf16[2,32,1792]{2,1,0:T(8,128)(2,1)S(1)}, bf16[2,32,1792]{2,1,0:T(8,128)(2,1)S(1)}, u32[]{:S(2)}, u32[]{:S(2)}) collective-permute-start(bf16[2,32,1792]{2,1,0:T(8,128)(2,1)S(1)} %fusion), channel_id=1, source_target_pairs={{0,2},{1,3},{2,0},{3,1},{4,6},{5,7},{6,4},{7,5},{8,10},{9,11},{10,... | collective-permute-start | bytes 688136 | tf_op jit(solution)/shard_map/ppermute | solution.py:259
  76.9 7.4 %collective-permute-start.29 = (bf16[2,1,32,1792]{3,2,1,0:T(8,128)(2,1)S(1)}, bf16[2,1,32,1792]{3,2,1,0:T(8,128)(2,1)S(1)}, u32[]{:S(2)}, u32[]{:S(2)}) collective-permute-start(bf16[2,1,32,1792]{3,2,1,0:T(8,128)(2,1)S(1)} %get-tuple-element.175), channel_id=1, source_target_pairs={{0,4},{1,5},{2,6},{3,7},{4,0},{5,1},{6,2},{7,3},{8,12},{9,13},{10,... | collective-permute-start | bytes 688136 | tf_op jit(solution)/shard_map/ppermute | solution.py:259
  78.4 6.6 %collective-permute-start.30 = (bf16[2,1,32,1792]{3,2,1,0:T(8,128)(2,1)S(1)}, bf16[2,1,32,1792]{3,2,1,0:T(8,128)(2,1)S(1)}, u32[]{:S(2)}, u32[]{:S(2)}) collective-permute-start(bf16[2,1,32,1792]{3,2,1,0:T(8,128)(2,1)S(1)} %get-tuple-element.176), channel_id=1, source_target_pairs={{0,2},{1,3},{2,0},{3,1},{4,6},{5,7},{6,4},{7,5},{8,10},{9,11},{10,... | collective-permute-start | bytes 688136 | tf_op jit(solution)/shard_map/ppermute | solution.py:259
  79.2 25.8 %collective-permute-start.27 = (bf16[32,3584]{1,0:T(8,128)(2,1)S(1)}, bf16[32,3584]{1,0:T(8,128)(2,1)S(1)}, u32[]{:S(2)}, u32[]{:S(2)}) collective-permute-start(bf16[32,3584]{1,0:T(8,128)(2,1)S(1)} %get-tuple-element.215), channel_id=1, source_target_pairs={{0,24},{1,25},{2,26},{3,27},{4,28},{5,29},{6,30},{7,31},{8,0},{9,1... | collective-permute-start | bytes 688136 | tf_op jit(solution)/shard_map/ppermute | solution.py:262
  81.5 23.4 %collective-permute-start.28 = (bf16[32,3584]{1,0:T(8,128)(2,1)S(1)}, bf16[32,3584]{1,0:T(8,128)(2,1)S(1)}, u32[]{:S(2)}, u32[]{:S(2)}) collective-permute-start(bf16[32,3584]{1,0:T(8,128)(2,1)S(1)} %get-tuple-element.214), channel_id=1, source_target_pairs={{0,8},{1,9},{2,10},{3,11},{4,12},{5,13},{6,14},{7,15},{8,16},{9,17... | collective-permute-start | bytes 688136 | tf_op jit(solution)/shard_map/ppermute | solution.py:262
  85.2 4.9 %collective-permute-start.32 = (bf16[1,32,1792]{2,1,0:T(8,128)(2,1)S(1)}, bf16[1,32,1792]{2,1,0:T(8,128)(2,1)S(1)}, u32[]{:S(2)}, u32[]{:S(2)}) collective-permute-start(bf16[1,32,1792]{2,1,0:T(8,128)(2,1)S(1)} %fusion.5), channel_id=1, source_target_pairs={{0,4},{1,5},{2,6},{3,7},{4,0},{5,1},{6,2},{7,3},{8,12},{9,13},{10,... | collective-permute-start | bytes 344072 | tf_op jit(solution)/shard_map/ppermute | solution.py:259
  90.6 6.3 %collective-permute-start.34 = (bf16[2,1,32,1792]{3,2,1,0:T(8,128)(2,1)S(1)}, bf16[2,1,32,1792]{3,2,1,0:T(8,128)(2,1)S(1)}, u32[]{:S(2)}, u32[]{:S(2)}) collective-permute-start(bf16[2,1,32,1792]{3,2,1,0:T(8,128)(2,1)S(1)} %get-tuple-element.193), channel_id=1, source_target_pairs={{0,4},{1,5},{2,6},{3,7},{4,0},{5,1},{6,2},{7,3},{8,12},{9,13},{10,... | collective-permute-start | bytes 688136 | tf_op jit(solution)/shard_map/ppermute | solution.py:259
  92.5 7.2 %collective-permute-start.35 = (bf16[2,1,32,1792]{3,2,1,0:T(8,128)(2,1)S(1)}, bf16[2,1,32,1792]{3,2,1,0:T(8,128)(2,1)S(1)}, u32[]{:S(2)}, u32[]{:S(2)}) collective-permute-start(bf16[2,1,32,1792]{3,2,1,0:T(8,128)(2,1)S(1)} %get-tuple-element.194), channel_id=1, source_target_pairs={{0,2},{1,3},{2,0},{3,1},{4,6},{5,7},{6,4},{7,5},{8,10},{9,11},{10,... | collective-permute-start | bytes 688136 | tf_op jit(solution)/shard_map/ppermute | solution.py:259
  93.0 12.0 %collective-permute-start.33 = (bf16[32,3584]{1,0:T(8,128)(2,1)S(1)}, bf16[32,3584]{1,0:T(8,128)(2,1)S(1)}, u32[]{:S(2)}, u32[]{:S(2)}) collective-permute-start(bf16[32,3584]{1,0:T(8,128)(2,1)S(1)} %maximum_bitcast_fusion.2), channel_id=1, source_target_pairs={{0,16},{1,17},{2,18},{3,19},{4,20},{5,21},{6,22},{7,23},{8,24},{9,... | collective-permute-start | bytes 688136 | tf_op jit(solution)/shard_map/ppermute | solution.py:262
  99.8 4.9 %collective-permute-start.36 = (bf16[1,32,1792]{2,1,0:T(8,128)(2,1)S(1)}, bf16[1,32,1792]{2,1,0:T(8,128)(2,1)S(1)}, u32[]{:S(2)}, u32[]{:S(2)}) collective-permute-start(bf16[1,32,1792]{2,1,0:T(8,128)(2,1)S(1)} %fusion.6), channel_id=1, source_target_pairs={{0,2},{1,3},{2,0},{3,1},{4,6},{5,7},{6,4},{7,5},{8,10},{9,11},{10,... | collective-permute-start | bytes 344072 | tf_op jit(solution)/shard_map/ppermute | solution.py:259
  (17 other events, 77.2 us)

commit v5 on v4

--- a/solution.py
+++ b/solution.py
@@ -405,16 +405,16 @@
     terms = returned(gather_rows(kept, got), early)
     got = send_first(late_sent)
     attended = attend_more(1, attended, *late_sent)
-    late_kept, got, attended = join((late_kept, got, attended))
+    late_kept, got, attended, own_sent = join((late_kept, got, attended, own_sent))
 
     kept, sent = gather_second(late_kept, got)
     got = send_second(sent)
     attended = attend_more(2, attended, *sent)
-    kept, got, attended, own_sent = join((kept, got, attended, own_sent))
+    kept, got, attended = join((kept, got, attended))
 
     terms += returned(gather_rows(kept, got), late)
     got = send_first(own_sent)
-    attended = attend_more(3, attended, *own_sent)
+    attended = attend_more(3, attended, *kept)
     own_kept, got, attended = join((own_kept, got, attended))
 
     kept, sent = gather_second(own_kept, got)

time: 108 us -> 107 us (level)
  waiting for transfers between devices: 37.7 us -> 35.6 us
  starting transfers between devices: 35.8 us -> 37.2 us
    ppermute x33, waiting for transfers between devices: 31.5 us -> 29.3 us  [swap(): return lax.ppermute(value, AXIS, [(i, i ^ bit) for i in range(devices)])]
    ppermute x33, starting transfers between devices: 26.8 us -> 27.9 us  [swap(): return lax.ppermute(value, AXIS, [(i, i ^ bit) for i in range(devices)])]
  transfers between devices with their start and end apart: 39 -> 39, of which waited for: 23 -> 22; matrix products, arithmetic and copies ran while one was open for 2% -> 2% of each run, Pallas kernels for 22% -> 22%
where the time goes in v5:
time: 107 us
  starting transfers between devices  37.2 us (35%)
  waiting for transfers between devices  35.6 us (33%)
  Pallas kernels  23.2 us (22%)
  local copies, waits for them, and re-layouts  5.86 us (5%)
  other arithmetic  3.45 us (3%)
  between operations  1.26 us (1%)
    ppermute x33, waiting for transfers between devices, swap(): return lax.ppermute(value, AXIS, [(i, i ^ bit) for i in range(devices)])  29.3 us
    ppermute x33, starting transfers between devices, swap(): return lax.ppermute(value, AXIS, [(i, i ^ bit) for i in range(devices)])  27.9 us
    pallas_call x4, Pallas kernels, attend(): pl.pallas_call(functools.partial(attend_kernel, first=first), grid_spec=p...  11 us
    ppermute x6, starting transfers between devices, shift(): lax.ppermute(value, AXIS, [(i, (i + SLICES * by) % devices) for i in rang...  9.31 us
    ppermute x6, waiting for transfers between devices, shift(): lax.ppermute(value, AXIS, [(i, (i + SLICES * by) % devices) for i in rang...  6.27 us
    unnamed x20, local copies, waits for them, and re-layouts  5.31 us
    pallas_call x4, Pallas kernels, entry(): pl.pallas_call(entry_kernel, in_specs=[pl.BlockSpec(memory_space=pltpu.VM...  4.43 us
    pallas_call x6, Pallas kernels, exit_sums(): pl.pallas_call(functools.partial(exit_kernel, sets=sets, rows=rows, sent=...  4.27 us
  transfers between devices with their start and end apart: 39, of which 22 were waited for; matrix products, arithmetic and copies ran while one was open for 2% of the time, Pallas kernels for 22%

profile of v5, /device:TPU:0, one launch (start us, length us, event | category | flops | bytes accessed | tf_op | source)
XLA Modules:
  0.0 106.5 jit_solution(522612113978835527)
XLA Ops:
  3.2 2.9 %collective-permute-start.1 = (bf16[1,32,1792]{2,1,0:T(8,128)(2,1)S(1)}, bf16[1,32,1792]{2,1,0:T(8,128)(2,1)S(1)}, u32[]{:S(2)}, u32[]{:S(2)}) collective-permute-start(bf16[1,32,1792]{2,1,0:T(8,128)(2,1)S(1)} %get-tuple-element.107), channel_id=1, source_target_pairs={{0,2},{1,3},{2,0},{3,1},{4,6},{5,7},{6,4},{7,5},{8,10},{9,11},{10,... | collective-permute-start | bytes 344072 | tf_op jit(solution)/shard_map/ppermute | solution.py:259
  6.1 1.5 %collective-permute-start.2 = (bf16[1,32,1792]{2,1,0:T(8,128)(2,1)S(1)}, bf16[1,32,1792]{2,1,0:T(8,128)(2,1)S(1)}, u32[]{:S(2)}, u32[]{:S(2)}) collective-permute-start(bf16[1,32,1792]{2,1,0:T(8,128)(2,1)S(1)} %get-tuple-element.109), channel_id=1, source_target_pairs={{0,4},{1,5},{2,6},{3,7},{4,0},{5,1},{6,2},{7,3},{8,12},{9,13},{10,... | collective-permute-start | bytes 344072 | tf_op jit(solution)/shard_map/ppermute | solution.py:259
  7.6 1.6 %collective-permute-start.5 = (bf16[32,3584]{1,0:T(8,128)(2,1)S(1)}, bf16[32,3584]{1,0:T(8,128)(2,1)S(1)}, u32[]{:S(2)}, u32[]{:S(2)}) collective-permute-start(bf16[32,3584]{1,0:T(8,128)(2,1)S(1)} %maximum_select_fusion), channel_id=1, source_target_pairs={{0,8},{1,9},{2,10},{3,11},{4,12},{5,13},{6,14},{7,15},{8,16},{9,17... | collective-permute-start | bytes 688136 | tf_op jit(solution)/shard_map/ppermute | solution.py:262
  9.2 2.2 %collective-permute-start.6 = (bf16[32,3584]{1,0:T(8,128)(2,1)S(1)}, bf16[32,3584]{1,0:T(8,128)(2,1)S(1)}, u32[]{:S(2)}, u32[]{:S(2)}) collective-permute-start(bf16[32,3584]{1,0:T(8,128)(2,1)S(1)} %maximum_select_fusion), channel_id=1, source_target_pairs={{0,24},{1,25},{2,26},{3,27},{4,28},{5,29},{6,30},{7,31},{8,0},{9,1... | collective-permute-start | bytes 688136 | tf_op jit(solution)/shard_map/ppermute | solution.py:262
  13.4 2.0 %copy-done.2 = bf16[1,7168,256]{2,1,0:T(8,128)(2,1)S(1)} copy-done((bf16[1,7168,256]{2,1,0:T(8,128)(2,1)S(1)}, bf16[1,7168,256]{2,1,0:T(8,128)(2,1)}, u32[]{:S(2)}) %copy-start.2) | copy-done | bytes 3670040
  15.4 2.0 %copy-done.3 = bf16[1,7168,256]{2,1,0:T(8,128)(2,1)S(1)} copy-done((bf16[1,7168,256]{2,1,0:T(8,128)(2,1)S(1)}, bf16[1,7168,256]{2,1,0:T(8,128)(2,1)}, u32[]{:S(2)}) %copy-start.3) | copy-done | bytes 3670040
  18.6 2.3 %collective-permute-done.6 = bf16[32,3584]{1,0:T(8,128)(2,1)S(1)} collective-permute-done((bf16[32,3584]{1,0:T(8,128)(2,1)S(1)}, bf16[32,3584]{1,0:T(8,128)(2,1)S(1)}, u32[]{:S(2)}, u32[]{:S(2)}) %collective-permute-start.6) | collective-permute-done | bytes 229408 | tf_op jit(solution)/shard_map/ppermute | solution.py:262
  22.5 1.7 %collective-permute-start.12 = (bf16[32,3584]{1,0:T(8,128)(2,1)S(1)}, bf16[32,3584]{1,0:T(8,128)(2,1)S(1)}, u32[]{:S(2)}, u32[]{:S(2)}) collective-permute-start(bf16[32,3584]{1,0:T(8,128)(2,1)S(1)} %maximum_select_fusion), channel_id=1, source_target_pairs={{0,16},{1,17},{2,18},{3,19},{4,20},{5,21},{6,22},{7,23},{8,24},{9,... | collective-permute-start | bytes 688136 | tf_op jit(solution)/shard_map/ppermute | solution.py:262
  24.2 4.9 %collective-permute-done.8 = bf16[2,32,1792]{2,1,0:T(8,128)(2,1)S(1)} collective-permute-done((bf16[2,32,1792]{2,1,0:T(8,128)(2,1)S(1)}, bf16[2,32,1792]{2,1,0:T(8,128)(2,1)S(1)}, u32[]{:S(2)}, u32[]{:S(2)}) %collective-permute-start.8) | collective-permute-done | bytes 229408 | tf_op jit(solution)/shard_map/ppermute | solution.py:259
  30.1 1.6 %collective-permute-start.10 = (bf16[2,2,32,1792]{3,2,1,0:T(8,128)(2,1)S(1)}, bf16[2,2,32,1792]{3,2,1,0:T(8,128)(2,1)S(1)}, u32[]{:S(2)}, u32[]{:S(2)}) collective-permute-start(bf16[2,2,32,1792]{3,2,1,0:T(8,128)(2,1)S(1)} %pad_maximum_fusion.1), channel_id=1, source_target_pairs={{0,4},{1,5},{2,6},{3,7},{4,0},{5,1},{6,2},{7,3},{8,12},{9,13},{10,... | collective-permute-start | bytes 1376264 | tf_op jit(solution)/shard_map/ppermute | solution.py:259
  31.7 3.9 %collective-permute-done.12 = bf16[32,3584]{1,0:T(8,128)(2,1)S(1)} collective-permute-done((bf16[32,3584]{1,0:T(8,128)(2,1)S(1)}, bf16[32,3584]{1,0:T(8,128)(2,1)S(1)}, u32[]{:S(2)}, u32[]{:S(2)}) %collective-permute-start.12) | collective-permute-done | bytes 229408 | tf_op jit(solution)/shard_map/ppermute | solution.py:262
  35.7 1.6 %collective-permute-start.13 = (bf16[1,32,1792]{2,1,0:T(8,128)(2,1)S(1)}, bf16[1,32,1792]{2,1,0:T(8,128)(2,1)S(1)}, u32[]{:S(2)}, u32[]{:S(2)}) collective-permute-start(bf16[1,32,1792]{2,1,0:T(8,128)(2,1)S(1)} %get-tuple-element.126), channel_id=1, source_target_pairs={{0,2},{1,3},{2,0},{3,1},{4,6},{5,7},{6,4},{7,5},{8,10},{9,11},{10,... | collective-permute-start | bytes 344072 | tf_op jit(solution)/shard_map/ppermute | solution.py:259
  37.2 1.5 %collective-permute-start.14 = (bf16[1,32,1792]{2,1,0:T(8,128)(2,1)S(1)}, bf16[1,32,1792]{2,1,0:T(8,128)(2,1)S(1)}, u32[]{:S(2)}, u32[]{:S(2)}) collective-permute-start(bf16[1,32,1792]{2,1,0:T(8,128)(2,1)S(1)} %get-tuple-element.128), channel_id=1, source_target_pairs={{0,4},{1,5},{2,6},{3,7},{4,0},{5,1},{6,2},{7,3},{8,12},{9,13},{10,... | collective-permute-start | bytes 344072 | tf_op jit(solution)/shard_map/ppermute | solution.py:259
  38.9 1.7 %exit_half.1 = (bf16[256,3584]{1,0:T(8,128)(2,1)S(1)}, bf16[256,3584]{1,0:T(8,128)(2,1)S(1)}) custom-call(s32[1]{0:T(128)} %bitcast.28._, bf16[256,7168]{1,0:T(8,128)(2,1)S(1)} %bitcast.122, bf16[256,7168]{1,0:T(8,128)(2,1)S(1)} %bitcast.123), custom_call_target="tpu_custom_call" | custom-call | flops 1 | bytes 1 | tf_op jit(solution)/shard_map/exit_half/pallas_call | solution.py:130
  40.6 3.2 %collective-permute-done.13 = bf16[1,32,1792]{2,1,0:T(8,128)(2,1)S(1)} collective-permute-done((bf16[1,32,1792]{2,1,0:T(8,128)(2,1)S(1)}, bf16[1,32,1792]{2,1,0:T(8,128)(2,1)S(1)}, u32[]{:S(2)}, u32[]{:S(2)}) %collective-permute-start.13) | collective-permute-done | bytes 114720 | tf_op jit(solution)/shard_map/ppermute | solution.py:259
  44.7 1.6 %entry_products.5 = f32[2,384,256]{2,1,0:T(8,128)S(1)} custom-call(bf16[384,3584]{1,0:T(8,128)(2,1)S(1)} %pad_maximum_fusion.rows_ref, bf16[2,3584,256]{2,1,0:T(8,128)(2,1)S(1)} %collective-permute-done.17.weight_ref), custom_call_target="tpu_custom_call" | custom-call | flops 1 | bytes 1 | tf_op jit(solution)/shard_map/entry_products/pallas_call | solution.py:156
  46.9 1.6 %collective-permute-start.16 = (bf16[2,1,32,1792]{3,2,0,1:T(8,128)(2,1)S(1)}, bf16[2,1,32,1792]{3,2,0,1:T(8,128)(2,1)S(1)}, u32[]{:S(2)}, u32[]{:S(2)}) collective-permute-start(bf16[2,1,32,1792]{3,2,0,1:T(8,128)(2,1)S(1)} %get-tuple-element.218), channel_id=1, source_target_pairs={{0,2},{1,3},{2,0},{3,1},{4,6},{5,7},{6,4},{7,5},{8,10},{9,11},{10,... | collective-permute-start | bytes 688136 | tf_op jit(solution)/shard_map/ppermute | solution.py:259
  48.5 1.6 %collective-permute-start.15 = (bf16[2,1,32,1792]{3,2,0,1:T(8,128)(2,1)S(1)}, bf16[2,1,32,1792]{3,2,0,1:T(8,128)(2,1)S(1)}, u32[]{:S(2)}, u32[]{:S(2)}) collective-permute-start(bf16[2,1,32,1792]{3,2,0,1:T(8,128)(2,1)S(1)} %pad_maximum_fusion.7), channel_id=1, source_target_pairs={{0,4},{1,5},{2,6},{3,7},{4,0},{5,1},{6,2},{7,3},{8,12},{9,13},{10,... | collective-permute-start | bytes 688136 | tf_op jit(solution)/shard_map/ppermute | solution.py:259
  50.0 1.6 %entry_products.4.own_ref = f32[2,384,256]{2,1,0:T(8,128)S(1)} custom-call(bf16[384,3584]{1,0:T(8,128)(2,1)S(1)} %pad_maximum_fusion.rows_ref, bf16[2,3584,256]{2,1,0:T(8,128)(2,1)S(1)} %get-tuple-element.138.weight_ref), custom_call_target="tpu_custom_call" | custom-call | flops 1 | bytes 1 | tf_op jit(solution)/shard_map/entry_products/pallas_call | solution.py:156
  51.9 1.4 %collective-permute-done.19.other_ref = bf16[384,256]{1,0:T(8,128)(2,1)S(1)} collective-permute-done((bf16[384,256]{1,0:T(8,128)(2,1)S(1)}, bf16[384,256]{1,0:T(8,128)(2,1)S(1)}, u32[]{:S(2)}, u32[]{:S(2)}) %collective-permute-start.19) | collective-permute-done | bytes 196640 | tf_op jit(solution)/shard_map/ppermute | solution.py:259
  55.8 1.5 %collective-permute-start.21 = (bf16[2,2,32,1792]{3,2,1,0:T(8,128)(2,1)S(1)}, bf16[2,2,32,1792]{3,2,1,0:T(8,128)(2,1)S(1)}, u32[]{:S(2)}, u32[]{:S(2)}) collective-permute-start(bf16[2,2,32,1792]{3,2,1,0:T(8,128)(2,1)S(1)} %get-tuple-element.148), channel_id=1, source_target_pairs={{0,4},{1,5},{2,6},{3,7},{4,0},{5,1},{6,2},{7,3},{8,12},{9,13},{10,... | collective-permute-start | bytes 1376264 | tf_op jit(solution)/shard_map/ppermute | solution.py:259
  59.9 2.8 %latent_attention.4.refs_0_ = bf16[16,128,512]{2,1,0:T(8,128)(2,1)} custom-call(s32[16]{0:T(128)S(1)} %copy-done.4, bf16[16,576,128]{2,1,0:T(8,128)(2,1)S(1)} %bitcast.118, bf16[16,576,512]{2,1,0:T(8,128)(2,1)S(1)} %bitcast.114), custom_call_target="tpu_custom_call" | custom-call | flops 1 | bytes 1 | tf_op jit(solution)/shard_map/latent_attention/pallas_call | solution.py:56
  65.4 1.6 %collective-permute-done.21 = bf16[2,2,32,1792]{3,2,1,0:T(8,128)(2,1)S(1)} collective-permute-done((bf16[2,2,32,1792]{3,2,1,0:T(8,128)(2,1)S(1)}, bf16[2,2,32,1792]{3,2,1,0:T(8,128)(2,1)S(1)}, u32[]{:S(2)}, u32[]{:S(2)}) %collective-permute-start.21) | collective-permute-done | bytes 458784 | tf_op jit(solution)/shard_map/ppermute | solution.py:259
  72.7 3.8 %collective-permute-done.24 = bf16[2,32,1792]{2,1,0:T(8,128)(2,1)S(1)} collective-permute-done((bf16[2,32,1792]{2,1,0:T(8,128)(2,1)S(1)}, bf16[2,32,1792]{2,1,0:T(8,128)(2,1)S(1)}, u32[]{:S(2)}, u32[]{:S(2)}) %collective-permute-start.24) | collective-permute-done | bytes 229408 | tf_op jit(solution)/shard_map/ppermute | solution.py:259
  76.9 1.5 %collective-permute-start.29 = (bf16[2,1,32,1792]{3,2,1,0:T(8,128)(2,1)S(1)}, bf16[2,1,32,1792]{3,2,1,0:T(8,128)(2,1)S(1)}, u32[]{:S(2)}, u32[]{:S(2)}) collective-permute-start(bf16[2,1,32,1792]{3,2,1,0:T(8,128)(2,1)S(1)} %get-tuple-element.175), channel_id=1, source_target_pairs={{0,4},{1,5},{2,6},{3,7},{4,0},{5,1},{6,2},{7,3},{8,12},{9,13},{10,... | collective-permute-start | bytes 688136 | tf_op jit(solution)/shard_map/ppermute | solution.py:259
  79.2 2.4 %collective-permute-start.27 = (bf16[32,3584]{1,0:T(8,128)(2,1)S(1)}, bf16[32,3584]{1,0:T(8,128)(2,1)S(1)}, u32[]{:S(2)}, u32[]{:S(2)}) collective-permute-start(bf16[32,3584]{1,0:T(8,128)(2,1)S(1)} %get-tuple-element.215), channel_id=1, source_target_pairs={{0,24},{1,25},{2,26},{3,27},{4,28},{5,29},{6,30},{7,31},{8,0},{9,1... | collective-permute-start | bytes 688136 | tf_op jit(solution)/shard_map/ppermute | solution.py:262
  81.5 2.8 %latent_attention.5.refs_0_ = bf16[16,128,512]{2,1,0:T(8,128)(2,1)} custom-call(s32[16]{0:T(128)S(1)} %copy-done.4, bf16[16,576,128]{2,1,0:T(8,128)(2,1)S(1)} %bitcast.119, bf16[16,576,512]{2,1,0:T(8,128)(2,1)S(1)} %bitcast.115, bf16[16,128,512]{2,1,0:T(8,128)(2,1)} %latent_attention.4.refs_0_), custom_call_target="tpu_custom_call", output_to_operand_aliasing={{}: (3, {})} | custom-call | flops 1 | bytes 1 | tf_op jit(solution)/shard_map/latent_attention/pallas_call | solution.py:56
  86.6 1.6 %collective-permute-start.34 = (bf16[2,1,32,1792]{3,2,1,0:T(8,128)(2,1)S(1)}, bf16[2,1,32,1792]{3,2,1,0:T(8,128)(2,1)S(1)}, u32[]{:S(2)}, u32[]{:S(2)}) collective-permute-start(bf16[2,1,32,1792]{3,2,1,0:T(8,128)(2,1)S(1)} %get-tuple-element.193), channel_id=1, source_target_pairs={{0,4},{1,5},{2,6},{3,7},{4,0},{5,1},{6,2},{7,3},{8,12},{9,13},{10,... | collective-permute-start | bytes 688136 | tf_op jit(solution)/shard_map/ppermute | solution.py:259
  88.2 2.8 %latent_attention.6.refs_0_ = bf16[16,128,512]{2,1,0:T(8,128)(2,1)} custom-call(s32[16]{0:T(128)S(1)} %copy-done.4, bf16[16,576,128]{2,1,0:T(8,128)(2,1)S(1)} %bitcast.120, bf16[16,576,512]{2,1,0:T(8,128)(2,1)S(1)} %bitcast.116, bf16[16,128,512]{2,1,0:T(8,128)(2,1)} %latent_attention.5.refs_0_), custom_call_target="tpu_custom_call", output_to_operand_aliasing={{}: (3, {})} | custom-call | flops 1 | bytes 1 | tf_op jit(solution)/shard_map/latent_attention/pallas_call | solution.py:56
  92.3 1.4 %collective-permute-start.33 = (bf16[32,3584]{1,0:T(8,128)(2,1)S(1)}, bf16[32,3584]{1,0:T(8,128)(2,1)S(1)}, u32[]{:S(2)}, u32[]{:S(2)}) collective-permute-start(bf16[32,3584]{1,0:T(8,128)(2,1)S(1)} %maximum_bitcast_fusion.2), channel_id=1, source_target_pairs={{0,16},{1,17},{2,18},{3,19},{4,20},{5,21},{6,22},{7,23},{8,24},{9,... | collective-permute-start | bytes 688136 | tf_op jit(solution)/shard_map/ppermute | solution.py:262
  93.7 2.7 %latent_attention.7 = bf16[16,128,512]{2,1,0:T(8,128)(2,1)} custom-call(s32[16]{0:T(128)S(1)} %copy-done.4, bf16[16,576,128]{2,1,0:T(8,128)(2,1)S(1)} %bitcast.121, bf16[16,576,512]{2,1,0:T(8,128)(2,1)S(1)} %bitcast.117, bf16[16,128,512]{2,1,0:T(8,128)(2,1)} %latent_attention.6.refs_0_), custom_call_target="tpu_custom_call", output_to_operand_aliasing={{}: (3, {})} | custom-call | flops 1 | bytes 1 | tf_op jit(solution)/shard_map/latent_attention/pallas_call | solution.py:56
  99.5 3.1 %collective-permute-done.36 = bf16[1,32,1792]{2,1,0:T(8,128)(2,1)S(1)} collective-permute-done((bf16[1,32,1792]{2,1,0:T(8,128)(2,1)S(1)}, bf16[1,32,1792]{2,1,0:T(8,128)(2,1)S(1)}, u32[]{:S(2)}, u32[]{:S(2)}) %collective-permute-start.36) | collective-permute-done | bytes 114720 | tf_op jit(solution)/shard_map/ppermute | solution.py:259
  (139 shorter events, 34.8 us)
Async XLA Ops:
  3.2 8.8 %collective-permute-start.1 = (bf16[1,32,1792]{2,1,0:T(8,128)(2,1)S(1)}, bf16[1,32,1792]{2,1,0:T(8,128)(2,1)S(1)}, u32[]{:S(2)}, u32[]{:S(2)}) collective-permute-start(bf16[1,32,1792]{2,1,0:T(8,128)(2,1)S(1)} %get-tuple-element.107), channel_id=1, source_target_pairs={{0,2},{1,3},{2,0},{3,1},{4,6},{5,7},{6,4},{7,5},{8,10},{9,11},{10,... | collective-permute-start | bytes 344072 | tf_op jit(solution)/shard_map/ppermute | solution.py:259
  6.1 5.9 %collective-permute-start.2 = (bf16[1,32,1792]{2,1,0:T(8,128)(2,1)S(1)}, bf16[1,32,1792]{2,1,0:T(8,128)(2,1)S(1)}, u32[]{:S(2)}, u32[]{:S(2)}) collective-permute-start(bf16[1,32,1792]{2,1,0:T(8,128)(2,1)S(1)} %get-tuple-element.109), channel_id=1, source_target_pairs={{0,4},{1,5},{2,6},{3,7},{4,0},{5,1},{6,2},{7,3},{8,12},{9,13},{10,... | collective-permute-start | bytes 344072 | tf_op jit(solution)/shard_map/ppermute | solution.py:259
  7.6 11.0 %collective-permute-start.5 = (bf16[32,3584]{1,0:T(8,128)(2,1)S(1)}, bf16[32,3584]{1,0:T(8,128)(2,1)S(1)}, u32[]{:S(2)}, u32[]{:S(2)}) collective-permute-start(bf16[32,3584]{1,0:T(8,128)(2,1)S(1)} %maximum_select_fusion), channel_id=1, source_target_pairs={{0,8},{1,9},{2,10},{3,11},{4,12},{5,13},{6,14},{7,15},{8,16},{9,17... | collective-permute-start | bytes 688136 | tf_op jit(solution)/shard_map/ppermute | solution.py:262
  9.2 11.7 %collective-permute-start.6 = (bf16[32,3584]{1,0:T(8,128)(2,1)S(1)}, bf16[32,3584]{1,0:T(8,128)(2,1)S(1)}, u32[]{:S(2)}, u32[]{:S(2)}) collective-permute-start(bf16[32,3584]{1,0:T(8,128)(2,1)S(1)} %maximum_select_fusion), channel_id=1, source_target_pairs={{0,24},{1,25},{2,26},{3,27},{4,28},{5,29},{6,30},{7,31},{8,0},{9,1... | collective-permute-start | bytes 688136 | tf_op jit(solution)/shard_map/ppermute | solution.py:262
  12.0 8.9 %collective-permute-start.4 = (bf16[2,1,32,1792]{3,2,0,1:T(8,128)(2,1)S(1)}, bf16[2,1,32,1792]{3,2,0,1:T(8,128)(2,1)S(1)}, u32[]{:S(2)}, u32[]{:S(2)}) collective-permute-start(bf16[2,1,32,1792]{3,2,0,1:T(8,128)(2,1)S(1)} %get-tuple-element.226), channel_id=1, source_target_pairs={{0,2},{1,3},{2,0},{3,1},{4,6},{5,7},{6,4},{7,5},{8,10},{9,11},{10,... | collective-permute-start | bytes 688136 | tf_op jit(solution)/shard_map/ppermute | solution.py:259
  12.7 8.3 %collective-permute-start.3 = (bf16[2,1,32,1792]{3,2,0,1:T(8,128)(2,1)S(1)}, bf16[2,1,32,1792]{3,2,0,1:T(8,128)(2,1)S(1)}, u32[]{:S(2)}, u32[]{:S(2)}) collective-permute-start(bf16[2,1,32,1792]{3,2,0,1:T(8,128)(2,1)S(1)} %pad_maximum_fusion.3), channel_id=1, source_target_pairs={{0,4},{1,5},{2,6},{3,7},{4,0},{5,1},{6,2},{7,3},{8,12},{9,13},{10,... | collective-permute-start | bytes 688136 | tf_op jit(solution)/shard_map/ppermute | solution.py:259
  13.3 9.1 %collective-permute-start.9 = (f32[16,4]{0,1:T(4,128)S(1)}, f32[16,4]{0,1:T(4,128)S(1)}, u32[]{:S(2)}, u32[]{:S(2)}) collective-permute-start(f32[16,4]{0,1:T(4,128)S(1)} %select_reduce_fusion), channel_id=1, source_target_pairs={{0,1},{1,0},{2,3},{3,2},{4,5},{5,4},{6,7},{7,6},{8,9},{9,8},{10,11... | collective-permute-start | bytes 776 | tf_op jit(solution)/shard_map/ppermute | solution.py:259
  20.9 23.7 %collective-permute-start.17 = (bf16[2,3584,256]{2,1,0:T(8,128)(2,1)S(1)}, bf16[2,3584,256]{2,1,0:T(8,128)(2,1)S(1)}, u32[]{:S(2)}, u32[]{:S(2)}) collective-permute-start(bf16[2,3584,256]{2,1,0:T(8,128)(2,1)S(1)} %get-tuple-element.139), channel_id=1, source_target_pairs={{0,1},{1,0},{2,3},{3,2},{4,5},{5,4},{6,7},{7,6},{8,9},{9,8},{10,11... | collective-permute-start | bytes 11010056 | tf_op jit(solution)/shard_map/ppermute | solution.py:259
  21.0 8.1 %collective-permute-start.8 = (bf16[2,32,1792]{2,1,0:T(8,128)(2,1)S(1)}, bf16[2,32,1792]{2,1,0:T(8,128)(2,1)S(1)}, u32[]{:S(2)}, u32[]{:S(2)}) collective-permute-start(bf16[2,32,1792]{2,1,0:T(8,128)(2,1)S(1)} %pad_maximum_fusion.6), channel_id=1, source_target_pairs={{0,4},{1,5},{2,6},{3,7},{4,0},{5,1},{6,2},{7,3},{8,12},{9,13},{10,... | collective-permute-start | bytes 688136 | tf_op jit(solution)/shard_map/ppermute | solution.py:259
  21.6 7.8 %collective-permute-start.7 = (bf16[2,32,1792]{2,1,0:T(8,128)(2,1)S(1)}, bf16[2,32,1792]{2,1,0:T(8,128)(2,1)S(1)}, u32[]{:S(2)}, u32[]{:S(2)}) collective-permute-start(bf16[2,32,1792]{2,1,0:T(8,128)(2,1)S(1)} %pad_maximum_fusion.5), channel_id=1, source_target_pairs={{0,2},{1,3},{2,0},{3,1},{4,6},{5,7},{6,4},{7,5},{8,10},{9,11},{10,... | collective-permute-start | bytes 688136 | tf_op jit(solution)/shard_map/ppermute | solution.py:259
  22.5 13.2 %collective-permute-start.12 = (bf16[32,3584]{1,0:T(8,128)(2,1)S(1)}, bf16[32,3584]{1,0:T(8,128)(2,1)S(1)}, u32[]{:S(2)}, u32[]{:S(2)}) collective-permute-start(bf16[32,3584]{1,0:T(8,128)(2,1)S(1)} %maximum_select_fusion), channel_id=1, source_target_pairs={{0,16},{1,17},{2,18},{3,19},{4,20},{5,21},{6,22},{7,23},{8,24},{9,... | collective-permute-start | bytes 688136 | tf_op jit(solution)/shard_map/ppermute | solution.py:262
  29.5 14.7 %collective-permute-start.11 = (bf16[2,2,32,1792]{3,2,1,0:T(8,128)(2,1)S(1)}, bf16[2,2,32,1792]{3,2,1,0:T(8,128)(2,1)S(1)}, u32[]{:S(2)}, u32[]{:S(2)}) collective-permute-start(bf16[2,2,32,1792]{3,2,1,0:T(8,128)(2,1)S(1)} %pad_maximum_fusion.2), channel_id=1, source_target_pairs={{0,2},{1,3},{2,0},{3,1},{4,6},{5,7},{6,4},{7,5},{8,10},{9,11},{10,... | collective-permute-start | bytes 1376264 | tf_op jit(solution)/shard_map/ppermute | solution.py:259
  30.1 14.1 %collective-permute-start.10 = (bf16[2,2,32,1792]{3,2,1,0:T(8,128)(2,1)S(1)}, bf16[2,2,32,1792]{3,2,1,0:T(8,128)(2,1)S(1)}, u32[]{:S(2)}, u32[]{:S(2)}) collective-permute-start(bf16[2,2,32,1792]{3,2,1,0:T(8,128)(2,1)S(1)} %pad_maximum_fusion.1), channel_id=1, source_target_pairs={{0,4},{1,5},{2,6},{3,7},{4,0},{5,1},{6,2},{7,3},{8,12},{9,13},{10,... | collective-permute-start | bytes 1376264 | tf_op jit(solution)/shard_map/ppermute | solution.py:259
  35.7 8.1 %collective-permute-start.13 = (bf16[1,32,1792]{2,1,0:T(8,128)(2,1)S(1)}, bf16[1,32,1792]{2,1,0:T(8,128)(2,1)S(1)}, u32[]{:S(2)}, u32[]{:S(2)}) collective-permute-start(bf16[1,32,1792]{2,1,0:T(8,128)(2,1)S(1)} %get-tuple-element.126), channel_id=1, source_target_pairs={{0,2},{1,3},{2,0},{3,1},{4,6},{5,7},{6,4},{7,5},{8,10},{9,11},{10,... | collective-permute-start | bytes 344072 | tf_op jit(solution)/shard_map/ppermute | solution.py:259
  37.2 7.0 %collective-permute-start.14 = (bf16[1,32,1792]{2,1,0:T(8,128)(2,1)S(1)}, bf16[1,32,1792]{2,1,0:T(8,128)(2,1)S(1)}, u32[]{:S(2)}, u32[]{:S(2)}) collective-permute-start(bf16[1,32,1792]{2,1,0:T(8,128)(2,1)S(1)} %get-tuple-element.128), channel_id=1, source_target_pairs={{0,4},{1,5},{2,6},{3,7},{4,0},{5,1},{6,2},{7,3},{8,12},{9,13},{10,... | collective-permute-start | bytes 344072 | tf_op jit(solution)/shard_map/ppermute | solution.py:259
  44.2 7.7 %collective-permute-start.20 = (bf16[256,3584]{1,0:T(8,128)(2,1)S(1)}, bf16[256,3584]{1,0:T(8,128)(2,1)S(1)}, u32[]{:S(2)}, u32[]{:S(2)}) collective-permute-start(bf16[256,3584]{1,0:T(8,128)(2,1)S(1)} %get-tuple-element.141), channel_id=1, source_target_pairs={{0,1},{1,0},{2,3},{3,2},{4,5},{5,4},{6,7},{7,6},{8,9},{9,8},{10,11... | collective-permute-start | bytes 5505032 | tf_op jit(solution)/shard_map/ppermute | solution.py:259
  46.3 5.4 %collective-permute-start.18 = (f32[2,384,256]{2,1,0:T(8,128)S(1)}, f32[2,384,256]{2,1,0:T(8,128)S(1)}, u32[]{:S(2)}, u32[]{:S(2)}) collective-permute-start(f32[2,384,256]{2,1,0:T(8,128)S(1)} %entry_products.5), channel_id=1, source_target_pairs={{0,1},{1,0},{2,3},{3,2},{4,5},{5,4},{6,7},{7,6},{8,9},{9,8},{10,11... | collective-permute-start | bytes 2359304 | tf_op jit(solution)/shard_map/ppermute | solution.py:259
  46.9 7.6 %collective-permute-start.16 = (bf16[2,1,32,1792]{3,2,0,1:T(8,128)(2,1)S(1)}, bf16[2,1,32,1792]{3,2,0,1:T(8,128)(2,1)S(1)}, u32[]{:S(2)}, u32[]{:S(2)}) collective-permute-start(bf16[2,1,32,1792]{3,2,0,1:T(8,128)(2,1)S(1)} %get-tuple-element.218), channel_id=1, source_target_pairs={{0,2},{1,3},{2,0},{3,1},{4,6},{5,7},{6,4},{7,5},{8,10},{9,11},{10,... | collective-permute-start | bytes 688136 | tf_op jit(solution)/shard_map/ppermute | solution.py:259
  48.5 7.3 %collective-permute-start.15 = (bf16[2,1,32,1792]{3,2,0,1:T(8,128)(2,1)S(1)}, bf16[2,1,32,1792]{3,2,0,1:T(8,128)(2,1)S(1)}, u32[]{:S(2)}, u32[]{:S(2)}) collective-permute-start(bf16[2,1,32,1792]{3,2,0,1:T(8,128)(2,1)S(1)} %pad_maximum_fusion.7), channel_id=1, source_target_pairs={{0,4},{1,5},{2,6},{3,7},{4,0},{5,1},{6,2},{7,3},{8,12},{9,13},{10,... | collective-permute-start | bytes 688136 | tf_op jit(solution)/shard_map/ppermute | solution.py:259
  55.8 11.3 %collective-permute-start.21 = (bf16[2,2,32,1792]{3,2,1,0:T(8,128)(2,1)S(1)}, bf16[2,2,32,1792]{3,2,1,0:T(8,128)(2,1)S(1)}, u32[]{:S(2)}, u32[]{:S(2)}) collective-permute-start(bf16[2,2,32,1792]{3,2,1,0:T(8,128)(2,1)S(1)} %get-tuple-element.148), channel_id=1, source_target_pairs={{0,4},{1,5},{2,6},{3,7},{4,0},{5,1},{6,2},{7,3},{8,12},{9,13},{10,... | collective-permute-start | bytes 1376264 | tf_op jit(solution)/shard_map/ppermute | solution.py:259
  57.3 11.0 %collective-permute-start.22 = (bf16[2,2,32,1792]{3,2,1,0:T(8,128)(2,1)S(1)}, bf16[2,2,32,1792]{3,2,1,0:T(8,128)(2,1)S(1)}, u32[]{:S(2)}, u32[]{:S(2)}) collective-permute-start(bf16[2,2,32,1792]{3,2,1,0:T(8,128)(2,1)S(1)} %get-tuple-element.149), channel_id=1, source_target_pairs={{0,2},{1,3},{2,0},{3,1},{4,6},{5,7},{6,4},{7,5},{8,10},{9,11},{10,... | collective-permute-start | bytes 1376264 | tf_op jit(solution)/shard_map/ppermute | solution.py:259
  68.4 8.1 %collective-permute-start.24 = (bf16[2,32,1792]{2,1,0:T(8,128)(2,1)S(1)}, bf16[2,32,1792]{2,1,0:T(8,128)(2,1)S(1)}, u32[]{:S(2)}, u32[]{:S(2)}) collective-permute-start(bf16[2,32,1792]{2,1,0:T(8,128)(2,1)S(1)} %fusion.1), channel_id=1, source_target_pairs={{0,4},{1,5},{2,6},{3,7},{4,0},{5,1},{6,2},{7,3},{8,12},{9,13},{10,... | collective-permute-start | bytes 688136 | tf_op jit(solution)/shard_map/ppermute | solution.py:259
  69.1 7.8 %collective-permute-start.23 = (bf16[2,32,1792]{2,1,0:T(8,128)(2,1)S(1)}, bf16[2,32,1792]{2,1,0:T(8,128)(2,1)S(1)}, u32[]{:S(2)}, u32[]{:S(2)}) collective-permute-start(bf16[2,32,1792]{2,1,0:T(8,128)(2,1)S(1)} %fusion), channel_id=1, source_target_pairs={{0,2},{1,3},{2,0},{3,1},{4,6},{5,7},{6,4},{7,5},{8,10},{9,11},{10,... | collective-permute-start | bytes 688136 | tf_op jit(solution)/shard_map/ppermute | solution.py:259
  76.9 7.4 %collective-permute-start.29 = (bf16[2,1,32,1792]{3,2,1,0:T(8,128)(2,1)S(1)}, bf16[2,1,32,1792]{3,2,1,0:T(8,128)(2,1)S(1)}, u32[]{:S(2)}, u32[]{:S(2)}) collective-permute-start(bf16[2,1,32,1792]{3,2,1,0:T(8,128)(2,1)S(1)} %get-tuple-element.175), channel_id=1, source_target_pairs={{0,4},{1,5},{2,6},{3,7},{4,0},{5,1},{6,2},{7,3},{8,12},{9,13},{10,... | collective-permute-start | bytes 688136 | tf_op jit(solution)/shard_map/ppermute | solution.py:259
  78.4 6.6 %collective-permute-start.30 = (bf16[2,1,32,1792]{3,2,1,0:T(8,128)(2,1)S(1)}, bf16[2,1,32,1792]{3,2,1,0:T(8,128)(2,1)S(1)}, u32[]{:S(2)}, u32[]{:S(2)}) collective-permute-start(bf16[2,1,32,1792]{3,2,1,0:T(8,128)(2,1)S(1)} %get-tuple-element.176), channel_id=1, source_target_pairs={{0,2},{1,3},{2,0},{3,1},{4,6},{5,7},{6,4},{7,5},{8,10},{9,11},{10,... | collective-permute-start | bytes 688136 | tf_op jit(solution)/shard_map/ppermute | solution.py:259
  79.2 24.9 %collective-permute-start.27 = (bf16[32,3584]{1,0:T(8,128)(2,1)S(1)}, bf16[32,3584]{1,0:T(8,128)(2,1)S(1)}, u32[]{:S(2)}, u32[]{:S(2)}) collective-permute-start(bf16[32,3584]{1,0:T(8,128)(2,1)S(1)} %get-tuple-element.215), channel_id=1, source_target_pairs={{0,24},{1,25},{2,26},{3,27},{4,28},{5,29},{6,30},{7,31},{8,0},{9,1... | collective-permute-start | bytes 688136 | tf_op jit(solution)/shard_map/ppermute | solution.py:262
  81.5 22.5 %collective-permute-start.28 = (bf16[32,3584]{1,0:T(8,128)(2,1)S(1)}, bf16[32,3584]{1,0:T(8,128)(2,1)S(1)}, u32[]{:S(2)}, u32[]{:S(2)}) collective-permute-start(bf16[32,3584]{1,0:T(8,128)(2,1)S(1)} %get-tuple-element.214), channel_id=1, source_target_pairs={{0,8},{1,9},{2,10},{3,11},{4,12},{5,13},{6,14},{7,15},{8,16},{9,17... | collective-permute-start | bytes 688136 | tf_op jit(solution)/shard_map/ppermute | solution.py:262
  85.2 5.8 %collective-permute-start.32 = (bf16[1,32,1792]{2,1,0:T(8,128)(2,1)S(1)}, bf16[1,32,1792]{2,1,0:T(8,128)(2,1)S(1)}, u32[]{:S(2)}, u32[]{:S(2)}) collective-permute-start(bf16[1,32,1792]{2,1,0:T(8,128)(2,1)S(1)} %fusion.5), channel_id=1, source_target_pairs={{0,4},{1,5},{2,6},{3,7},{4,0},{5,1},{6,2},{7,3},{8,12},{9,13},{10,... | collective-permute-start | bytes 344072 | tf_op jit(solution)/shard_map/ppermute | solution.py:259
  85.8 6.4 %collective-permute-start.31 = (bf16[1,32,1792]{2,1,0:T(8,128)(2,1)S(1)}, bf16[1,32,1792]{2,1,0:T(8,128)(2,1)S(1)}, u32[]{:S(2)}, u32[]{:S(2)}) collective-permute-start(bf16[1,32,1792]{2,1,0:T(8,128)(2,1)S(1)} %fusion.4), channel_id=1, source_target_pairs={{0,2},{1,3},{2,0},{3,1},{4,6},{5,7},{6,4},{7,5},{8,10},{9,11},{10,... | collective-permute-start | bytes 344072 | tf_op jit(solution)/shard_map/ppermute | solution.py:259
  86.6 9.9 %collective-permute-start.34 = (bf16[2,1,32,1792]{3,2,1,0:T(8,128)(2,1)S(1)}, bf16[2,1,32,1792]{3,2,1,0:T(8,128)(2,1)S(1)}, u32[]{:S(2)}, u32[]{:S(2)}) collective-permute-start(bf16[2,1,32,1792]{3,2,1,0:T(8,128)(2,1)S(1)} %get-tuple-element.193), channel_id=1, source_target_pairs={{0,4},{1,5},{2,6},{3,7},{4,0},{5,1},{6,2},{7,3},{8,12},{9,13},{10,... | collective-permute-start | bytes 688136 | tf_op jit(solution)/shard_map/ppermute | solution.py:259
  91.0 6.7 %collective-permute-start.35 = (bf16[2,1,32,1792]{3,2,1,0:T(8,128)(2,1)S(1)}, bf16[2,1,32,1792]{3,2,1,0:T(8,128)(2,1)S(1)}, u32[]{:S(2)}, u32[]{:S(2)}) collective-permute-start(bf16[2,1,32,1792]{3,2,1,0:T(8,128)(2,1)S(1)} %get-tuple-element.194), channel_id=1, source_target_pairs={{0,2},{1,3},{2,0},{3,1},{4,6},{5,7},{6,4},{7,5},{8,10},{9,11},{10,... | collective-permute-start | bytes 688136 | tf_op jit(solution)/shard_map/ppermute | solution.py:259
  92.3 11.8 %collective-permute-start.33 = (bf16[32,3584]{1,0:T(8,128)(2,1)S(1)}, bf16[32,3584]{1,0:T(8,128)(2,1)S(1)}, u32[]{:S(2)}, u32[]{:S(2)}) collective-permute-start(bf16[32,3584]{1,0:T(8,128)(2,1)S(1)} %maximum_bitcast_fusion.2), channel_id=1, source_target_pairs={{0,16},{1,17},{2,18},{3,19},{4,20},{5,21},{6,22},{7,23},{8,24},{9,... | collective-permute-start | bytes 688136 | tf_op jit(solution)/shard_map/ppermute | solution.py:262
  (17 other events, 77.3 us)

commit v6 on v5

--- a/solution.py
+++ b/solution.py
@@ -334,7 +334,7 @@
             for at, k in enumerate(slots)
         ]
 
-    early = [1, planes - 1]
+    early = [planes - 1, 1]
     late = list(range(2, planes - 1))
     own_set, early_set, late_set = (0, 1), (1, len(early)), (0, len(late))
     join = lax.optimization_barrier

time: 107 us -> 109 us (1.019)
  waiting for transfers between devices: 35.6 us -> 38 us
    ppermute x33, waiting for transfers between devices: 29.3 us -> 31 us  [swap(): return lax.ppermute(value, AXIS, [(i, i ^ bit) for i in range(devices)])]
  transfers between devices with their start and end apart: 39 -> 39, of which waited for: 22 -> 20; matrix products, arithmetic and copies ran while one was open for 2% -> 2% of each run, Pallas kernels for 22% -> 21%
where the time goes in v6:
time: 109 us
  waiting for transfers between devices  38 us (35%)
  starting transfers between devices  36.9 us (34%)
  Pallas kernels  23.2 us (21%)
  local copies, waits for them, and re-layouts  5.86 us (5%)
  other arithmetic  3.45 us (3%)
  between operations  1.27 us (1%)
    ppermute x33, waiting for transfers between devices, swap(): return lax.ppermute(value, AXIS, [(i, i ^ bit) for i in range(devices)])  31 us
    ppermute x33, starting transfers between devices, swap(): return lax.ppermute(value, AXIS, [(i, i ^ bit) for i in range(devices)])  28.2 us
    pallas_call x4, Pallas kernels, attend(): pl.pallas_call(functools.partial(attend_kernel, first=first), grid_spec=p...  11 us
    ppermute x6, starting transfers between devices, shift(): lax.ppermute(value, AXIS, [(i, (i + SLICES * by) % devices) for i in rang...  8.65 us
    ppermute x6, waiting for transfers between devices, shift(): lax.ppermute(value, AXIS, [(i, (i + SLICES * by) % devices) for i in rang...  6.99 us
    unnamed x20, local copies, waits for them, and re-layouts  5.3 us
    pallas_call x4, Pallas kernels, entry(): pl.pallas_call(entry_kernel, in_specs=[pl.BlockSpec(memory_space=pltpu.VM...  4.43 us
    pallas_call x6, Pallas kernels, exit_sums(): pl.pallas_call(functools.partial(exit_kernel, sets=sets, rows=rows, sent=...  4.26 us
  transfers between devices with their start and end apart: 39, of which 20 were waited for; matrix products, arithmetic and copies ran while one was open for 2% of the time, Pallas kernels for 21%

profile of v6, /device:TPU:0, one launch (start us, length us, event | category | flops | bytes accessed | tf_op | source)
XLA Modules:
  0.0 108.6 jit_solution(8481165723682875975)
XLA Ops:
  3.2 2.9 %collective-permute-start.1 = (bf16[1,32,1792]{2,1,0:T(8,128)(2,1)S(1)}, bf16[1,32,1792]{2,1,0:T(8,128)(2,1)S(1)}, u32[]{:S(2)}, u32[]{:S(2)}) collective-permute-start(bf16[1,32,1792]{2,1,0:T(8,128)(2,1)S(1)} %get-tuple-element.107), channel_id=1, source_target_pairs={{0,2},{1,3},{2,0},{3,1},{4,6},{5,7},{6,4},{7,5},{8,10},{9,11},{10,... | collective-permute-start | bytes 344072 | tf_op jit(solution)/shard_map/ppermute | solution.py:259
  6.1 1.5 %collective-permute-start.2 = (bf16[1,32,1792]{2,1,0:T(8,128)(2,1)S(1)}, bf16[1,32,1792]{2,1,0:T(8,128)(2,1)S(1)}, u32[]{:S(2)}, u32[]{:S(2)}) collective-permute-start(bf16[1,32,1792]{2,1,0:T(8,128)(2,1)S(1)} %get-tuple-element.109), channel_id=1, source_target_pairs={{0,4},{1,5},{2,6},{3,7},{4,0},{5,1},{6,2},{7,3},{8,12},{9,13},{10,... | collective-permute-start | bytes 344072 | tf_op jit(solution)/shard_map/ppermute | solution.py:259
  7.6 3.6 %collective-permute-start.5 = (bf16[32,3584]{1,0:T(8,128)(2,1)S(1)}, bf16[32,3584]{1,0:T(8,128)(2,1)S(1)}, u32[]{:S(2)}, u32[]{:S(2)}) collective-permute-start(bf16[32,3584]{1,0:T(8,128)(2,1)S(1)} %maximum_select_fusion), channel_id=1, source_target_pairs={{0,24},{1,25},{2,26},{3,27},{4,28},{5,29},{6,30},{7,31},{8,0},{9,1... | collective-permute-start | bytes 688136 | tf_op jit(solution)/shard_map/ppermute | solution.py:262
  13.4 2.0 %copy-done.2 = bf16[1,7168,256]{2,1,0:T(8,128)(2,1)S(1)} copy-done((bf16[1,7168,256]{2,1,0:T(8,128)(2,1)S(1)}, bf16[1,7168,256]{2,1,0:T(8,128)(2,1)}, u32[]{:S(2)}) %copy-start.2) | copy-done | bytes 3670040
  15.4 2.0 %copy-done.3 = bf16[1,7168,256]{2,1,0:T(8,128)(2,1)S(1)} copy-done((bf16[1,7168,256]{2,1,0:T(8,128)(2,1)S(1)}, bf16[1,7168,256]{2,1,0:T(8,128)(2,1)}, u32[]{:S(2)}) %copy-start.3) | copy-done | bytes 3670040
  18.6 3.0 %collective-permute-done.6 = bf16[32,3584]{1,0:T(8,128)(2,1)S(1)} collective-permute-done((bf16[32,3584]{1,0:T(8,128)(2,1)S(1)}, bf16[32,3584]{1,0:T(8,128)(2,1)S(1)}, u32[]{:S(2)}, u32[]{:S(2)}) %collective-permute-start.6) | collective-permute-done | bytes 229408 | tf_op jit(solution)/shard_map/ppermute | solution.py:262
  24.2 5.7 %collective-permute-done.8 = bf16[2,32,1792]{2,1,0:T(8,128)(2,1)S(1)} collective-permute-done((bf16[2,32,1792]{2,1,0:T(8,128)(2,1)S(1)}, bf16[2,32,1792]{2,1,0:T(8,128)(2,1)S(1)}, u32[]{:S(2)}, u32[]{:S(2)}) %collective-permute-start.8) | collective-permute-done | bytes 229408 | tf_op jit(solution)/shard_map/ppermute | solution.py:259
  30.9 1.6 %collective-permute-start.10 = (bf16[2,2,32,1792]{3,2,1,0:T(8,128)(2,1)S(1)}, bf16[2,2,32,1792]{3,2,1,0:T(8,128)(2,1)S(1)}, u32[]{:S(2)}, u32[]{:S(2)}) collective-permute-start(bf16[2,2,32,1792]{3,2,1,0:T(8,128)(2,1)S(1)} %pad_maximum_fusion.1), channel_id=1, source_target_pairs={{0,4},{1,5},{2,6},{3,7},{4,0},{5,1},{6,2},{7,3},{8,12},{9,13},{10,... | collective-permute-start | bytes 1376264 | tf_op jit(solution)/shard_map/ppermute | solution.py:259
  32.4 3.9 %collective-permute-done.12 = bf16[32,3584]{1,0:T(8,128)(2,1)S(1)} collective-permute-done((bf16[32,3584]{1,0:T(8,128)(2,1)S(1)}, bf16[32,3584]{1,0:T(8,128)(2,1)S(1)}, u32[]{:S(2)}, u32[]{:S(2)}) %collective-permute-start.12) | collective-permute-done | bytes 229408 | tf_op jit(solution)/shard_map/ppermute | solution.py:262
  36.4 1.6 %collective-permute-start.13 = (bf16[1,32,1792]{2,1,0:T(8,128)(2,1)S(1)}, bf16[1,32,1792]{2,1,0:T(8,128)(2,1)S(1)}, u32[]{:S(2)}, u32[]{:S(2)}) collective-permute-start(bf16[1,32,1792]{2,1,0:T(8,128)(2,1)S(1)} %get-tuple-element.126), channel_id=1, source_target_pairs={{0,2},{1,3},{2,0},{3,1},{4,6},{5,7},{6,4},{7,5},{8,10},{9,11},{10,... | collective-permute-start | bytes 344072 | tf_op jit(solution)/shard_map/ppermute | solution.py:259
  38.0 1.5 %collective-permute-start.14 = (bf16[1,32,1792]{2,1,0:T(8,128)(2,1)S(1)}, bf16[1,32,1792]{2,1,0:T(8,128)(2,1)S(1)}, u32[]{:S(2)}, u32[]{:S(2)}) collective-permute-start(bf16[1,32,1792]{2,1,0:T(8,128)(2,1)S(1)} %get-tuple-element.128), channel_id=1, source_target_pairs={{0,4},{1,5},{2,6},{3,7},{4,0},{5,1},{6,2},{7,3},{8,12},{9,13},{10,... | collective-permute-start | bytes 344072 | tf_op jit(solution)/shard_map/ppermute | solution.py:259
  39.6 1.7 %exit_half.1 = (bf16[256,3584]{1,0:T(8,128)(2,1)S(1)}, bf16[256,3584]{1,0:T(8,128)(2,1)S(1)}) custom-call(s32[1]{0:T(128)} %bitcast.28._, bf16[256,7168]{1,0:T(8,128)(2,1)S(1)} %bitcast.122, bf16[256,7168]{1,0:T(8,128)(2,1)S(1)} %bitcast.123), custom_call_target="tpu_custom_call" | custom-call | flops 1 | bytes 1 | tf_op jit(solution)/shard_map/exit_half/pallas_call | solution.py:130
  41.3 3.2 %collective-permute-done.13 = bf16[1,32,1792]{2,1,0:T(8,128)(2,1)S(1)} collective-permute-done((bf16[1,32,1792]{2,1,0:T(8,128)(2,1)S(1)}, bf16[1,32,1792]{2,1,0:T(8,128)(2,1)S(1)}, u32[]{:S(2)}, u32[]{:S(2)}) %collective-permute-start.13) | collective-permute-done | bytes 114720 | tf_op jit(solution)/shard_map/ppermute | solution.py:259
  45.4 1.6 %entry_products.5 = f32[2,384,256]{2,1,0:T(8,128)S(1)} custom-call(bf16[384,3584]{1,0:T(8,128)(2,1)S(1)} %pad_maximum_fusion.rows_ref, bf16[2,3584,256]{2,1,0:T(8,128)(2,1)S(1)} %collective-permute-done.17.weight_ref), custom_call_target="tpu_custom_call" | custom-call | flops 1 | bytes 1 | tf_op jit(solution)/shard_map/entry_products/pallas_call | solution.py:156
  47.6 1.6 %collective-permute-start.16 = (bf16[2,1,32,1792]{3,2,0,1:T(8,128)(2,1)S(1)}, bf16[2,1,32,1792]{3,2,0,1:T(8,128)(2,1)S(1)}, u32[]{:S(2)}, u32[]{:S(2)}) collective-permute-start(bf16[2,1,32,1792]{3,2,0,1:T(8,128)(2,1)S(1)} %get-tuple-element.218), channel_id=1, source_target_pairs={{0,2},{1,3},{2,0},{3,1},{4,6},{5,7},{6,4},{7,5},{8,10},{9,11},{10,... | collective-permute-start | bytes 688136 | tf_op jit(solution)/shard_map/ppermute | solution.py:259
  49.2 1.6 %collective-permute-start.15 = (bf16[2,1,32,1792]{3,2,0,1:T(8,128)(2,1)S(1)}, bf16[2,1,32,1792]{3,2,0,1:T(8,128)(2,1)S(1)}, u32[]{:S(2)}, u32[]{:S(2)}) collective-permute-start(bf16[2,1,32,1792]{3,2,0,1:T(8,128)(2,1)S(1)} %pad_maximum_fusion.7), channel_id=1, source_target_pairs={{0,4},{1,5},{2,6},{3,7},{4,0},{5,1},{6,2},{7,3},{8,12},{9,13},{10,... | collective-permute-start | bytes 688136 | tf_op jit(solution)/shard_map/ppermute | solution.py:259
  50.8 1.6 %entry_products.4.own_ref = f32[2,384,256]{2,1,0:T(8,128)S(1)} custom-call(bf16[384,3584]{1,0:T(8,128)(2,1)S(1)} %pad_maximum_fusion.rows_ref, bf16[2,3584,256]{2,1,0:T(8,128)(2,1)S(1)} %get-tuple-element.138.weight_ref), custom_call_target="tpu_custom_call" | custom-call | flops 1 | bytes 1 | tf_op jit(solution)/shard_map/entry_products/pallas_call | solution.py:156
  52.6 1.4 %collective-permute-done.19.other_ref = bf16[384,256]{1,0:T(8,128)(2,1)S(1)} collective-permute-done((bf16[384,256]{1,0:T(8,128)(2,1)S(1)}, bf16[384,256]{1,0:T(8,128)(2,1)S(1)}, u32[]{:S(2)}, u32[]{:S(2)}) %collective-permute-start.19) | collective-permute-done | bytes 196640 | tf_op jit(solution)/shard_map/ppermute | solution.py:259
  56.5 1.5 %collective-permute-start.21 = (bf16[2,2,32,1792]{3,2,1,0:T(8,128)(2,1)S(1)}, bf16[2,2,32,1792]{3,2,1,0:T(8,128)(2,1)S(1)}, u32[]{:S(2)}, u32[]{:S(2)}) collective-permute-start(bf16[2,2,32,1792]{3,2,1,0:T(8,128)(2,1)S(1)} %get-tuple-element.148), channel_id=1, source_target_pairs={{0,4},{1,5},{2,6},{3,7},{4,0},{5,1},{6,2},{7,3},{8,12},{9,13},{10,... | collective-permute-start | bytes 1376264 | tf_op jit(solution)/shard_map/ppermute | solution.py:259
  60.6 2.7 %latent_attention.4.refs_0_ = bf16[16,128,512]{2,1,0:T(8,128)(2,1)} custom-call(s32[16]{0:T(128)S(1)} %copy-done.4, bf16[16,576,128]{2,1,0:T(8,128)(2,1)S(1)} %bitcast.118, bf16[16,576,512]{2,1,0:T(8,128)(2,1)S(1)} %bitcast.114), custom_call_target="tpu_custom_call" | custom-call | flops 1 | bytes 1 | tf_op jit(solution)/shard_map/latent_attention/pallas_call | solution.py:56
  66.1 1.7 %collective-permute-done.21 = bf16[2,2,32,1792]{3,2,1,0:T(8,128)(2,1)S(1)} collective-permute-done((bf16[2,2,32,1792]{3,2,1,0:T(8,128)(2,1)S(1)}, bf16[2,2,32,1792]{3,2,1,0:T(8,128)(2,1)S(1)}, u32[]{:S(2)}, u32[]{:S(2)}) %collective-permute-start.21) | collective-permute-done | bytes 458784 | tf_op jit(solution)/shard_map/ppermute | solution.py:259
  73.4 3.8 %collective-permute-done.24 = bf16[2,32,1792]{2,1,0:T(8,128)(2,1)S(1)} collective-permute-done((bf16[2,32,1792]{2,1,0:T(8,128)(2,1)S(1)}, bf16[2,32,1792]{2,1,0:T(8,128)(2,1)S(1)}, u32[]{:S(2)}, u32[]{:S(2)}) %collective-permute-start.24) | collective-permute-done | bytes 229408 | tf_op jit(solution)/shard_map/ppermute | solution.py:259
  77.7 1.5 %collective-permute-start.29 = (bf16[2,1,32,1792]{3,2,1,0:T(8,128)(2,1)S(1)}, bf16[2,1,32,1792]{3,2,1,0:T(8,128)(2,1)S(1)}, u32[]{:S(2)}, u32[]{:S(2)}) collective-permute-start(bf16[2,1,32,1792]{3,2,1,0:T(8,128)(2,1)S(1)} %get-tuple-element.175), channel_id=1, source_target_pairs={{0,4},{1,5},{2,6},{3,7},{4,0},{5,1},{6,2},{7,3},{8,12},{9,13},{10,... | collective-permute-start | bytes 688136 | tf_op jit(solution)/shard_map/ppermute | solution.py:259
  79.9 1.7 %collective-permute-start.27 = (bf16[32,3584]{1,0:T(8,128)(2,1)S(1)}, bf16[32,3584]{1,0:T(8,128)(2,1)S(1)}, u32[]{:S(2)}, u32[]{:S(2)}) collective-permute-start(bf16[32,3584]{1,0:T(8,128)(2,1)S(1)} %get-tuple-element.215), channel_id=1, source_target_pairs={{0,8},{1,9},{2,10},{3,11},{4,12},{5,13},{6,14},{7,15},{8,16},{9,17... | collective-permute-start | bytes 688136 | tf_op jit(solution)/shard_map/ppermute | solution.py:262
  81.6 2.2 %collective-permute-start.28 = (bf16[32,3584]{1,0:T(8,128)(2,1)S(1)}, bf16[32,3584]{1,0:T(8,128)(2,1)S(1)}, u32[]{:S(2)}, u32[]{:S(2)}) collective-permute-start(bf16[32,3584]{1,0:T(8,128)(2,1)S(1)} %get-tuple-element.214), channel_id=1, source_target_pairs={{0,24},{1,25},{2,26},{3,27},{4,28},{5,29},{6,30},{7,31},{8,0},{9,1... | collective-permute-start | bytes 688136 | tf_op jit(solution)/shard_map/ppermute | solution.py:262
  83.8 2.7 %latent_attention.5.refs_0_ = bf16[16,128,512]{2,1,0:T(8,128)(2,1)} custom-call(s32[16]{0:T(128)S(1)} %copy-done.4, bf16[16,576,128]{2,1,0:T(8,128)(2,1)S(1)} %bitcast.119, bf16[16,576,512]{2,1,0:T(8,128)(2,1)S(1)} %bitcast.115, bf16[16,128,512]{2,1,0:T(8,128)(2,1)} %latent_attention.4.refs_0_), custom_call_target="tpu_custom_call", output_to_operand_aliasing={{}: (3, {})} | custom-call | flops 1 | bytes 1 | tf_op jit(solution)/shard_map/latent_attention/pallas_call | solution.py:56
  87.3 1.5 %collective-permute-start.31 = (bf16[1,32,1792]{2,1,0:T(8,128)(2,1)S(1)}, bf16[1,32,1792]{2,1,0:T(8,128)(2,1)S(1)}, u32[]{:S(2)}, u32[]{:S(2)}) collective-permute-start(bf16[1,32,1792]{2,1,0:T(8,128)(2,1)S(1)} %fusion.4), channel_id=1, source_target_pairs={{0,2},{1,3},{2,0},{3,1},{4,6},{5,7},{6,4},{7,5},{8,10},{9,11},{10,... | collective-permute-start | bytes 344072 | tf_op jit(solution)/shard_map/ppermute | solution.py:259
  88.8 1.6 %collective-permute-start.34 = (bf16[2,1,32,1792]{3,2,1,0:T(8,128)(2,1)S(1)}, bf16[2,1,32,1792]{3,2,1,0:T(8,128)(2,1)S(1)}, u32[]{:S(2)}, u32[]{:S(2)}) collective-permute-start(bf16[2,1,32,1792]{3,2,1,0:T(8,128)(2,1)S(1)} %get-tuple-element.193), channel_id=1, source_target_pairs={{0,4},{1,5},{2,6},{3,7},{4,0},{5,1},{6,2},{7,3},{8,12},{9,13},{10,... | collective-permute-start | bytes 688136 | tf_op jit(solution)/shard_map/ppermute | solution.py:259
  90.4 2.8 %latent_attention.6.refs_0_ = bf16[16,128,512]{2,1,0:T(8,128)(2,1)} custom-call(s32[16]{0:T(128)S(1)} %copy-done.4, bf16[16,576,128]{2,1,0:T(8,128)(2,1)S(1)} %bitcast.120, bf16[16,576,512]{2,1,0:T(8,128)(2,1)S(1)} %bitcast.116, bf16[16,128,512]{2,1,0:T(8,128)(2,1)} %latent_attention.5.refs_0_), custom_call_target="tpu_custom_call", output_to_operand_aliasing={{}: (3, {})} | custom-call | flops 1 | bytes 1 | tf_op jit(solution)/shard_map/latent_attention/pallas_call | solution.py:56
  94.2 2.8 %latent_attention.7 = bf16[16,128,512]{2,1,0:T(8,128)(2,1)} custom-call(s32[16]{0:T(128)S(1)} %copy-done.4, bf16[16,576,128]{2,1,0:T(8,128)(2,1)S(1)} %bitcast.121, bf16[16,576,512]{2,1,0:T(8,128)(2,1)S(1)} %bitcast.117, bf16[16,128,512]{2,1,0:T(8,128)(2,1)} %latent_attention.6.refs_0_), custom_call_target="tpu_custom_call", output_to_operand_aliasing={{}: (3, {})} | custom-call | flops 1 | bytes 1 | tf_op jit(solution)/shard_map/latent_attention/pallas_call | solution.py:56
  97.0 3.1 %collective-permute-done.35 = bf16[2,1,32,1792]{3,2,1,0:T(8,128)(2,1)S(1)} collective-permute-done((bf16[2,1,32,1792]{3,2,1,0:T(8,128)(2,1)S(1)}, bf16[2,1,32,1792]{3,2,1,0:T(8,128)(2,1)S(1)}, u32[]{:S(2)}, u32[]{:S(2)}) %collective-permute-start.35) | collective-permute-done | bytes 229408 | tf_op jit(solution)/shard_map/ppermute | solution.py:259
  101.6 3.4 %collective-permute-done.36 = bf16[1,32,1792]{2,1,0:T(8,128)(2,1)S(1)} collective-permute-done((bf16[1,32,1792]{2,1,0:T(8,128)(2,1)S(1)}, bf16[1,32,1792]{2,1,0:T(8,128)(2,1)S(1)}, u32[]{:S(2)}, u32[]{:S(2)}) %collective-permute-start.36) | collective-permute-done | bytes 114720 | tf_op jit(solution)/shard_map/ppermute | solution.py:259
  (139 shorter events, 32.5 us)
Async XLA Ops:
  3.2 8.6 %collective-permute-start.1 = (bf16[1,32,1792]{2,1,0:T(8,128)(2,1)S(1)}, bf16[1,32,1792]{2,1,0:T(8,128)(2,1)S(1)}, u32[]{:S(2)}, u32[]{:S(2)}) collective-permute-start(bf16[1,32,1792]{2,1,0:T(8,128)(2,1)S(1)} %get-tuple-element.107), channel_id=1, source_target_pairs={{0,2},{1,3},{2,0},{3,1},{4,6},{5,7},{6,4},{7,5},{8,10},{9,11},{10,... | collective-permute-start | bytes 344072 | tf_op jit(solution)/shard_map/ppermute | solution.py:259
  6.1 5.7 %collective-permute-start.2 = (bf16[1,32,1792]{2,1,0:T(8,128)(2,1)S(1)}, bf16[1,32,1792]{2,1,0:T(8,128)(2,1)S(1)}, u32[]{:S(2)}, u32[]{:S(2)}) collective-permute-start(bf16[1,32,1792]{2,1,0:T(8,128)(2,1)S(1)} %get-tuple-element.109), channel_id=1, source_target_pairs={{0,4},{1,5},{2,6},{3,7},{4,0},{5,1},{6,2},{7,3},{8,12},{9,13},{10,... | collective-permute-start | bytes 344072 | tf_op jit(solution)/shard_map/ppermute | solution.py:259
  7.6 11.0 %collective-permute-start.5 = (bf16[32,3584]{1,0:T(8,128)(2,1)S(1)}, bf16[32,3584]{1,0:T(8,128)(2,1)S(1)}, u32[]{:S(2)}, u32[]{:S(2)}) collective-permute-start(bf16[32,3584]{1,0:T(8,128)(2,1)S(1)} %maximum_select_fusion), channel_id=1, source_target_pairs={{0,24},{1,25},{2,26},{3,27},{4,28},{5,29},{6,30},{7,31},{8,0},{9,1... | collective-permute-start | bytes 688136 | tf_op jit(solution)/shard_map/ppermute | solution.py:262
  11.2 10.4 %collective-permute-start.6 = (bf16[32,3584]{1,0:T(8,128)(2,1)S(1)}, bf16[32,3584]{1,0:T(8,128)(2,1)S(1)}, u32[]{:S(2)}, u32[]{:S(2)}) collective-permute-start(bf16[32,3584]{1,0:T(8,128)(2,1)S(1)} %maximum_select_fusion), channel_id=1, source_target_pairs={{0,8},{1,9},{2,10},{3,11},{4,12},{5,13},{6,14},{7,15},{8,16},{9,17... | collective-permute-start | bytes 688136 | tf_op jit(solution)/shard_map/ppermute | solution.py:262
  11.8 9.9 %collective-permute-start.4 = (bf16[2,1,32,1792]{3,2,0,1:T(8,128)(2,1)S(1)}, bf16[2,1,32,1792]{3,2,0,1:T(8,128)(2,1)S(1)}, u32[]{:S(2)}, u32[]{:S(2)}) collective-permute-start(bf16[2,1,32,1792]{3,2,0,1:T(8,128)(2,1)S(1)} %get-tuple-element.226), channel_id=1, source_target_pairs={{0,2},{1,3},{2,0},{3,1},{4,6},{5,7},{6,4},{7,5},{8,10},{9,11},{10,... | collective-permute-start | bytes 688136 | tf_op jit(solution)/shard_map/ppermute | solution.py:259
  12.4 9.2 %collective-permute-start.3 = (bf16[2,1,32,1792]{3,2,0,1:T(8,128)(2,1)S(1)}, bf16[2,1,32,1792]{3,2,0,1:T(8,128)(2,1)S(1)}, u32[]{:S(2)}, u32[]{:S(2)}) collective-permute-start(bf16[2,1,32,1792]{3,2,0,1:T(8,128)(2,1)S(1)} %pad_maximum_fusion.3), channel_id=1, source_target_pairs={{0,4},{1,5},{2,6},{3,7},{4,0},{5,1},{6,2},{7,3},{8,12},{9,13},{10,... | collective-permute-start | bytes 688136 | tf_op jit(solution)/shard_map/ppermute | solution.py:259
  13.3 9.7 %collective-permute-start.9 = (f32[16,4]{0,1:T(4,128)S(1)}, f32[16,4]{0,1:T(4,128)S(1)}, u32[]{:S(2)}, u32[]{:S(2)}) collective-permute-start(f32[16,4]{0,1:T(4,128)S(1)} %select_reduce_fusion), channel_id=1, source_target_pairs={{0,1},{1,0},{2,3},{3,2},{4,5},{5,4},{6,7},{7,6},{8,9},{9,8},{10,11... | collective-permute-start | bytes 776 | tf_op jit(solution)/shard_map/ppermute | solution.py:259
  21.7 23.7 %collective-permute-start.17 = (bf16[2,3584,256]{2,1,0:T(8,128)(2,1)S(1)}, bf16[2,3584,256]{2,1,0:T(8,128)(2,1)S(1)}, u32[]{:S(2)}, u32[]{:S(2)}) collective-permute-start(bf16[2,3584,256]{2,1,0:T(8,128)(2,1)S(1)} %get-tuple-element.139), channel_id=1, source_target_pairs={{0,1},{1,0},{2,3},{3,2},{4,5},{5,4},{6,7},{7,6},{8,9},{9,8},{10,11... | collective-permute-start | bytes 11010056 | tf_op jit(solution)/shard_map/ppermute | solution.py:259
  21.8 8.1 %collective-permute-start.8 = (bf16[2,32,1792]{2,1,0:T(8,128)(2,1)S(1)}, bf16[2,32,1792]{2,1,0:T(8,128)(2,1)S(1)}, u32[]{:S(2)}, u32[]{:S(2)}) collective-permute-start(bf16[2,32,1792]{2,1,0:T(8,128)(2,1)S(1)} %pad_maximum_fusion.6), channel_id=1, source_target_pairs={{0,4},{1,5},{2,6},{3,7},{4,0},{5,1},{6,2},{7,3},{8,12},{9,13},{10,... | collective-permute-start | bytes 688136 | tf_op jit(solution)/shard_map/ppermute | solution.py:259
  22.4 7.8 %collective-permute-start.7 = (bf16[2,32,1792]{2,1,0:T(8,128)(2,1)S(1)}, bf16[2,32,1792]{2,1,0:T(8,128)(2,1)S(1)}, u32[]{:S(2)}, u32[]{:S(2)}) collective-permute-start(bf16[2,32,1792]{2,1,0:T(8,128)(2,1)S(1)} %pad_maximum_fusion.5), channel_id=1, source_target_pairs={{0,2},{1,3},{2,0},{3,1},{4,6},{5,7},{6,4},{7,5},{8,10},{9,11},{10,... | collective-permute-start | bytes 688136 | tf_op jit(solution)/shard_map/ppermute | solution.py:259
  23.1 13.3 %collective-permute-start.12 = (bf16[32,3584]{1,0:T(8,128)(2,1)S(1)}, bf16[32,3584]{1,0:T(8,128)(2,1)S(1)}, u32[]{:S(2)}, u32[]{:S(2)}) collective-permute-start(bf16[32,3584]{1,0:T(8,128)(2,1)S(1)} %maximum_select_fusion), channel_id=1, source_target_pairs={{0,16},{1,17},{2,18},{3,19},{4,20},{5,21},{6,22},{7,23},{8,24},{9,... | collective-permute-start | bytes 688136 | tf_op jit(solution)/shard_map/ppermute | solution.py:262
  30.2 14.7 %collective-permute-start.11 = (bf16[2,2,32,1792]{3,2,1,0:T(8,128)(2,1)S(1)}, bf16[2,2,32,1792]{3,2,1,0:T(8,128)(2,1)S(1)}, u32[]{:S(2)}, u32[]{:S(2)}) collective-permute-start(bf16[2,2,32,1792]{3,2,1,0:T(8,128)(2,1)S(1)} %pad_maximum_fusion.2), channel_id=1, source_target_pairs={{0,2},{1,3},{2,0},{3,1},{4,6},{5,7},{6,4},{7,5},{8,10},{9,11},{10,... | collective-permute-start | bytes 1376264 | tf_op jit(solution)/shard_map/ppermute | solution.py:259
  30.9 14.1 %collective-permute-start.10 = (bf16[2,2,32,1792]{3,2,1,0:T(8,128)(2,1)S(1)}, bf16[2,2,32,1792]{3,2,1,0:T(8,128)(2,1)S(1)}, u32[]{:S(2)}, u32[]{:S(2)}) collective-permute-start(bf16[2,2,32,1792]{3,2,1,0:T(8,128)(2,1)S(1)} %pad_maximum_fusion.1), channel_id=1, source_target_pairs={{0,4},{1,5},{2,6},{3,7},{4,0},{5,1},{6,2},{7,3},{8,12},{9,13},{10,... | collective-permute-start | bytes 1376264 | tf_op jit(solution)/shard_map/ppermute | solution.py:259
  36.4 8.1 %collective-permute-start.13 = (bf16[1,32,1792]{2,1,0:T(8,128)(2,1)S(1)}, bf16[1,32,1792]{2,1,0:T(8,128)(2,1)S(1)}, u32[]{:S(2)}, u32[]{:S(2)}) collective-permute-start(bf16[1,32,1792]{2,1,0:T(8,128)(2,1)S(1)} %get-tuple-element.126), channel_id=1, source_target_pairs={{0,2},{1,3},{2,0},{3,1},{4,6},{5,7},{6,4},{7,5},{8,10},{9,11},{10,... | collective-permute-start | bytes 344072 | tf_op jit(solution)/shard_map/ppermute | solution.py:259
  38.0 7.0 %collective-permute-start.14 = (bf16[1,32,1792]{2,1,0:T(8,128)(2,1)S(1)}, bf16[1,32,1792]{2,1,0:T(8,128)(2,1)S(1)}, u32[]{:S(2)}, u32[]{:S(2)}) collective-permute-start(bf16[1,32,1792]{2,1,0:T(8,128)(2,1)S(1)} %get-tuple-element.128), channel_id=1, source_target_pairs={{0,4},{1,5},{2,6},{3,7},{4,0},{5,1},{6,2},{7,3},{8,12},{9,13},{10,... | collective-permute-start | bytes 344072 | tf_op jit(solution)/shard_map/ppermute | solution.py:259
  44.9 7.7 %collective-permute-start.20 = (bf16[256,3584]{1,0:T(8,128)(2,1)S(1)}, bf16[256,3584]{1,0:T(8,128)(2,1)S(1)}, u32[]{:S(2)}, u32[]{:S(2)}) collective-permute-start(bf16[256,3584]{1,0:T(8,128)(2,1)S(1)} %get-tuple-element.141), channel_id=1, source_target_pairs={{0,1},{1,0},{2,3},{3,2},{4,5},{5,4},{6,7},{7,6},{8,9},{9,8},{10,11... | collective-permute-start | bytes 5505032 | tf_op jit(solution)/shard_map/ppermute | solution.py:259
  47.0 5.4 %collective-permute-start.18 = (f32[2,384,256]{2,1,0:T(8,128)S(1)}, f32[2,384,256]{2,1,0:T(8,128)S(1)}, u32[]{:S(2)}, u32[]{:S(2)}) collective-permute-start(f32[2,384,256]{2,1,0:T(8,128)S(1)} %entry_products.5), channel_id=1, source_target_pairs={{0,1},{1,0},{2,3},{3,2},{4,5},{5,4},{6,7},{7,6},{8,9},{9,8},{10,11... | collective-permute-start | bytes 2359304 | tf_op jit(solution)/shard_map/ppermute | solution.py:259
  47.6 7.6 %collective-permute-start.16 = (bf16[2,1,32,1792]{3,2,0,1:T(8,128)(2,1)S(1)}, bf16[2,1,32,1792]{3,2,0,1:T(8,128)(2,1)S(1)}, u32[]{:S(2)}, u32[]{:S(2)}) collective-permute-start(bf16[2,1,32,1792]{3,2,0,1:T(8,128)(2,1)S(1)} %get-tuple-element.218), channel_id=1, source_target_pairs={{0,2},{1,3},{2,0},{3,1},{4,6},{5,7},{6,4},{7,5},{8,10},{9,11},{10,... | collective-permute-start | bytes 688136 | tf_op jit(solution)/shard_map/ppermute | solution.py:259
  49.2 7.3 %collective-permute-start.15 = (bf16[2,1,32,1792]{3,2,0,1:T(8,128)(2,1)S(1)}, bf16[2,1,32,1792]{3,2,0,1:T(8,128)(2,1)S(1)}, u32[]{:S(2)}, u32[]{:S(2)}) collective-permute-start(bf16[2,1,32,1792]{3,2,0,1:T(8,128)(2,1)S(1)} %pad_maximum_fusion.7), channel_id=1, source_target_pairs={{0,4},{1,5},{2,6},{3,7},{4,0},{5,1},{6,2},{7,3},{8,12},{9,13},{10,... | collective-permute-start | bytes 688136 | tf_op jit(solution)/shard_map/ppermute | solution.py:259
  56.5 11.3 %collective-permute-start.21 = (bf16[2,2,32,1792]{3,2,1,0:T(8,128)(2,1)S(1)}, bf16[2,2,32,1792]{3,2,1,0:T(8,128)(2,1)S(1)}, u32[]{:S(2)}, u32[]{:S(2)}) collective-permute-start(bf16[2,2,32,1792]{3,2,1,0:T(8,128)(2,1)S(1)} %get-tuple-element.148), channel_id=1, source_target_pairs={{0,4},{1,5},{2,6},{3,7},{4,0},{5,1},{6,2},{7,3},{8,12},{9,13},{10,... | collective-permute-start | bytes 1376264 | tf_op jit(solution)/shard_map/ppermute | solution.py:259
  58.0 11.0 %collective-permute-start.22 = (bf16[2,2,32,1792]{3,2,1,0:T(8,128)(2,1)S(1)}, bf16[2,2,32,1792]{3,2,1,0:T(8,128)(2,1)S(1)}, u32[]{:S(2)}, u32[]{:S(2)}) collective-permute-start(bf16[2,2,32,1792]{3,2,1,0:T(8,128)(2,1)S(1)} %get-tuple-element.149), channel_id=1, source_target_pairs={{0,2},{1,3},{2,0},{3,1},{4,6},{5,7},{6,4},{7,5},{8,10},{9,11},{10,... | collective-permute-start | bytes 1376264 | tf_op jit(solution)/shard_map/ppermute | solution.py:259
  69.1 8.1 %collective-permute-start.24 = (bf16[2,32,1792]{2,1,0:T(8,128)(2,1)S(1)}, bf16[2,32,1792]{2,1,0:T(8,128)(2,1)S(1)}, u32[]{:S(2)}, u32[]{:S(2)}) collective-permute-start(bf16[2,32,1792]{2,1,0:T(8,128)(2,1)S(1)} %fusion.1), channel_id=1, source_target_pairs={{0,4},{1,5},{2,6},{3,7},{4,0},{5,1},{6,2},{7,3},{8,12},{9,13},{10,... | collective-permute-start | bytes 688136 | tf_op jit(solution)/shard_map/ppermute | solution.py:259
  69.8 7.8 %collective-permute-start.23 = (bf16[2,32,1792]{2,1,0:T(8,128)(2,1)S(1)}, bf16[2,32,1792]{2,1,0:T(8,128)(2,1)S(1)}, u32[]{:S(2)}, u32[]{:S(2)}) collective-permute-start(bf16[2,32,1792]{2,1,0:T(8,128)(2,1)S(1)} %fusion), channel_id=1, source_target_pairs={{0,2},{1,3},{2,0},{3,1},{4,6},{5,7},{6,4},{7,5},{8,10},{9,11},{10,... | collective-permute-start | bytes 688136 | tf_op jit(solution)/shard_map/ppermute | solution.py:259
  77.7 8.9 %collective-permute-start.29 = (bf16[2,1,32,1792]{3,2,1,0:T(8,128)(2,1)S(1)}, bf16[2,1,32,1792]{3,2,1,0:T(8,128)(2,1)S(1)}, u32[]{:S(2)}, u32[]{:S(2)}) collective-permute-start(bf16[2,1,32,1792]{3,2,1,0:T(8,128)(2,1)S(1)} %get-tuple-element.175), channel_id=1, source_target_pairs={{0,4},{1,5},{2,6},{3,7},{4,0},{5,1},{6,2},{7,3},{8,12},{9,13},{10,... | collective-permute-start | bytes 688136 | tf_op jit(solution)/shard_map/ppermute | solution.py:259
  79.2 7.3 %collective-permute-start.30 = (bf16[2,1,32,1792]{3,2,1,0:T(8,128)(2,1)S(1)}, bf16[2,1,32,1792]{3,2,1,0:T(8,128)(2,1)S(1)}, u32[]{:S(2)}, u32[]{:S(2)}) collective-permute-start(bf16[2,1,32,1792]{3,2,1,0:T(8,128)(2,1)S(1)} %get-tuple-element.176), channel_id=1, source_target_pairs={{0,2},{1,3},{2,0},{3,1},{4,6},{5,7},{6,4},{7,5},{8,10},{9,11},{10,... | collective-permute-start | bytes 688136 | tf_op jit(solution)/shard_map/ppermute | solution.py:259
  79.9 26.3 %collective-permute-start.27 = (bf16[32,3584]{1,0:T(8,128)(2,1)S(1)}, bf16[32,3584]{1,0:T(8,128)(2,1)S(1)}, u32[]{:S(2)}, u32[]{:S(2)}) collective-permute-start(bf16[32,3584]{1,0:T(8,128)(2,1)S(1)} %get-tuple-element.215), channel_id=1, source_target_pairs={{0,8},{1,9},{2,10},{3,11},{4,12},{5,13},{6,14},{7,15},{8,16},{9,17... | collective-permute-start | bytes 688136 | tf_op jit(solution)/shard_map/ppermute | solution.py:262
  81.6 24.7 %collective-permute-start.28 = (bf16[32,3584]{1,0:T(8,128)(2,1)S(1)}, bf16[32,3584]{1,0:T(8,128)(2,1)S(1)}, u32[]{:S(2)}, u32[]{:S(2)}) collective-permute-start(bf16[32,3584]{1,0:T(8,128)(2,1)S(1)} %get-tuple-element.214), channel_id=1, source_target_pairs={{0,24},{1,25},{2,26},{3,27},{4,28},{5,29},{6,30},{7,31},{8,0},{9,1... | collective-permute-start | bytes 688136 | tf_op jit(solution)/shard_map/ppermute | solution.py:262
  86.7 6.4 %collective-permute-start.32 = (bf16[1,32,1792]{2,1,0:T(8,128)(2,1)S(1)}, bf16[1,32,1792]{2,1,0:T(8,128)(2,1)S(1)}, u32[]{:S(2)}, u32[]{:S(2)}) collective-permute-start(bf16[1,32,1792]{2,1,0:T(8,128)(2,1)S(1)} %fusion.5), channel_id=1, source_target_pairs={{0,4},{1,5},{2,6},{3,7},{4,0},{5,1},{6,2},{7,3},{8,12},{9,13},{10,... | collective-permute-start | bytes 344072 | tf_op jit(solution)/shard_map/ppermute | solution.py:259
  87.3 6.8 %collective-permute-start.31 = (bf16[1,32,1792]{2,1,0:T(8,128)(2,1)S(1)}, bf16[1,32,1792]{2,1,0:T(8,128)(2,1)S(1)}, u32[]{:S(2)}, u32[]{:S(2)}) collective-permute-start(bf16[1,32,1792]{2,1,0:T(8,128)(2,1)S(1)} %fusion.4), channel_id=1, source_target_pairs={{0,2},{1,3},{2,0},{3,1},{4,6},{5,7},{6,4},{7,5},{8,10},{9,11},{10,... | collective-permute-start | bytes 344072 | tf_op jit(solution)/shard_map/ppermute | solution.py:259
  88.8 8.2 %collective-permute-start.34 = (bf16[2,1,32,1792]{3,2,1,0:T(8,128)(2,1)S(1)}, bf16[2,1,32,1792]{3,2,1,0:T(8,128)(2,1)S(1)}, u32[]{:S(2)}, u32[]{:S(2)}) collective-permute-start(bf16[2,1,32,1792]{3,2,1,0:T(8,128)(2,1)S(1)} %get-tuple-element.193), channel_id=1, source_target_pairs={{0,4},{1,5},{2,6},{3,7},{4,0},{5,1},{6,2},{7,3},{8,12},{9,13},{10,... | collective-permute-start | bytes 688136 | tf_op jit(solution)/shard_map/ppermute | solution.py:259
  93.1 6.9 %collective-permute-start.35 = (bf16[2,1,32,1792]{3,2,1,0:T(8,128)(2,1)S(1)}, bf16[2,1,32,1792]{3,2,1,0:T(8,128)(2,1)S(1)}, u32[]{:S(2)}, u32[]{:S(2)}) collective-permute-start(bf16[2,1,32,1792]{3,2,1,0:T(8,128)(2,1)S(1)} %get-tuple-element.194), channel_id=1, source_target_pairs={{0,2},{1,3},{2,0},{3,1},{4,6},{5,7},{6,4},{7,5},{8,10},{9,11},{10,... | collective-permute-start | bytes 688136 | tf_op jit(solution)/shard_map/ppermute | solution.py:259
  94.1 12.1 %collective-permute-start.33 = (bf16[32,3584]{1,0:T(8,128)(2,1)S(1)}, bf16[32,3584]{1,0:T(8,128)(2,1)S(1)}, u32[]{:S(2)}, u32[]{:S(2)}) collective-permute-start(bf16[32,3584]{1,0:T(8,128)(2,1)S(1)} %maximum_bitcast_fusion.2), channel_id=1, source_target_pairs={{0,16},{1,17},{2,18},{3,19},{4,20},{5,21},{6,22},{7,23},{8,24},{9,... | collective-permute-start | bytes 688136 | tf_op jit(solution)/shard_map/ppermute | solution.py:262
  (17 other events, 77.3 us)
